TPU v7x, 32 devices: a whole 2x2x4 slice. The times are simulated.
32 devices in a mesh: group: 4 (over y, x), sector: 8 (over z, core).
Axes of the slice: x: 2, y: 2, z: 4, core: 2. Of those that a mesh axis runs over, the one named last changes fastest.
Arguments:
- state: float32 [32, 128, 4, 128], P(('group', 'sector')), may hold values from -180 to 180
- panel: bfloat16 [32, 32, 256], P('group'), may hold values from -3 to 3
- left_env: bfloat16 [32, 32, 128, 128], P(('group', 'sector')), may hold values from -1.5 to 1.5
- right_env: bfloat16 [32, 32, 128, 128], P(('group', 'sector')), may hold values from -1 to 1
- left_match: int32 [32], P(('group', 'sector')), may hold values from 0 to 7
- right_match: int32 [32], P(('group', 'sector')), may hold values from 0 to 7
- phys_states: int32 [32, 4], P(('group', 'sector')), may hold values from 0 to 15, all different within a row
Outputs:
- new_state: float32 [32, 128, 4, 128], P(('group', 'sector'))
- hessenberg: float32 [8, 8], replicated
Inputs may be any that keep to these rules, and one draw needn't show every extreme that they name: `left_match`: environment block index within the sector's own group, below 8. `right_match`: environment block index within the sector's own group, below 8. `phys_states`: each sector's 4 states are different.
All inputs are finite; a program needn't handle non-finite values.
Results may differ from a plain program's by a relative error of at most 0.025.
Values may be sent and summed in bfloat16 or wider, within the bound.
No kernel may reach another device: no remote copies, remote signals or barrier semaphores. Data moves between devices by JAX's collectives and lax.ppermute only.
A program may use at most 128 MiB of HBM per device.

v0:
```python
import jax
import jax.numpy as jnp
from jax import lax
from jax.sharding import PartitionSpec as P

KRYLOV = 8


TAU = 3.0
EPS = 1e-06
HIGH = lax.Precision.HIGHEST


def select_mix(panel, states):
    pairs = states[:, None] * 16 + states[None, :]
    choose = (
        jnp.arange(panel.shape[2], dtype=jnp.int32)[None, None, :] == pairs[:, :, None]
    ).astype(jnp.bfloat16)
    mixed = jnp.einsum("acz,qpz->aqcp", panel, choose, preferred_element_type=jnp.float32)
    return mixed.astype(jnp.bfloat16)


def apply_sector(block_in, left_block, right_block, mixing):
    channels, size = (left_block.shape[0], left_block.shape[1])
    states = block_in.shape[1]
    inner = jnp.dot(
        left_block.reshape(channels * size, size),
        block_in.reshape(size, states * size),
        preferred_element_type=jnp.float32,
    )
    inner = inner.astype(jnp.bfloat16).reshape(channels, size, states, size)
    middle = jnp.einsum(
        "aiqj,aqcp->cipj", inner, mixing, preferred_element_type=jnp.float32
    ).astype(jnp.bfloat16)
    return jnp.einsum("cipj,crj->ipr", middle, right_block, preferred_element_type=jnp.float32)


def exponent_column(hessenberg):
    scaled = -TAU / 16.0 * hessenberg
    power_term = jnp.eye(hessenberg.shape[0], dtype=jnp.float32)
    series = power_term
    for order in range(1, 11):
        power_term = jnp.dot(power_term, scaled, precision=HIGH) / float(order)
        series = series + power_term
    for square in range(4):
        series = jnp.dot(series, series, precision=HIGH)
    return series[:, 0]


def local(state, panel, left_env, right_env, left_match, right_match, phys_states):
    owned, block_size, states = (state.shape[0], state.shape[1], state.shape[2])
    channels = left_env.shape[1]
    full_panel = lax.all_gather(panel, "group", axis=0, tiled=True)
    mixes = jax.vmap(lambda chosen: select_mix(full_panel, chosen))(phys_states)
    left_rows = left_env.reshape(owned, channels * block_size, block_size)
    right_rows = right_env.reshape(owned, channels * block_size, block_size)
    sector_count = lax.axis_size("sector")
    match_lists = (
        lax.all_gather(left_match, "sector", axis=0, tiled=True),
        lax.all_gather(right_match, "sector", axis=0, tiled=True),
    )
    left_index = match_lists[0].reshape(sector_count, owned).T
    right_index = match_lists[1].reshape(sector_count, owned).T
    spread = (
        lax.all_to_all(left_rows, "sector", split_axis=1, concat_axis=0, tiled=True),
        lax.all_to_all(right_rows, "sector", split_axis=1, concat_axis=0, tiled=True),
    )
    sends = (jnp.take(spread[0], left_index, axis=0), jnp.take(spread[1], right_index, axis=0))
    routed = (
        lax.all_to_all(sends[0], "sector", split_axis=1, concat_axis=1, tiled=True),
        lax.all_to_all(sends[1], "sector", split_axis=1, concat_axis=1, tiled=True),
    )
    left_blocks = routed[0].reshape(owned, channels, block_size, block_size)
    right_blocks = routed[1].reshape(owned, channels, block_size, block_size)
    flattened = state.reshape(-1)
    length = flattened.shape[0]
    start_sq = lax.psum(jnp.sum(flattened * flattened), ("group", "sector"))
    krylov_basis = (
        jnp.zeros((KRYLOV, length), jnp.float32).at[0].set(flattened / jnp.sqrt(start_sq + EPS))
    )
    hessenberg = jnp.zeros((KRYLOV, KRYLOV), jnp.float32)
    for column in range(KRYLOV):
        blocks = (
            krylov_basis[column].reshape(owned, block_size, states, block_size).astype(jnp.bfloat16)
        )
        applied = jax.vmap(apply_sector)(blocks, left_blocks, right_blocks, mixes).reshape(-1)
        local_projection = jnp.dot(krylov_basis, applied, precision=HIGH)
        projection = lax.psum(local_projection, ("group", "sector"))
        remainder = applied - jnp.dot(projection, krylov_basis, precision=HIGH)
        if column + 1 < KRYLOV:
            norm_sq = lax.psum(jnp.sum(remainder * remainder), ("group", "sector"))
        hessenberg = hessenberg.at[:, column].set(projection)
        if column + 1 < KRYLOV:
            subdiag = jnp.sqrt(norm_sq + EPS)
            hessenberg = hessenberg.at[column + 1, column].set(subdiag)
            krylov_basis = krylov_basis.at[column + 1].set(remainder / subdiag)
    coefficients = exponent_column(hessenberg)
    entries = float(length * lax.axis_size("group") * sector_count)
    rescale = jnp.sqrt(jnp.float32(entries)) / jnp.sqrt(jnp.sum(coefficients * coefficients))
    evolved = jnp.dot(coefficients, krylov_basis, precision=HIGH) * rescale
    return (evolved.reshape(state.shape), hessenberg)


def solution(mesh):
    return jax.shard_map(
        local,
        mesh=mesh,
        in_specs=(
            P(("group", "sector"), None, None, None),
            P("group", None, None),
            P(("group", "sector"), None, None, None),
            P(("group", "sector"), None, None, None),
            P(("group", "sector")),
            P(("group", "sector")),
            P(("group", "sector"), None),
        ),
        out_specs=(P(("group", "sector"), None, None, None), P()),
        check_vma=False,
    )
```

profile of v0, /device:TPU:0, one launch (start us, length us, event | category | flops | bytes accessed | tf_op | source)
XLA Modules:
  0.0 1071.1 jit_solution(1273151619001540604)
XLA Ops:
  4.3 22.4 %reduce.93 = bf16[4096,128]{1,0:T(8,128)(2,1)S(1)} reduce(bf16[4096,1,128]{2,1,0:T(2,128)(2,1)S(1)} %bitcast.413, bf16[]{:T(256)} %broadcast.486), dimensions={1}, to_apply=%bitcast.402.reduce_sub_computation | reduce | bytes 2097154
  27.9 6.3 all-to-all-start
  37.4 23.4 %reduce.92 = bf16[4096,128]{1,0:T(8,128)(2,1)} reduce(bf16[4096,1,128]{2,1,0:T(2,128)(2,1)S(1)} %bitcast.414, bf16[]{:T(256)} %broadcast.486), dimensions={1}, to_apply=%bitcast.401.reduce_sub_computation | reduce | bytes 2097154
  71.5 23.7 %all-reduce.4 = (s32[8]{0:T(128)S(1)}, s32[8]{0:T(128)S(1)}) all-reduce(s32[8]{0:T(128)S(1)} %dynamic-update-slice.63, s32[8]{0:T(128)S(1)} %dynamic-update-slice.62), channel_id=1, replica_groups=mesh['group'=4,'sector'=8] {'sector'}, use_global_device_ids=true, to_apply=%add.3 | all-reduce | flops 16 | bytes 128
  110.7 17.7 %all-to-all-done.1 = bf16[1,8,512,128]{3,2,0,1:T(8,128)(2,1)S(1)} async-done(((bf16[1,8,512,128]{3,2,0,1:T(8,128)(2,1)}), bf16[1,8,512,128]{3,2,0,1:T(8,128)(2,1)S(1)}, u32[]{:S(2)}, u32[]{:S(2)}) %all-to-all-start.1) | async-done | bytes 1048608 | tf_op jit(solution)/shard_map/all_to_all | solution.py:70
  132.7 46.1 %psum.112 = f32[]{:T(128)} all-reduce(f32[]{:T(128)} %multiply_reduce_fusion.7), channel_id=1, replica_groups=mesh['group'=4,'sector'=8] {'group','sector'}, use_global_device_ids=true, to_apply=%region_2.3 | all-reduce | flops 1 | bytes 8 | tf_op jit(solution)/shard_map/psum | solution.py:77
  179.5 11.7 %all_gather.9 = bf16[32,32,256]{2,1,0:T(8,128)(2,1)S(1)} all-gather(bf16[8,32,256]{2,1,0:T(8,128)(2,1)S(1)} %copy-done.11), channel_id=1, replica_groups=mesh['group'=4,'sector'=8] {'group'}, dimensions={0}, use_global_device_ids=true | all-gather | bytes 655360 | tf_op jit(solution)/shard_map/all_gather | solution.py:53
  199.9 6.9 reshape.961
  206.8 7.6 fusion
  223.9 46.7 %psum.113 = f32[8]{0:T(128)S(1)} all-reduce(f32[8]{0:T(128)S(1)} %fusion.94), channel_id=1, replica_groups=mesh['group'=4,'sector'=8] {'group','sector'}, use_global_device_ids=true, to_apply=%region_3.5 | all-reduce | flops 8 | bytes 64 | tf_op jit(solution)/shard_map/psum | solution.py:88
  274.1 40.9 %psum.114 = f32[]{:T(128)} all-reduce(f32[]{:T(128)} %get-tuple-element.315), channel_id=1, replica_groups=mesh['group'=4,'sector'=8] {'group','sector'}, use_global_device_ids=true, to_apply=%region_5.7 | all-reduce | flops 1 | bytes 8 | tf_op jit(solution)/shard_map/psum | solution.py:91
  319.7 7.0 reshape.968
  326.6 5.7 fusion.1
  342.6 39.9 %psum.115 = f32[8]{0:T(128)S(1)} all-reduce(f32[8]{0:T(128)S(1)} %convolution_bitcast_fusion.6), channel_id=1, replica_groups=mesh['group'=4,'sector'=8] {'group','sector'}, use_global_device_ids=true, to_apply=%region_7.9 | all-reduce | flops 8 | bytes 64 | tf_op jit(solution)/shard_map/psum | solution.py:88
  385.7 40.8 %psum.116 = f32[]{:T(128)} all-reduce(f32[]{:T(128)} %get-tuple-element.311), channel_id=1, replica_groups=mesh['group'=4,'sector'=8] {'group','sector'}, use_global_device_ids=true, to_apply=%region_9.11 | all-reduce | flops 1 | bytes 8 | tf_op jit(solution)/shard_map/psum | solution.py:91
  432.2 6.9 reshape.973
  455.1 39.8 %psum.117 = f32[8]{0:T(128)S(1)} all-reduce(f32[8]{0:T(128)S(1)} %convolution_bitcast_fusion.5), channel_id=1, replica_groups=mesh['group'=4,'sector'=8] {'group','sector'}, use_global_device_ids=true, to_apply=%region_11.13 | all-reduce | flops 8 | bytes 64 | tf_op jit(solution)/shard_map/psum | solution.py:88
  498.1 40.9 %psum.118 = f32[]{:T(128)} all-reduce(f32[]{:T(128)} %get-tuple-element.307), channel_id=1, replica_groups=mesh['group'=4,'sector'=8] {'group','sector'}, use_global_device_ids=true, to_apply=%region_13.15 | all-reduce | flops 1 | bytes 8 | tf_op jit(solution)/shard_map/psum | solution.py:91
  544.6 6.9 reshape.978
  567.5 40.0 %psum.119 = f32[8]{0:T(128)S(1)} all-reduce(f32[8]{0:T(128)S(1)} %convolution_bitcast_fusion.4), channel_id=1, replica_groups=mesh['group'=4,'sector'=8] {'group','sector'}, use_global_device_ids=true, to_apply=%region_15.17 | all-reduce | flops 8 | bytes 64 | tf_op jit(solution)/shard_map/psum | solution.py:88
  610.7 40.8 %psum.120 = f32[]{:T(128)} all-reduce(f32[]{:T(128)} %get-tuple-element.303), channel_id=1, replica_groups=mesh['group'=4,'sector'=8] {'group','sector'}, use_global_device_ids=true, to_apply=%region_17.19 | all-reduce | flops 1 | bytes 8 | tf_op jit(solution)/shard_map/psum | solution.py:91
  657.1 6.9 reshape.983
  680.6 39.9 %psum.121 = f32[8]{0:T(128)S(1)} all-reduce(f32[8]{0:T(128)} %convolution_bitcast_fusion.3), channel_id=1, replica_groups=mesh['group'=4,'sector'=8] {'group','sector'}, use_global_device_ids=true, to_apply=%region_19.21 | all-reduce | flops 8 | bytes 64 | tf_op jit(solution)/shard_map/psum | solution.py:88
  723.7 40.9 %psum.122 = f32[]{:T(128)} all-reduce(f32[]{:T(128)} %get-tuple-element.299), channel_id=1, replica_groups=mesh['group'=4,'sector'=8] {'group','sector'}, use_global_device_ids=true, to_apply=%region_21.23 | all-reduce | flops 1 | bytes 8 | tf_op jit(solution)/shard_map/psum | solution.py:91
  770.2 6.9 reshape.988
  793.7 40.1 %psum.123 = f32[8]{0:T(128)} all-reduce(f32[8]{0:T(128)} %convolution_bitcast_fusion.2), channel_id=1, replica_groups=mesh['group'=4,'sector'=8] {'group','sector'}, use_global_device_ids=true, to_apply=%region_23.25 | all-reduce | flops 8 | bytes 64 | tf_op jit(solution)/shard_map/psum | solution.py:88
  837.7 41.2 %psum.124 = f32[]{:T(128)} all-reduce(f32[]{:T(128)} %get-tuple-element.295), channel_id=1, replica_groups=mesh['group'=4,'sector'=8] {'group','sector'}, use_global_device_ids=true, to_apply=%region_25.27 | all-reduce | flops 1 | bytes 8 | tf_op jit(solution)/shard_map/psum | solution.py:91
  884.4 6.9 reshape.993
  907.4 39.5 %psum.125 = f32[8]{0:T(128)S(1)} all-reduce(f32[8]{0:T(128)S(1)} %convolution_bitcast_fusion.1), channel_id=1, replica_groups=mesh['group'=4,'sector'=8] {'group','sector'}, use_global_device_ids=true, to_apply=%region_27.29 | all-reduce | flops 8 | bytes 64 | tf_op jit(solution)/shard_map/psum | solution.py:88
  950.1 41.1 %psum.126 = f32[]{:T(128)} all-reduce(f32[]{:T(128)} %get-tuple-element.291), channel_id=1, replica_groups=mesh['group'=4,'sector'=8] {'group','sector'}, use_global_device_ids=true, to_apply=%region_29.31 | all-reduce | flops 1 | bytes 8 | tf_op jit(solution)/shard_map/psum | solution.py:91
  998.9 7.0 reshape.998
  1019.7 39.6 %psum.127 = f32[8,1]{0,1:T(1,128)S(1)} all-reduce(f32[8,1]{0,1:T(1,128)S(1)} %convolution_bitcast_fusion), channel_id=1, replica_groups=mesh['group'=4,'sector'=8] {'group','sector'}, use_global_device_ids=true, to_apply=%region_30.32 | all-reduce | flops 8 | bytes 64 | tf_op jit(solution)/shard_map/psum | solution.py:88
  (203 shorter events, 230.1 us)
Async XLA Ops:
  27.9 35.1 %all-to-all-start = ((bf16[8,2,32768]{2,1,0:T(2,128)(2,1)}), bf16[8,2,32768]{2,1,0:T(2,128)(2,1)S(1)}, u32[]{:S(2)}, u32[]{:S(2)}) async-start(bf16[8,2,32768]{2,1,0:T(2,128)(2,1)} %reshape.1111), calls=%async_computation | async-start | bytes 2097152 | tf_op jit(solution)/shard_map/all_to_all | solution.py:65
  37.4 32.0 %copy-start.22 = (u32[32]{0:T(128)S(1)}, u32[32]{0:T(128)}, u32[]{:S(2)}) copy-start(u32[32]{0:T(128)} %constant.676) | copy-start | bytes 388
  63.0 35.3 %all-to-all-start.2 = ((bf16[8,2,32768]{2,1,0:T(2,128)(2,1)}), bf16[8,2,32768]{2,1,0:T(2,128)(2,1)}, u32[]{:S(2)}, u32[]{:S(2)}) async-start(bf16[8,2,32768]{2,1,0:T(2,128)(2,1)} %reshape.1109), calls=%async_computation.2 | async-start | bytes 2097152 | tf_op jit(solution)/shard_map/all_to_all | solution.py:66
  98.3 30.1 %all-to-all-start.1 = ((bf16[1,8,512,128]{3,2,0,1:T(8,128)(2,1)}), bf16[1,8,512,128]{3,2,0,1:T(8,128)(2,1)S(1)}, u32[]{:S(2)}, u32[]{:S(2)}) async-start(bf16[1,8,512,128]{3,2,0,1:T(8,128)(2,1)} %fusion.98), calls=%async_computation.1 | async-start | bytes 2097152 | tf_op jit(solution)/shard_map/all_to_all | solution.py:70
  106.2 25.7 %copy-start.8 = (f32[1,128,4,128]{3,2,1,0:T(4,128)S(1)}, f32[1,128,4,128]{3,2,1,0:T(4,128)}, u32[]{:S(2)}) copy-start(f32[1,128,4,128]{3,2,1,0:T(4,128)} %param.55) | copy-start | bytes 786436
  106.2 73.3 %copy-start.11 = (bf16[8,32,256]{2,1,0:T(8,128)(2,1)S(1)}, bf16[8,32,256]{2,1,0:T(8,128)(2,1)}, u32[]{:S(2)}) copy-start(bf16[8,32,256]{2,1,0:T(8,128)(2,1)} %param.56) | copy-start | bytes 393220
  107.4 83.8 %copy-start.19 = (s32[1,4]{1,0:T(1,128)S(1)}, s32[1,4]{1,0:T(1,128)}, u32[]{:S(2)}) copy-start(s32[1,4]{1,0:T(1,128)} %param.61) | copy-start | bytes 52
  107.4 89.3 %copy-start.9 = (f32[1,128,4,128]{3,2,1,0:T(4,128)S(1)}, f32[1,128,4,128]{3,2,1,0:T(4,128)}, u32[]{:S(2)}) copy-start(f32[1,128,4,128]{3,2,1,0:T(4,128)} %param.55) | copy-start | bytes 786436
  128.4 86.0 %all-to-all-start.3 = ((bf16[1,8,512,128]{3,2,0,1:T(8,128)(2,1)}), bf16[1,8,512,128]{3,2,0,1:T(8,128)(2,1)S(1)}, u32[]{:S(2)}, u32[]{:S(2)}) async-start(bf16[1,8,512,128]{3,2,0,1:T(8,128)(2,1)} %fusion.97), calls=%async_computation.3 | async-start | bytes 2097152 | tf_op jit(solution)/shard_map/all_to_all | solution.py:71
  191.9 14.9 %copy-start.12 = (bf16[32,4,32,4,1]{0,2,1,4,3:T(8,128)(2,1)}, bf16[32,4,32,4,1]{0,2,1,4,3:T(8,128)(2,1)S(1)}, u32[]{:S(2)}) copy-start(bf16[32,4,32,4,1]{0,2,1,4,3:T(8,128)(2,1)S(1)} %copy.138) | copy-start | bytes 98308
  214.4 4.1 copy-start
  218.5 0.7 copy-start.10
  270.7 45.0 %copy-start.20 = (f32[8]{0:T(128)}, f32[8]{0:T(128)S(1)}, u32[]{:S(2)}) copy-start(f32[8]{0:T(128)S(1)} %psum.113) | copy-start | bytes 100
  319.7 7.0 copy-start.13
  326.6 5.7 copy-start.1
  439.1 5.7 copy-start.2
  551.5 5.7 copy-start.3
  664.1 5.7 copy-start.4
  777.1 5.7 copy-start.5
  891.4 5.7 copy-start.6
  898.4 93.4 %copy-start.21 = (f32[8]{0:T(128)S(1)}, f32[8]{0:T(128)}, u32[]{:S(2)}) copy-start(f32[8]{0:T(128)} %copy-done.20) | copy-start | bytes 100
  946.9 47.8 %copy-start.16 = (f32[8]{0:T(128)}, f32[8]{0:T(128)S(1)}, u32[]{:S(2)}) copy-start(f32[8]{0:T(128)S(1)} %psum.125) | copy-start | bytes 100
  998.9 7.0 copy-start.14
  1005.8 5.7 copy-start.7
  1011.6 8.1 copy-start.18
  1011.6 51.1 %copy-start.15 = (f32[8]{0:T(128)S(1)}, f32[8]{0:T(128)}, u32[]{:S(2)}) copy-start(f32[8]{0:T(128)} %psum.123) | copy-start | bytes 100
  1011.6 51.9 %copy-start.17 = (f32[8]{0:T(128)S(1)}, f32[8]{0:T(128)}, u32[]{:S(2)}) copy-start(f32[8]{0:T(128)} %copy-done.16) | copy-start | bytes 100
where the time goes:
time: 1080 us; the launch traced here: 1070 us
  blocking collectives  694 us (64%)
  matrix products  142 us (13%)
  local copies, waits for them, and re-layouts  110 us (10%)
  other arithmetic  81 us (8%)
  starting transfers between devices  18.5 us (2%)
  waiting for transfers between devices  17.7 us (2%)
    psum x8, blocking collectives, local(): projection = lax.psum(local_projection, ('group', 'sector'))  326 us
    psum x7, blocking collectives, local(): norm_sq = lax.psum(jnp.sum(remainder * remainder), ('group', 'sector'))  287 us
    another operation x9, local copies, waits for them, and re-layouts  55.6 us
    dot_general x8, matrix products, apply_sector(): jnp.einsum('aiqj,aqcp->cipj', inner, mixing, preferred_element_type=jnp.f...  47.6 us
    psum x1, blocking collectives, local(): start_sq = lax.psum(jnp.sum(flattened * flattened), ('group', 'sector'))  46.1 us
    unnamed x2, other arithmetic  45.8 us
    dot_general x8, matrix products, local(): local_projection = jnp.dot(krylov_basis, applied, precision=HIGH)  38 us
    scatter x7, local copies, waits for them, and re-layouts, local(): krylov_basis = krylov_basis.at[column + 1].set(remainder / subdiag)  26.8 us
  transfers between devices with their start and end apart: 4, of which 1 were waited for; matrix products, arithmetic and copies ran while one was open for 6% of the time, Pallas kernels for 0%

commit v1 on v0

v1 whole, which is shorter than its diff:
```python
import jax
import jax.numpy as jnp
from jax import lax
from jax.experimental import pallas as pl
from jax.experimental.pallas import tpu as pltpu
from jax.sharding import PartitionSpec as P

KRYLOV = 8
LOCAL = 16
TAU = 3.0
EPS = 1e-06
TINY = 1e-30
LANES = 128
STREAMS = 2
OWN = 4
FIXED_ROUNDS = 5
TAIL_ROUNDS = 7
SLOTS = 64
LINE = 4


def spread_rows(x, axis, combine, fallback):
    count = lax.axis_size(axis)
    if count & (count - 1):
        return fallback(x, axis)
    while count > 1:
        radix = 4 if count % 4 == 0 else 2
        count //= radix
        size = lax.axis_size(axis)
        others = [
            lax.ppermute(x, axis, [(k, k ^ (count * turn)) for k in range(size)])
            for turn in range(1, radix)
        ]
        for other in others:
            x = combine(x, other)
    return x


def select_mix(slices, states):
    pairs = states[:, None] * LOCAL + states[None, :]
    choose = (
        jnp.arange(slices[0].shape[2], dtype=jnp.int32)[None, None, :] == pairs[:, :, None]
    ).astype(jnp.bfloat16)
    panel = jnp.concatenate(slices, axis=0)
    mixed = jnp.einsum("acz,qpz->cpqa", panel, choose, preferred_element_type=jnp.float32)
    return mixed.astype(jnp.bfloat16)


def arrange_mix(mixed, share):
    group = lax.axis_size("group")
    turned = (group - lax.axis_index("group")) % group * share
    mixed = lax.dynamic_slice_in_dim(
        jnp.concatenate([mixed, mixed], axis=3), turned, mixed.shape[3], axis=3
    )
    channels, phys = mixed.shape[0], mixed.shape[1]
    same = jnp.eye(2, dtype=jnp.bfloat16)
    both = mixed[:, None, :, None] * same[None, :, None, :, None, None]
    return both.reshape(channels * 2 * phys, 2 * phys * channels)


def krylov_kernel(table_ref, me_ref, state_ref, mix_ref, theirs_ref, *refs):
    pieces, refs = refs[:-10], refs[-10:]
    basis_ref, stats_ref, mine_ref, wide_ref, rows_ref, turned_ref, x_ref, m_ref, w_ref, sems = refs
    channels, size = theirs_ref.shape[1], theirs_ref.shape[2]
    loads = []
    if pieces:
        loads = [
            held_copies(kind, 0, me_ref, table_ref, pieces, mine_ref.at[kind], sems)
            for kind in range(2)
        ]
        for copies in loads:
            run_copies(copies, "start")
    phys = state_ref.shape[0] // size
    count = basis_ref.shape[0]
    f32, bf16 = jnp.float32, jnp.bfloat16

    def load_left(part):
        def turn(n, carry):
            for k in range(8):
                wide_ref[pl.ds(8 * n + k, size, stride=channels), :] = part[0, 8 * n + k].astype(f32)
            return carry

        lax.fori_loop(0, channels // 8, turn, 0)

    def load_right(part):
        def turn(n, carry):
            for k in range(8):
                at = pl.multiple_of((8 * n + k) * size, size)
                turned_ref[pl.ds(at, size), :] = part[1, 8 * n + k].T
            return carry

        lax.fori_loop(0, channels // 8, turn, 0)

    for kind, load in enumerate((load_left, load_right)):
        here = table_ref[1, kind] >= 0
        if loads:
            run_copies(loads[kind], "wait")

        @pl.when(here)
        def _(load=load):
            load(mine_ref)

        @pl.when(jnp.logical_not(here))
        def _(load=load):
            load(theirs_ref)

    rows_ref[...] = wide_ref[...].astype(bf16)

    basis_ref[...] = jnp.zeros_like(basis_ref)
    start = state_ref[...]
    start_sq = jnp.sum(start * start, keepdims=True)
    start_scale = jnp.sqrt(jnp.maximum(start_sq, TINY))
    basis_ref[0] = start / start_scale

    sub = lax.broadcasted_iota(jnp.int32, (8, LANES), 0)
    lane = lax.broadcasted_iota(jnp.int32, (8, LANES), 1)
    stats = jnp.where((sub == 7) & (lane == 7), start_scale, 0.0)

    group_rows = 4 * channels
    chunk = 64
    once = 64

    def column(j, stats):
        for q in range(phys):
            x_ref[:, q * size : (q + 1) * size] = basis_ref[
                j, pl.ds(q, size, stride=phys), :
            ].astype(bf16)

        def part(n, carry):
            for k in range(chunk // 4):
                if k % (once // 4) == 0:
                    at = n * chunk * channels + k * group_rows
                    at = pl.multiple_of(at, once * channels)
                    z = jnp.dot(
                        rows_ref[pl.ds(at, once * channels), :],
                        x_ref[...],
                        preferred_element_type=f32,
                    ).astype(bf16)
                first = k % (once // 4) * group_rows
                four = z[first : first + group_rows]
                halves = []
                for h in range(2):
                    pieces = []
                    for i2 in range(2):
                        base = (2 * h + i2) * channels
                        for q in range(phys):
                            pieces.append(
                                four[base : base + channels, q * size : (q + 1) * size]
                            )
                    halves.append(jnp.concatenate(pieces, axis=0))
                mixed = jnp.dot(
                    mix_ref[...], jnp.concatenate(halves, axis=1), preferred_element_type=f32
                )
                to = pl.multiple_of(n * chunk * phys, chunk * phys) + k * 4 * phys
                for c in range(channels):
                    block = mixed[c * 2 * phys : (c + 1) * 2 * phys]
                    m_ref[pl.ds(to, 4 * phys), c * size : (c + 1) * size] = jnp.concatenate(
                        [block[:, :size], block[:, size:]], axis=0
                    ).astype(bf16)
            return carry

        lax.fori_loop(0, size // chunk, part, 0)
        step = 64
        half = size * phys // 2
        sums = [jnp.zeros((8, LANES), f32) for _ in range(count + 1)]
        for start in range(0, size * phys, half):
            whole = jnp.dot(
                m_ref[start : start + half, :], turned_ref[...], preferred_element_type=f32
            )
            w_ref[start : start + half, :] = whole
            for at in range(start, start + half, step):
                w = whole[at - start : at - start + step]
                for i in range(count):
                    product = basis_ref[i, at : at + step, :] * w
                    sums[i] = sums[i] + jnp.sum(product.reshape(step // 8, 8, LANES), axis=0)
                sums[count] = sums[count] + jnp.sum((w * w).reshape(step // 8, 8, LANES), axis=0)
        stacked = jnp.zeros((8, LANES), f32)
        for i in range(count):
            stacked = jnp.where(sub == i, jnp.sum(sums[i], axis=0, keepdims=True), stacked)
        h = jnp.sum(stacked, axis=1, keepdims=True)
        w_sq = jnp.sum(sums[count], keepdims=True)
        left_sq = w_sq - jnp.sum(h * h, axis=0, keepdims=True)
        scale = jnp.sqrt(jnp.maximum(jnp.maximum(left_sq, 1e-10 * w_sq), TINY))
        inverse = 1.0 / scale

        @pl.when(j + 1 < count)
        def _():
            for at in range(0, size * phys, step):
                rest = w_ref[at : at + step, :]
                for i in range(count):
                    rest = rest - h[i : i + 1, :] * basis_ref[i, at : at + step, :]
                basis_ref[j + 1, at : at + step, :] = rest * inverse

        entry = jnp.where((sub == j + 1), scale, jnp.broadcast_to(h, (8, LANES)))
        return stats + jnp.where(lane == 8 * j + sub, entry, 0.0)

    stats = lax.fori_loop(0, count, column, stats)

    pairs = [(i, k) for i in range(count) for k in range(i + 1)]

    def gram(r, sums):
        for part in range(4):
            at = pl.multiple_of((4 * r + part) * 8, 8)
            rows = [basis_ref[i, pl.ds(at, 8), :] for i in range(count)]
            sums = [total + rows[i] * rows[k] for total, (i, k) in zip(sums, pairs)]
        return sums

    totals = lax.fori_loop(
        0, size * phys // 32, gram, [jnp.zeros((8, LANES), f32) for _ in pairs]
    )
    for (i, k), total in zip(pairs, totals):
        value = jnp.sum(total, keepdims=True)
        here = (lane == 64 + 8 * i + k) | (lane == 64 + 8 * k + i)
        stats = stats + jnp.where(here & (sub == 0), value, 0.0)
    seats = lax.broadcasted_iota(jnp.int32, stats_ref.shape, 0)
    stats_ref[...] = jnp.where(seats == me_ref[0], jnp.sum(stats, axis=0, keepdims=True), 0.0)


def schedule(origin, reach, own_slot, rows):
    sub = lax.broadcasted_iota(jnp.int32, (rows, LANES), 0)
    lane = lax.broadcasted_iota(jnp.int32, (rows, LANES), 1)
    wanted = (origin <= sub) & (reach > sub)
    score = jnp.where(wanted, (reach * LANES + lane) * SLOTS, -1)
    ready = jnp.where(wanted & (origin == sub), score + own_slot, -1)
    later = jnp.where(origin == sub, -1, score)

    def step(carry, turn):
        ready, later, held, table, used = carry
        best = jnp.max(ready, axis=1, keepdims=True)
        chosen = (ready == best) & (best >= 0)
        table = jnp.where(lane == turn, jnp.where(best >= 0, best & (SLOTS - 1), -1), table)
        used = jnp.where(jnp.max(best, axis=0, keepdims=True) >= 0, turn + 1, used)
        passed = jnp.where(chosen, 1, 0)
        arrived = jnp.concatenate([jnp.zeros((1, LANES), jnp.int32), passed[:-1]], axis=0) > 0
        slot = OWN + turn
        ready = jnp.where(chosen, -1, ready)
        ready = jnp.where(arrived & (later >= 0), later + slot, ready)
        later = jnp.where(arrived, -1, later)
        return ready, later, jnp.where(arrived, slot, held), table, used

    start = jnp.zeros((rows, LANES), jnp.int32)
    return (ready, later, start, start - 1, jnp.zeros((1, 1), jnp.int32)), step


def route_kernel(sectors, where_ref, lists_ref, table_ref, count_ref):
    chips = sectors // 2
    rows = -(-chips // 8) * 8
    lane = lax.broadcasted_iota(jnp.int32, (1, LANES), 1)
    valid = lane < 2 * sectors
    block = lane % sectors
    origin = jnp.where(valid, block // 2, chips)
    own_slot = 2 * (lane // sectors) + block % 2
    reach = jnp.full((1, LANES), -1, jnp.int32)
    back = jnp.full((1, LANES), -1, jnp.int32)
    for k in range(sectors):
        asked = jnp.where(lane < sectors, lists_ref[0, 2 * k], lists_ref[0, 2 * k + 1])
        hit = (block == asked) & valid
        reach = jnp.where(hit, k // 2, reach)
        back = jnp.where(hit, jnp.maximum(back, chips - 1 - k // 2), back)
    right, right_step = schedule(origin, reach, own_slot, rows)
    mirrored = jnp.where(valid, chips - 1 - origin, chips)
    left, left_step = schedule(mirrored, back, own_slot, rows)

    def busy(carry):
        _, right, left = carry
        return jnp.maximum(jnp.max(right[0]), jnp.max(left[0])) >= 0

    def step(carry):
        turn, right, left = carry
        return turn + 1, right_step(right, turn), left_step(left, turn)

    carry = (jnp.int32(0), right, left)
    for _ in range(FIXED_ROUNDS):
        carry = step(carry)
    _, right, left = lax.while_loop(busy, step, carry)
    me = where_ref[0]
    chip = me // 2
    sub = lax.broadcasted_iota(jnp.int32, (rows, LANES), 0)

    def row(array, index):
        return jnp.sum(jnp.where(sub == index, array, 0), axis=0, keepdims=True)

    core = me % 2
    arrived = jnp.where(core == 0, row(right[2], chip), row(left[2], chips - 1 - chip))
    behind = ((chip - origin) * (1 - 2 * core) > 0) & valid
    ends = jnp.full((1, LANES), -1, jnp.int32)
    for at, owner in enumerate((me, me + 1 - 2 * core)):
        for kind in range(2):
            hit = lane == kind * sectors + lists_ref[0, 2 * owner + kind]
            slot = jnp.where(behind, arrived, -1)
            if at == 0:
                slot = jnp.where(origin == chip, own_slot, slot)
            slot = jnp.sum(jnp.where(hit, slot + 1, 0), axis=1, keepdims=True) - 1
            ends = jnp.where(lane == 2 * at + kind, slot, ends)
    sends = jnp.where(core == 0, row(right[3] + 1, chip), row(left[3] + 1, chips - 1 - chip)) - 1
    table_ref[...] = jnp.concatenate([sends, ends, jnp.zeros((6, LANES), jnp.int32)], axis=0)
    count_ref[...] = jnp.broadcast_to(jnp.maximum(right[4], left[4]), (8, LANES))


def fetches(slot, stream, core, target, sem, blocks, pieces, tail):
    share = target.shape[0]
    half = pl.ds(stream * share, share)
    sources = []
    for at, block in enumerate(blocks):
        kind, other = at % 2, at // 2
        seat = core if other == 0 else 1 - core
        sources.append((slot == 2 * kind + seat, block.at[half]))
    for at, piece in enumerate(pieces):
        sources.append((slot == OWN + at, piece))
    if tail is not None:
        base = OWN + FIXED_ROUNDS
        sources.append((slot >= base, tail.at[jnp.clip(slot - base, 0, tail.shape[0] - 1)]))
    return [(use, pltpu.make_async_copy(source, target, sem)) for use, source in sources]


def run_copies(copies, verb):
    for use, copy in copies:

        @pl.when(use)
        def _(copy=copy):
            getattr(copy, verb)()


def stage_kernel(stream, has_tail, turn_ref, where_ref, table_ref, *refs):
    blocks, pieces, (out_ref, sem) = refs[:4], list(refs[4:-2]), refs[-2:]
    tail = pieces.pop() if has_tail else None
    slot = table_ref[0, turn_ref[0]]
    copies = fetches(slot, stream, where_ref[0] % 2, out_ref, sem.at[0], blocks, pieces, tail)
    run_copies(copies, "start")
    run_copies(copies, "wait")


def held_copies(kind, at, where_ref, table_ref, pieces, target, sems):
    blocks, pieces, tails = pieces[:4], pieces[4:-STREAMS], pieces[-STREAMS:]
    share = target.shape[0] // STREAMS
    copies = []
    for stream in range(STREAMS):
        copies += fetches(
            table_ref[1, 2 * at + kind],
            stream,
            where_ref[0] % 2,
            target.at[pl.ds(stream * share, share)],
            sems.at[kind * STREAMS + stream],
            blocks,
            pieces[stream * FIXED_ROUNDS : (stream + 1) * FIXED_ROUNDS],
            tails[stream],
        )
    return copies


def last_kernel(where_ref, table_ref, *refs):
    pieces, (out_ref, sems) = refs[:-2], refs[-2:]
    copies = []
    for kind in range(2):
        copies += held_copies(kind, 1, where_ref, table_ref, pieces, out_ref.at[kind], sems)
    run_copies(copies, "start")
    run_copies(copies, "wait")


def small_product(a, b):
    total = a[:, 0:1] * b[0:1, :]
    for k in range(1, 8):
        total = total + a[:, k : k + 1] * b[k : k + 1, :]
    return total


def finish_kernel(entries, me_ref, all_ref, basis_ref, state_ref, hess_ref):
    f32 = jnp.float32
    count = basis_ref.shape[0]
    sectors = all_ref.shape[0]
    data = all_ref[...]
    if sectors < LANES:
        data = jnp.concatenate([data, jnp.zeros((LANES - sectors, LANES), f32)], axis=0)
    data = data.T
    width = data.shape[1]
    sub = lax.broadcasted_iota(jnp.int32, (8, width), 0)
    lane = lax.broadcasted_iota(jnp.int32, (8, width), 1)
    start = data[7:8, :]
    moves = [data[8 * j : 8 * j + 8, :] for j in range(count)]
    moves[0] = jnp.where(sub == 7, 0.0, moves[0])
    grams = [data[64 + 8 * j : 64 + 8 * j + 8, :] for j in range(count)]

    def combine(columns, x, upto=count):
        total = columns[0] * x[0:1, :]
        for b in range(1, upto):
            total = total + columns[b] * x[b : b + 1, :]
        return total

    inner = [combine(grams, moves[j]) for j in range(count - 1)] + [moves[count - 1]]
    start_sq = jnp.sum(start * start * grams[0][0:1, :], axis=1, keepdims=True)
    basis = [jnp.where(sub == 0, start / jnp.sqrt(start_sq + EPS), 0.0)]
    hess = jnp.zeros((8, width), f32)
    for t in range(count):
        seen = combine(inner, basis[t], t + 1)
        stacked = jnp.zeros((8, width), f32)
        for s in range(t + 1):
            stacked = jnp.where(sub == s, jnp.sum(basis[s] * seen, axis=0, keepdims=True), stacked)
        h = jnp.sum(stacked, axis=1, keepdims=True)
        hess = jnp.where((lane == t) & (sub <= t), h, hess)
        if t + 1 < count:
            rest = combine(moves, basis[t], t + 1)
            for s in range(t + 1):
                rest = rest - h[s : s + 1, :] * basis[s]
            rest_sq = jnp.sum(rest * combine(grams, rest), keepdims=True)
            beta = jnp.sqrt(jnp.maximum(rest_sq, 0.0) + EPS)
            hess = jnp.where((lane == t) & (sub == t + 1), beta, hess)
            basis.append(rest / beta)
    hess_ref[...] = hess[:, :count]

    scaled = -TAU / 16.0 * hess
    term = jnp.where((sub == lane), 1.0, 0.0)
    series = term
    for order in range(1, 11):
        term = small_product(term, scaled) / float(order)
        series = series + term
    for square in range(4):
        series = small_product(series, series)
    coefficients = series[:, 0:1]
    norm = jnp.sum(coefficients * coefficients, axis=0, keepdims=True)
    rescale = jnp.sqrt(jnp.float32(entries)) / jnp.sqrt(norm)
    mine = jnp.zeros((8, width), f32)
    for t in range(count):
        mine = mine + coefficients[t : t + 1, :] * basis[t]
    mine = jnp.sum(jnp.where(lane == me_ref[0], mine, 0.0), axis=1, keepdims=True) * rescale
    step = 64
    for at in range(0, state_ref.shape[0], step):
        total = mine[0:1, :] * basis_ref[0, at : at + step, :]
        for i in range(1, count):
            total = total + mine[i : i + 1, :] * basis_ref[i, at : at + step, :]
        state_ref[at : at + step, :] = total


def shifted(x, step):
    group = lax.axis_size("group")
    return lax.ppermute(x, "group", [((k + step) % group, k) for k in range(group)])


def fetch_blocks(left_env, right_env, lists, mixing, sectors, me):
    channels, size = left_env.shape[0], left_env.shape[1]
    share = channels // STREAMS
    bf16 = left_env.dtype
    small = pl.BlockSpec(memory_space=pltpu.SMEM)
    whole = pl.BlockSpec(memory_space=pltpu.VMEM)
    place = pl.BlockSpec(memory_space=pl.ANY)
    swap = [(k, k + 1 - 2 * (k % 2)) for k in range(sectors)]
    along = [(k, k + 2) for k in range(0, sectors - 2, 2)]
    along += [(k, k - 2) for k in range(3, sectors, 2)]

    def pieces_of(*lead):
        return jax.ShapeDtypeStruct(lead + (share, size, size), bf16)

    where = me.reshape(1)
    blocks = [left_env, right_env] + [
        lax.ppermute(env, "sector", swap) for env in (left_env, right_env)
    ]
    table, count = pl.pallas_call(
        lambda *refs: route_kernel(sectors, *refs),
        out_shape=(jax.ShapeDtypeStruct((8, LANES), jnp.int32),) * 2,
        in_specs=[small, small],
        out_specs=(whole, whole),
        name="route",
    )(where, lists)
    rounds = spread_rows(count, "group", jnp.maximum, lax.pmax)[0, 0]

    def stage(stream, turn, held, tail=None):
        inputs = blocks + held + ([] if tail is None else [tail])
        return pl.pallas_call(
            lambda *refs: stage_kernel(stream, tail is not None, *refs),
            out_shape=pieces_of(),
            in_specs=[small] * 3 + [place] * len(inputs),
            out_specs=whole,
            scratch_shapes=[pltpu.SemaphoreType.DMA((1,))],
            name="stage",
        )(jnp.asarray(turn, jnp.int32).reshape(1), where, table, *inputs)

    held = [[] for _ in range(STREAMS)]
    for turn in range(FIXED_ROUNDS):
        for stream in range(STREAMS):
            flow = stage(stream, turn, held[stream])
            if (turn, stream) == (2, 0):
                flow, mixing = lax.optimization_barrier((flow, mixing))
            held[stream] = held[stream] + [lax.ppermute(flow, "sector", along)]

    def more(carry):
        return carry[0] < rounds

    def again(carry):
        turn, tails = carry
        moved = [
            lax.ppermute(stage(stream, turn, held[stream], tails[stream]), "sector", along)
            for stream in range(STREAMS)
        ]
        tails = [
            lax.dynamic_update_slice_in_dim(tail, piece[None], turn - FIXED_ROUNDS, axis=0)
            for tail, piece in zip(tails, moved)
        ]
        return turn + 1, tails

    room = pl.pallas_call(
        lambda *refs: None,
        out_shape=tuple(pieces_of(TAIL_ROUNDS) for _ in range(STREAMS)),
        out_specs=tuple(place for _ in range(STREAMS)),
        name="room",
    )()
    _, tails = lax.while_loop(more, again, (jnp.int32(FIXED_ROUNDS), list(room)))

    pieces = blocks + [piece for each in held for piece in each] + tails
    theirs = pl.pallas_call(
        last_kernel,
        out_shape=jax.ShapeDtypeStruct((2, channels, size, size), bf16),
        in_specs=[small] * 2 + [place] * len(pieces),
        out_specs=whole,
        scratch_shapes=[pltpu.SemaphoreType.DMA((2 * STREAMS,))],
        name="last",
    )(where, table, *pieces)
    return table, mixing, lax.ppermute(theirs, "sector", swap), pieces


def spread_blocks(left_env, right_env, lists, sectors):
    channels, size = left_env.shape[0], left_env.shape[1]
    sides = []
    for side, env in enumerate((left_env, right_env)):
        pieces = env.reshape(sectors, channels // sectors, size, size)
        spread = lax.all_to_all(pieces, "sector", split_axis=0, concat_axis=0, tiled=True)
        sends = jnp.take(spread, lists[0, side : 2 * sectors : 2], axis=0, mode="clip")
        sides.append(
            lax.all_to_all(sends, "sector", split_axis=0, concat_axis=0, tiled=True).reshape(
                channels, size, size
            )
        )
    return jnp.stack(sides)


def local(state, panel, left_env, right_env, left_match, right_match, phys_states):
    _, size, phys, _ = state.shape
    channels = left_env.shape[1]
    sector_count = lax.axis_size("sector")
    seat = lax.axis_index("sector").astype(jnp.int32)

    lane = lax.broadcasted_iota(jnp.int32, (8, LANES), 1)
    lists = jnp.where(lane == 2 * seat + 1, right_match, -1)
    lists = jnp.where(lane == 2 * seat, left_match, lists)
    lists = spread_rows(lists, "sector", jnp.maximum, lax.pmax)

    slices = [panel] + [shifted(panel, step) for step in range(1, lax.axis_size("group"))]
    mixing = arrange_mix(select_mix(slices, phys_states[0]), panel.shape[0])
    if sector_count <= 2 * LINE:
        table, mixing, theirs, pieces = fetch_blocks(
            left_env[0], right_env[0], lists, mixing, sector_count, seat
        )
    else:
        theirs, pieces = spread_blocks(left_env[0], right_env[0], lists, sector_count), []
        table = jnp.full((8, LANES), -1, jnp.int32)

    whole = pl.BlockSpec(memory_space=pltpu.VMEM)
    rows, f32, bf16 = size * phys, jnp.float32, jnp.bfloat16
    small = pl.BlockSpec(memory_space=pltpu.SMEM)
    place = pl.BlockSpec(memory_space=pl.ANY)
    devices = lax.axis_size("group") * sector_count
    me = (lax.axis_index("group").astype(jnp.int32) * sector_count + seat).reshape(1)
    basis, stats = pl.pallas_call(
        krylov_kernel,
        out_shape=(
            jax.ShapeDtypeStruct((KRYLOV, rows, size), f32),
            jax.ShapeDtypeStruct((devices, LANES), f32),
        ),
        in_specs=[small] * 2 + [whole] * 3 + [place] * len(pieces),
        out_specs=(whole, whole),
        scratch_shapes=[
            pltpu.VMEM((2, channels, size, size), bf16),
            pltpu.VMEM((channels * size, size), f32),
            pltpu.VMEM((channels * size, size), bf16),
            pltpu.VMEM((channels * size, size), bf16),
            pltpu.VMEM((size, rows), bf16),
            pltpu.VMEM((rows, channels * size), bf16),
            pltpu.VMEM((rows, size), f32),
            pltpu.SemaphoreType.DMA((2 * STREAMS,)),
        ],
        compiler_params=pltpu.CompilerParams(vmem_limit_bytes=40 * 1024 * 1024),
        name="krylov",
    )(table, me, state.reshape(rows, size), mixing, theirs, *pieces)

    gathered = spread_rows(stats, "sector", jnp.add, lax.psum)
    gathered = spread_rows(gathered, "group", jnp.add, lax.psum)
    entries = rows * size * devices
    evolved, hessenberg = pl.pallas_call(
        lambda *refs: finish_kernel(entries, *refs),
        out_shape=(
            jax.ShapeDtypeStruct((rows, size), f32),
            jax.ShapeDtypeStruct((KRYLOV, KRYLOV), f32),
        ),
        in_specs=[small, whole, whole],
        out_specs=(whole, whole),
        compiler_params=pltpu.CompilerParams(vmem_limit_bytes=24 * 1024 * 1024),
        name="finish",
    )(me, gathered, basis)
    return (evolved.reshape(state.shape), hessenberg)


def solution(mesh):
    return jax.shard_map(
        local,
        mesh=mesh,
        in_specs=(
            P(("group", "sector"), None, None, None),
            P("group", None, None),
            P(("group", "sector"), None, None, None),
            P(("group", "sector"), None, None, None),
            P(("group", "sector")),
            P(("group", "sector")),
            P(("group", "sector"), None),
        ),
        out_specs=(P(("group", "sector"), None, None, None), P()),
        check_vma=False,
    )
```

time: 1080 us -> 158 us (0.15)
  blocking collectives: 694 us -> 0 us
  matrix products: 142 us -> 1.58 us
  local copies, waits for them, and re-layouts: 110 us -> 3.14 us
  other arithmetic: 81 us -> 2.21 us
  Pallas kernels: 0 us -> 64.9 us
  starting transfers between devices: 18.5 us -> 63.2 us
    psum x16 -> x0, blocking collectives: 658 us -> none  [the longest x8 326 us: local(): projection = lax.psum(local_projection, ('group', 'sector'))]
    dot_general x55 -> x1, matrix products: 142 us -> 1.58 us  [select_mix(): jnp.einsum('acz,qpz->cpqa', panel, choose, preferred_element_type=jnp.flo...]
    pallas_call x0 -> x15, Pallas kernels: none -> 64.9 us  [the longest x1 37.7 us: local(): pl.pallas_call(krylov_kernel, out_shape=(jax.ShapeDtypeStruct((KRYLOV, ro...]
    ppermute x0 -> x30, starting transfers between devices: none -> 63.2 us  [the longest x10 40.5 us: fetch_blocks(): held[stream] = held[stream] + [lax.ppermute(flow, 'sector', along)]]
    another operation x9 -> x0, local copies, waits for them, and re-layouts: 55.6 us -> none
    unnamed x2 -> x0, other arithmetic: 45.8 us -> none
    scatter x23 -> x0, local copies, waits for them, and re-layouts: 28.1 us -> none  [the longest x7 26.8 us: local(): krylov_basis = krylov_basis.at[column + 1].set(remainder / subdiag)]
    unnamed x1 -> x0, blocking collectives: 23.7 us -> none
  transfers between devices with their start and end apart: 4 -> 30, of which waited for: 1 -> 13; matrix products, arithmetic and copies ran while one was open for 6% -> 4% of each run, Pallas kernels for 0% -> 13%
where the time goes in v1:
time: 158 us
  Pallas kernels  64.9 us (41%)
  starting transfers between devices  63.2 us (40%)
  waiting for transfers between devices  20.1 us (13%)
  local copies, waits for them, and re-layouts  3.14 us (2%)
  between operations  2.29 us (1%)
  other arithmetic  2.21 us (1%)
  matrix products  1.58 us (1%)
    ppermute x10, starting transfers between devices, fetch_blocks(): held[stream] = held[stream] + [lax.ppermute(flow, 'sector', along)]  40.5 us
    pallas_call x1, Pallas kernels, local(): pl.pallas_call(krylov_kernel, out_shape=(jax.ShapeDtypeStruct((KRYLOV, ro...  37.7 us
    pallas_call x10, Pallas kernels, stage(): pl.pallas_call(lambda *refs: stage_kernel(stream, tail is not None, *refs...  18.7 us
    ppermute x14, starting transfers between devices, spread_rows(): lax.ppermute(x, axis, [(k, k ^ count * turn) for k in range(size)])  18.4 us
    ppermute x14, waiting for transfers between devices, spread_rows(): lax.ppermute(x, axis, [(k, k ^ count * turn) for k in range(size)])  13.7 us
    ppermute x1, waiting for transfers between devices, fetch_blocks(): return (table, mixing, lax.ppermute(theirs, 'sector', swap), pieces)  4.35 us
    pallas_call x1, Pallas kernels, local(): pl.pallas_call(lambda *refs: finish_kernel(entries, *refs), out_shape=(ja...  4.03 us
    ppermute x3, starting transfers between devices, shifted(): lax.ppermute(x, 'group', [((k + step) % group, k) for k in range(group)])  3.66 us
  transfers between devices with their start and end apart: 30, of which 13 were waited for; matrix products, arithmetic and copies ran while one was open for 4% of the time, Pallas kernels for 13%

profile of v1, /device:TPU:0, one launch (start us, length us, event | category | flops | bytes accessed | tf_op | source)
XLA Modules:
  0.0 158.2 jit_solution(14022106286058089872)
XLA Ops:
  2.6 4.1 %collective-permute-start.3 = (s32[8,128]{1,0:T(8,128)S(1)}, s32[8,128]{1,0:T(8,128)S(1)}, u32[]{:S(2)}, u32[]{:S(2)}) collective-permute-start(s32[8,128]{1,0:T(8,128)S(1)} %broadcast_select_fusion), channel_id=1, source_target_pairs={{0,4},{1,5},{2,6},{3,7},{4,0},{5,1},{6,2},{7,3},{8,12},{9,13},{10,... | collective-permute-start | bytes 12296 | tf_op jit(solution)/shard_map/ppermute | solution.py:31
  8.3 3.8 %collective-permute-done.4 = s32[8,128]{1,0:T(8,128)S(1)} collective-permute-done((s32[8,128]{1,0:T(8,128)S(1)}, s32[8,128]{1,0:T(8,128)S(1)}, u32[]{:S(2)}, u32[]{:S(2)}) %collective-permute-start.4) | collective-permute-done | bytes 4128 | tf_op jit(solution)/shard_map/ppermute | solution.py:31
  12.2 1.6 %collective-permute-start.11 = (bf16[8,32,256]{2,1,0:T(8,128)(2,1)}, bf16[8,32,256]{2,1,0:T(8,128)(2,1)}, u32[]{:S(2)}, u32[]{:S(2)}) collective-permute-start(bf16[8,32,256]{2,1,0:T(8,128)(2,1)} %param.10), channel_id=1, source_target_pairs={{16,0},{24,8},{0,16},{8,24},{17,1},{25,9},{1,17},{9,25},{18,2},{26... | collective-permute-start | bytes 393224 | tf_op jit(solution)/shard_map/ppermute | solution.py:435
  15.8 2.4 %route.1 = (s32[8,128]{1,0:T(8,128)S(1)}, s32[8,128]{1,0:T(8,128)}) custom-call(s32[1]{0:T(128)} %bitcast.4.refs_0_.refs_1_.where_ref, s32[8,128]{1,0:T(8,128)} %max.24.refs_1_), custom_call_target="tpu_custom_call" | custom-call | tf_op jit(solution)/shard_map/route/pallas_call | solution.py:456
  18.2 2.5 %stage.24 = bf16[16,128,128]{2,1,0:T(8,128)(2,1)} custom-call(s32[1]{0:T(128)} %constant.67.clone.1.refs_0_, s32[1]{0:T(128)} %bitcast.4.refs_0_.refs_1_.where_ref, s32[8,128]{1,0:T(8,128)S(1)} %get-tuple-element.565.refs_2_.table_ref, bf16[32,128,128]{2,1,0:T(8,128)(2,1)} %bitcast.37, bf16[32,128,128]{2,1,0:T(8,128)(2,1)} %bitcast.49, ...), custom_call_target="tpu_custom_call" | custom-call | tf_op jit(solution)/shard_map/stage/pallas_call | solution.py:467
  20.7 1.7 %collective-permute-start.8 = (bf16[16,128,128]{2,1,0:T(8,128)(2,1)}, bf16[16,128,128]{2,1,0:T(8,128)(2,1)S(1)}, u32[]{:S(2)}, u32[]{:S(2)}) collective-permute-start(bf16[16,128,128]{2,1,0:T(8,128)(2,1)} %stage.24), channel_id=1, source_target_pairs={{0,2},{2,4},{4,6},{3,1},{5,3},{7,5},{8,10},{10,12},{12,14},{11,9},... | collective-permute-start | bytes 1572872 | tf_op jit(solution)/shard_map/ppermute | solution.py:482
  22.4 2.5 %stage.29 = bf16[16,128,128]{2,1,0:T(8,128)(2,1)} custom-call(s32[1]{0:T(128)} %constant.67.clone.1.refs_0_, s32[1]{0:T(128)} %bitcast.4.refs_0_.refs_1_.where_ref, s32[8,128]{1,0:T(8,128)S(1)} %get-tuple-element.565.refs_2_.table_ref, bf16[32,128,128]{2,1,0:T(8,128)(2,1)S(1)} %bitcast.38, bf16[32,128,128]{2,1,0:T(8,128)(2,1)S(1)} %bitcast.50, ...), custom_call_target="tpu_custom_call" | custom-call | tf_op jit(solution)/shard_map/stage/pallas_call | solution.py:467
  24.9 3.9 %collective-permute-start.16 = (bf16[16,128,128]{2,1,0:T(8,128)(2,1)}, bf16[16,128,128]{2,1,0:T(8,128)(2,1)S(1)}, u32[]{:S(2)}, u32[]{:S(2)}) collective-permute-start(bf16[16,128,128]{2,1,0:T(8,128)(2,1)} %stage.29), channel_id=1, source_target_pairs={{0,2},{2,4},{4,6},{3,1},{5,3},{7,5},{8,10},{10,12},{12,14},{11,9},... | collective-permute-start | bytes 1572872 | tf_op jit(solution)/shard_map/ppermute | solution.py:482
  29.6 2.5 %stage.25 = bf16[16,128,128]{2,1,0:T(8,128)(2,1)} custom-call(s32[1]{0:T(128)} %constant.68.clone.1.refs_0_, s32[1]{0:T(128)} %bitcast.4.refs_0_.refs_1_.where_ref, s32[8,128]{1,0:T(8,128)S(1)} %get-tuple-element.565.refs_2_.table_ref, bf16[32,128,128]{2,1,0:T(8,128)(2,1)S(1)} %bitcast.39, bf16[32,128,128]{2,1,0:T(8,128)(2,1)S(1)} %bitcast.51, ...), custom_call_target="tpu_custom_call" | custom-call | tf_op jit(solution)/shard_map/stage/pallas_call | solution.py:467
  32.0 3.9 %collective-permute-start.9 = (bf16[16,128,128]{2,1,0:T(8,128)(2,1)}, bf16[16,128,128]{2,1,0:T(8,128)(2,1)}, u32[]{:S(2)}, u32[]{:S(2)}) collective-permute-start(bf16[16,128,128]{2,1,0:T(8,128)(2,1)} %stage.25), channel_id=1, source_target_pairs={{0,2},{2,4},{4,6},{3,1},{5,3},{7,5},{8,10},{10,12},{12,14},{11,9},... | collective-permute-start | bytes 1572872 | tf_op jit(solution)/shard_map/ppermute | solution.py:482
  35.9 2.5 %stage.30 = bf16[16,128,128]{2,1,0:T(8,128)(2,1)} custom-call(s32[1]{0:T(128)} %constant.68.clone.1.refs_0_, s32[1]{0:T(128)} %bitcast.4.refs_0_.refs_1_.where_ref, s32[8,128]{1,0:T(8,128)S(1)} %get-tuple-element.565.refs_2_.table_ref, bf16[32,128,128]{2,1,0:T(8,128)(2,1)S(1)} %bitcast.40, bf16[32,128,128]{2,1,0:T(8,128)(2,1)S(1)} %bitcast.52, ...), custom_call_target="tpu_custom_call" | custom-call | tf_op jit(solution)/shard_map/stage/pallas_call | solution.py:467
  38.4 4.0 %collective-permute-start.17 = (bf16[16,128,128]{2,1,0:T(8,128)(2,1)}, bf16[16,128,128]{2,1,0:T(8,128)(2,1)}, u32[]{:S(2)}, u32[]{:S(2)}) collective-permute-start(bf16[16,128,128]{2,1,0:T(8,128)(2,1)} %stage.30), channel_id=1, source_target_pairs={{0,2},{2,4},{4,6},{3,1},{5,3},{7,5},{8,10},{10,12},{12,14},{11,9},... | collective-permute-start | bytes 1572872 | tf_op jit(solution)/shard_map/ppermute | solution.py:482
  42.4 1.6 fusion
  47.1 1.5 stage.26
  48.6 4.1 %collective-permute-start.13 = (bf16[16,128,128]{2,1,0:T(8,128)(2,1)}, bf16[16,128,128]{2,1,0:T(8,128)(2,1)}, u32[]{:S(2)}, u32[]{:S(2)}) collective-permute-start(bf16[16,128,128]{2,1,0:T(8,128)(2,1)} %stage.26), channel_id=1, source_target_pairs={{0,2},{2,4},{4,6},{3,1},{5,3},{7,5},{8,10},{10,12},{12,14},{11,9},... | collective-permute-start | bytes 1572872 | tf_op jit(solution)/shard_map/ppermute | solution.py:482
  52.7 1.5 stage.31
  54.2 3.2 %collective-permute-start.18 = (bf16[16,128,128]{2,1,0:T(8,128)(2,1)}, bf16[16,128,128]{2,1,0:T(8,128)(2,1)}, u32[]{:S(2)}, u32[]{:S(2)}) collective-permute-start(bf16[16,128,128]{2,1,0:T(8,128)(2,1)} %stage.31), channel_id=1, source_target_pairs={{0,2},{2,4},{4,6},{3,1},{5,3},{7,5},{8,10},{10,12},{12,14},{11,9},... | collective-permute-start | bytes 1572872 | tf_op jit(solution)/shard_map/ppermute | solution.py:482
  57.4 1.5 collective-permute-done.13.refs_9_.refs_6_
  60.4 6.2 %collective-permute-start.14 = (bf16[16,128,128]{2,1,0:T(8,128)(2,1)}, bf16[16,128,128]{2,1,0:T(8,128)(2,1)}, u32[]{:S(2)}, u32[]{:S(2)}) collective-permute-start(bf16[16,128,128]{2,1,0:T(8,128)(2,1)} %stage.27), channel_id=1, source_target_pairs={{0,2},{2,4},{4,6},{3,1},{5,3},{7,5},{8,10},{10,12},{12,14},{11,9},... | collective-permute-start | bytes 1572872 | tf_op jit(solution)/shard_map/ppermute | solution.py:482
  68.0 4.2 %collective-permute-start.19 = (bf16[16,128,128]{2,1,0:T(8,128)(2,1)}, bf16[16,128,128]{2,1,0:T(8,128)(2,1)}, u32[]{:S(2)}, u32[]{:S(2)}) collective-permute-start(bf16[16,128,128]{2,1,0:T(8,128)(2,1)} %stage.32), channel_id=1, source_target_pairs={{0,2},{2,4},{4,6},{3,1},{5,3},{7,5},{8,10},{10,12},{12,14},{11,9},... | collective-permute-start | bytes 1572872 | tf_op jit(solution)/shard_map/ppermute | solution.py:482
  72.8 1.5 stage.28
  74.3 5.2 %collective-permute-start.15 = (bf16[16,128,128]{2,1,0:T(8,128)(2,1)}, bf16[16,128,128]{2,1,0:T(8,128)(2,1)}, u32[]{:S(2)}, u32[]{:S(2)}) collective-permute-start(bf16[16,128,128]{2,1,0:T(8,128)(2,1)} %stage.28), channel_id=1, source_target_pairs={{0,2},{2,4},{4,6},{3,1},{5,3},{7,5},{8,10},{10,12},{12,14},{11,9},... | collective-permute-start | bytes 1572872 | tf_op jit(solution)/shard_map/ppermute | solution.py:482
  81.0 4.1 %collective-permute-start.20 = (bf16[16,128,128]{2,1,0:T(8,128)(2,1)}, bf16[16,128,128]{2,1,0:T(8,128)(2,1)}, u32[]{:S(2)}, u32[]{:S(2)}) collective-permute-start(bf16[16,128,128]{2,1,0:T(8,128)(2,1)} %stage.33), channel_id=1, source_target_pairs={{0,2},{2,4},{4,6},{3,1},{5,3},{7,5},{8,10},{10,12},{12,14},{11,9},... | collective-permute-start | bytes 1572872 | tf_op jit(solution)/shard_map/ppermute | solution.py:482
  85.1 2.0 %collective-permute-start.22 = (s32[8,128]{1,0:T(8,128)S(1)}, s32[8,128]{1,0:T(8,128)S(1)}, u32[]{:S(2)}, u32[]{:S(2)}) collective-permute-start(s32[8,128]{1,0:T(8,128)S(1)} %copy-done.5), channel_id=1, source_target_pairs={{0,16},{8,24},{16,0},{24,8},{1,17},{9,25},{17,1},{25,9},{2,18},{10... | collective-permute-start | bytes 12296 | tf_op jit(solution)/shard_map/ppermute | solution.py:31
  92.9 2.1 %last.1 = bf16[2,32,128,128]{3,2,1,0:T(8,128)(2,1)} custom-call(s32[1]{0:T(128)} %bitcast.4.refs_0_.refs_1_.where_ref, s32[8,128]{1,0:T(8,128)S(1)} %get-tuple-element.647, bf16[32,128,128]{2,1,0:T(8,128)(2,1)S(1)} %get-tuple-element.637, bf16[32,128,128]{2,1,0:T(8,128)(2,1)S(1)} %get-tuple-element.639, ...), custom_call_target="tpu_custom_call" | custom-call | tf_op jit(solution)/shard_map/last/pallas_call | solution.py:508
  95.2 4.3 %collective-permute-done.24.theirs_ref = bf16[2,32,128,128]{3,2,1,0:T(8,128)(2,1)S(1)} collective-permute-done((bf16[2,32,128,128]{3,2,1,0:T(8,128)(2,1)}, bf16[2,32,128,128]{3,2,1,0:T(8,128)(2,1)S(1)}, u32[]{:S(2)}, u32[]{:S(2)}) %collective-permute-start.24) | collective-permute-done | bytes 2097184 | tf_op jit(solution)/shard_map/ppermute | solution.py:516
  99.5 37.7 %krylov.1 = (f32[8,512,128]{2,1,0:T(8,128)S(1)}, f32[32,128]{1,0:T(8,128)S(1)}) custom-call(s32[8,128]{1,0:T(8,128)S(1)} %get-tuple-element.647, s32[1]{0:T(128)} %bitcast.3.me_ref.refs_0_, f32[512,128]{1,0:T(8,128)S(1)} %bitcast.35, bf16[256,256]{1,0:T(8,128)(2,1)S(1)} %mul.42.mix_ref, bf16[2,32,128,128]{3,2,1,0:T(8,128)(2,1)S(1)} %collective-permute-done.24.theirs_ref, ...), custom_call_target="tpu_custom_call" | custom-call | tf_op jit(solution)/shard_map/krylov/pallas_call | solution.py:561
  137.2 3.9 %collective-permute-start.27 = (f32[32,128]{1,0:T(8,128)S(1)}, f32[32,128]{1,0:T(8,128)S(1)}, u32[]{:S(2)}, u32[]{:S(2)}) collective-permute-start(f32[32,128]{1,0:T(8,128)S(1)} %get-tuple-element.394), channel_id=1, source_target_pairs={{0,6},{1,7},{2,4},{3,5},{4,2},{5,3},{6,0},{7,1},{8,14},{9,15},{10,... | collective-permute-start | bytes 49160 | tf_op jit(solution)/shard_map/ppermute | solution.py:31
  142.8 2.9 %collective-permute-done.26 = f32[32,128]{1,0:T(8,128)S(1)} collective-permute-done((f32[32,128]{1,0:T(8,128)S(1)}, f32[32,128]{1,0:T(8,128)S(1)}, u32[]{:S(2)}, u32[]{:S(2)}) %collective-permute-start.26) | collective-permute-done | bytes 16416 | tf_op jit(solution)/shard_map/ppermute | solution.py:31
  147.9 2.5 %collective-permute-start.30 = (f32[32,128]{1,0:T(8,128)S(1)}, f32[32,128]{1,0:T(8,128)S(1)}, u32[]{:S(2)}, u32[]{:S(2)}) collective-permute-start(f32[32,128]{1,0:T(8,128)S(1)} %add.91), channel_id=1, source_target_pairs={{0,16},{8,24},{16,0},{24,8},{1,17},{9,25},{17,1},{25,9},{2,18},{10... | collective-permute-start | bytes 49160 | tf_op jit(solution)/shard_map/ppermute | solution.py:31
  152.1 2.0 %collective-permute-done.29 = f32[32,128]{1,0:T(8,128)S(1)} collective-permute-done((f32[32,128]{1,0:T(8,128)S(1)}, f32[32,128]{1,0:T(8,128)S(1)}, u32[]{:S(2)}, u32[]{:S(2)}) %collective-permute-start.29) | collective-permute-done | bytes 16416 | tf_op jit(solution)/shard_map/ppermute | solution.py:31
  154.1 4.0 %finish.1 = (f32[512,128]{1,0:T(8,128)}, f32[8,8]{1,0:T(8,128)}) custom-call(s32[1]{0:T(128)} %bitcast.3.me_ref.refs_0_, f32[32,128]{1,0:T(8,128)S(1)} %add_add_fusion.refs_1_, f32[8,512,128]{2,1,0:T(8,128)S(1)} %get-tuple-element.395.refs_2_), custom_call_target="tpu_custom_call" | custom-call | tf_op jit(solution)/shard_map/finish/pallas_call | solution.py:586
  (78 shorter events, 24.5 us)
Async XLA Ops:
  0.6 21.8 %copy-start.1 = (bf16[1,32,128,128]{3,2,1,0:T(8,128)(2,1)S(1)}, bf16[1,32,128,128]{3,2,1,0:T(8,128)(2,1)}, u32[]{:S(2)}) copy-start(bf16[1,32,128,128]{3,2,1,0:T(8,128)(2,1)} %param.11) | copy-start | bytes 3145732
  0.6 21.8 %copy-start.2 = (bf16[1,32,128,128]{3,2,1,0:T(8,128)(2,1)S(1)}, bf16[1,32,128,128]{3,2,1,0:T(8,128)(2,1)}, u32[]{:S(2)}) copy-start(bf16[1,32,128,128]{3,2,1,0:T(8,128)(2,1)} %param.12) | copy-start | bytes 3145732
  0.7 17.5 %collective-permute-start.6 = (bf16[32,128,128]{2,1,0:T(8,128)(2,1)}, bf16[32,128,128]{2,1,0:T(8,128)(2,1)}, u32[]{:S(2)}, u32[]{:S(2)}) collective-permute-start(bf16[32,128,128]{2,1,0:T(8,128)(2,1)} %bitcast.36), channel_id=1, source_target_pairs={{0,1},{1,0},{2,3},{3,2},{4,5},{5,4},{6,7},{7,6},{8,9},{9,8},{10,11... | collective-permute-start | bytes 3145736 | tf_op jit(solution)/shard_map/ppermute | solution.py:454
  1.2 17.0 %collective-permute-start.7 = (bf16[32,128,128]{2,1,0:T(8,128)(2,1)}, bf16[32,128,128]{2,1,0:T(8,128)(2,1)}, u32[]{:S(2)}, u32[]{:S(2)}) collective-permute-start(bf16[32,128,128]{2,1,0:T(8,128)(2,1)} %bitcast.48), channel_id=1, source_target_pairs={{0,1},{1,0},{2,3},{3,2},{4,5},{5,4},{6,7},{7,6},{8,9},{9,8},{10,11... | collective-permute-start | bytes 3145736 | tf_op jit(solution)/shard_map/ppermute | solution.py:454
  2.6 5.7 %collective-permute-start.3 = (s32[8,128]{1,0:T(8,128)S(1)}, s32[8,128]{1,0:T(8,128)S(1)}, u32[]{:S(2)}, u32[]{:S(2)}) collective-permute-start(s32[8,128]{1,0:T(8,128)S(1)} %broadcast_select_fusion), channel_id=1, source_target_pairs={{0,4},{1,5},{2,6},{3,7},{4,0},{5,1},{6,2},{7,3},{8,12},{9,13},{10,... | collective-permute-start | bytes 12296 | tf_op jit(solution)/shard_map/ppermute | solution.py:31
  6.7 5.4 %collective-permute-start.4 = (s32[8,128]{1,0:T(8,128)S(1)}, s32[8,128]{1,0:T(8,128)S(1)}, u32[]{:S(2)}, u32[]{:S(2)}) collective-permute-start(s32[8,128]{1,0:T(8,128)S(1)} %broadcast_select_fusion), channel_id=1, source_target_pairs={{0,6},{1,7},{2,4},{3,5},{4,2},{5,3},{6,0},{7,1},{8,14},{9,15},{10,... | collective-permute-start | bytes 12296 | tf_op jit(solution)/shard_map/ppermute | solution.py:31
  8.1 4.1 %collective-permute-start.2 = (s32[8,128]{1,0:T(8,128)S(1)}, s32[8,128]{1,0:T(8,128)S(1)}, u32[]{:S(2)}, u32[]{:S(2)}) collective-permute-start(s32[8,128]{1,0:T(8,128)S(1)} %broadcast_select_fusion), channel_id=1, source_target_pairs={{0,2},{1,3},{2,0},{3,1},{4,6},{5,7},{6,4},{7,5},{8,10},{9,11},{10,... | collective-permute-start | bytes 12296 | tf_op jit(solution)/shard_map/ppermute | solution.py:31
  12.1 3.1 %collective-permute-start.5 = (s32[8,128]{1,0:T(8,128)S(1)}, s32[8,128]{1,0:T(8,128)S(1)}, u32[]{:S(2)}, u32[]{:S(2)}) collective-permute-start(s32[8,128]{1,0:T(8,128)S(1)} %maximum_maximum_fusion.1), channel_id=1, source_target_pairs={{0,1},{1,0},{2,3},{3,2},{4,5},{5,4},{6,7},{7,6},{8,9},{9,8},{10,11... | collective-permute-start | bytes 12296 | tf_op jit(solution)/shard_map/ppermute | solution.py:31
  12.2 30.2 %collective-permute-start.11 = (bf16[8,32,256]{2,1,0:T(8,128)(2,1)}, bf16[8,32,256]{2,1,0:T(8,128)(2,1)}, u32[]{:S(2)}, u32[]{:S(2)}) collective-permute-start(bf16[8,32,256]{2,1,0:T(8,128)(2,1)} %param.10), channel_id=1, source_target_pairs={{16,0},{24,8},{0,16},{8,24},{17,1},{25,9},{1,17},{9,25},{18,2},{26... | collective-permute-start | bytes 393224 | tf_op jit(solution)/shard_map/ppermute | solution.py:435
  13.8 28.6 %collective-permute-start.10 = (bf16[8,32,256]{2,1,0:T(8,128)(2,1)}, bf16[8,32,256]{2,1,0:T(8,128)(2,1)}, u32[]{:S(2)}, u32[]{:S(2)}) collective-permute-start(bf16[8,32,256]{2,1,0:T(8,128)(2,1)} %param.10), channel_id=1, source_target_pairs={{8,0},{16,8},{24,16},{0,24},{9,1},{17,9},{25,17},{1,25},{10,2},{18... | collective-permute-start | bytes 393224 | tf_op jit(solution)/shard_map/ppermute | solution.py:435
  20.7 8.9 %collective-permute-start.8 = (bf16[16,128,128]{2,1,0:T(8,128)(2,1)}, bf16[16,128,128]{2,1,0:T(8,128)(2,1)S(1)}, u32[]{:S(2)}, u32[]{:S(2)}) collective-permute-start(bf16[16,128,128]{2,1,0:T(8,128)(2,1)} %stage.24), channel_id=1, source_target_pairs={{0,2},{2,4},{4,6},{3,1},{5,3},{7,5},{8,10},{10,12},{12,14},{11,9},... | collective-permute-start | bytes 1572872 | tf_op jit(solution)/shard_map/ppermute | solution.py:482
  24.9 11.0 %collective-permute-start.16 = (bf16[16,128,128]{2,1,0:T(8,128)(2,1)}, bf16[16,128,128]{2,1,0:T(8,128)(2,1)S(1)}, u32[]{:S(2)}, u32[]{:S(2)}) collective-permute-start(bf16[16,128,128]{2,1,0:T(8,128)(2,1)} %stage.29), channel_id=1, source_target_pairs={{0,2},{2,4},{4,6},{3,1},{5,3},{7,5},{8,10},{10,12},{12,14},{11,9},... | collective-permute-start | bytes 1572872 | tf_op jit(solution)/shard_map/ppermute | solution.py:482
  28.9 13.5 %collective-permute-start.12 = (bf16[8,32,256]{2,1,0:T(8,128)(2,1)S(1)}, bf16[8,32,256]{2,1,0:T(8,128)(2,1)}, u32[]{:S(2)}, u32[]{:S(2)}) collective-permute-start(bf16[8,32,256]{2,1,0:T(8,128)(2,1)S(1)} %copy-done.7), channel_id=1, source_target_pairs={{24,0},{0,8},{8,16},{16,24},{25,1},{1,9},{9,17},{17,25},{26,2},{2,... | collective-permute-start | bytes 393224 | tf_op jit(solution)/shard_map/ppermute | solution.py:435
  32.0 15.1 %collective-permute-start.9 = (bf16[16,128,128]{2,1,0:T(8,128)(2,1)}, bf16[16,128,128]{2,1,0:T(8,128)(2,1)}, u32[]{:S(2)}, u32[]{:S(2)}) collective-permute-start(bf16[16,128,128]{2,1,0:T(8,128)(2,1)} %stage.25), channel_id=1, source_target_pairs={{0,2},{2,4},{4,6},{3,1},{5,3},{7,5},{8,10},{10,12},{12,14},{11,9},... | collective-permute-start | bytes 1572872 | tf_op jit(solution)/shard_map/ppermute | solution.py:482
  38.4 14.3 %collective-permute-start.17 = (bf16[16,128,128]{2,1,0:T(8,128)(2,1)}, bf16[16,128,128]{2,1,0:T(8,128)(2,1)}, u32[]{:S(2)}, u32[]{:S(2)}) collective-permute-start(bf16[16,128,128]{2,1,0:T(8,128)(2,1)} %stage.30), channel_id=1, source_target_pairs={{0,2},{2,4},{4,6},{3,1},{5,3},{7,5},{8,10},{10,12},{12,14},{11,9},... | collective-permute-start | bytes 1572872 | tf_op jit(solution)/shard_map/ppermute | solution.py:482
  48.6 10.3 %collective-permute-start.13 = (bf16[16,128,128]{2,1,0:T(8,128)(2,1)}, bf16[16,128,128]{2,1,0:T(8,128)(2,1)}, u32[]{:S(2)}, u32[]{:S(2)}) collective-permute-start(bf16[16,128,128]{2,1,0:T(8,128)(2,1)} %stage.26), channel_id=1, source_target_pairs={{0,2},{2,4},{4,6},{3,1},{5,3},{7,5},{8,10},{10,12},{12,14},{11,9},... | collective-permute-start | bytes 1572872 | tf_op jit(solution)/shard_map/ppermute | solution.py:482
  54.2 12.3 %collective-permute-start.18 = (bf16[16,128,128]{2,1,0:T(8,128)(2,1)}, bf16[16,128,128]{2,1,0:T(8,128)(2,1)}, u32[]{:S(2)}, u32[]{:S(2)}) collective-permute-start(bf16[16,128,128]{2,1,0:T(8,128)(2,1)} %stage.31), channel_id=1, source_target_pairs={{0,2},{2,4},{4,6},{3,1},{5,3},{7,5},{8,10},{10,12},{12,14},{11,9},... | collective-permute-start | bytes 1572872 | tf_op jit(solution)/shard_map/ppermute | solution.py:482
  60.4 12.4 %collective-permute-start.14 = (bf16[16,128,128]{2,1,0:T(8,128)(2,1)}, bf16[16,128,128]{2,1,0:T(8,128)(2,1)}, u32[]{:S(2)}, u32[]{:S(2)}) collective-permute-start(bf16[16,128,128]{2,1,0:T(8,128)(2,1)} %stage.27), channel_id=1, source_target_pairs={{0,2},{2,4},{4,6},{3,1},{5,3},{7,5},{8,10},{10,12},{12,14},{11,9},... | collective-permute-start | bytes 1572872 | tf_op jit(solution)/shard_map/ppermute | solution.py:482
  68.0 11.5 %collective-permute-start.19 = (bf16[16,128,128]{2,1,0:T(8,128)(2,1)}, bf16[16,128,128]{2,1,0:T(8,128)(2,1)}, u32[]{:S(2)}, u32[]{:S(2)}) collective-permute-start(bf16[16,128,128]{2,1,0:T(8,128)(2,1)} %stage.32), channel_id=1, source_target_pairs={{0,2},{2,4},{4,6},{3,1},{5,3},{7,5},{8,10},{10,12},{12,14},{11,9},... | collective-permute-start | bytes 1572872 | tf_op jit(solution)/shard_map/ppermute | solution.py:482
  74.3 17.0 %collective-permute-start.15 = (bf16[16,128,128]{2,1,0:T(8,128)(2,1)}, bf16[16,128,128]{2,1,0:T(8,128)(2,1)}, u32[]{:S(2)}, u32[]{:S(2)}) collective-permute-start(bf16[16,128,128]{2,1,0:T(8,128)(2,1)} %stage.28), channel_id=1, source_target_pairs={{0,2},{2,4},{4,6},{3,1},{5,3},{7,5},{8,10},{10,12},{12,14},{11,9},... | collective-permute-start | bytes 1572872 | tf_op jit(solution)/shard_map/ppermute | solution.py:482
  81.0 10.3 %collective-permute-start.20 = (bf16[16,128,128]{2,1,0:T(8,128)(2,1)}, bf16[16,128,128]{2,1,0:T(8,128)(2,1)}, u32[]{:S(2)}, u32[]{:S(2)}) collective-permute-start(bf16[16,128,128]{2,1,0:T(8,128)(2,1)} %stage.33), channel_id=1, source_target_pairs={{0,2},{2,4},{4,6},{3,1},{5,3},{7,5},{8,10},{10,12},{12,14},{11,9},... | collective-permute-start | bytes 1572872 | tf_op jit(solution)/shard_map/ppermute | solution.py:482
  85.1 4.5 %collective-permute-start.23 = (s32[8,128]{1,0:T(8,128)S(1)}, s32[8,128]{1,0:T(8,128)S(1)}, u32[]{:S(2)}, u32[]{:S(2)}) collective-permute-start(s32[8,128]{1,0:T(8,128)S(1)} %copy-done.5), channel_id=1, source_target_pairs={{0,24},{8,16},{16,8},{24,0},{1,25},{9,17},{17,9},{25,1},{2,26},{10... | collective-permute-start | bytes 12296 | tf_op jit(solution)/shard_map/ppermute | solution.py:31
  85.1 4.5 %collective-permute-start.22 = (s32[8,128]{1,0:T(8,128)S(1)}, s32[8,128]{1,0:T(8,128)S(1)}, u32[]{:S(2)}, u32[]{:S(2)}) collective-permute-start(s32[8,128]{1,0:T(8,128)S(1)} %copy-done.5), channel_id=1, source_target_pairs={{0,16},{8,24},{16,0},{24,8},{1,17},{9,25},{17,1},{25,9},{2,18},{10... | collective-permute-start | bytes 12296 | tf_op jit(solution)/shard_map/ppermute | solution.py:31
  87.2 3.6 %collective-permute-start.21 = (s32[8,128]{1,0:T(8,128)S(1)}, s32[8,128]{1,0:T(8,128)S(1)}, u32[]{:S(2)}, u32[]{:S(2)}) collective-permute-start(s32[8,128]{1,0:T(8,128)S(1)} %copy-done.5), channel_id=1, source_target_pairs={{0,8},{8,0},{16,24},{24,16},{1,9},{9,1},{17,25},{25,17},{2,10},{10... | collective-permute-start | bytes 12296 | tf_op jit(solution)/shard_map/ppermute | solution.py:31
  95.1 4.4 %collective-permute-start.24 = (bf16[2,32,128,128]{3,2,1,0:T(8,128)(2,1)}, bf16[2,32,128,128]{3,2,1,0:T(8,128)(2,1)S(1)}, u32[]{:S(2)}, u32[]{:S(2)}) collective-permute-start(bf16[2,32,128,128]{3,2,1,0:T(8,128)(2,1)} %last.1), channel_id=1, source_target_pairs={{0,1},{1,0},{2,3},{3,2},{4,5},{5,4},{6,7},{7,6},{8,9},{9,8},{10,11... | collective-permute-start | bytes 6291464 | tf_op jit(solution)/shard_map/ppermute | solution.py:516
  137.2 5.6 %collective-permute-start.27 = (f32[32,128]{1,0:T(8,128)S(1)}, f32[32,128]{1,0:T(8,128)S(1)}, u32[]{:S(2)}, u32[]{:S(2)}) collective-permute-start(f32[32,128]{1,0:T(8,128)S(1)} %get-tuple-element.394), channel_id=1, source_target_pairs={{0,6},{1,7},{2,4},{3,5},{4,2},{5,3},{6,0},{7,1},{8,14},{9,15},{10,... | collective-permute-start | bytes 49160 | tf_op jit(solution)/shard_map/ppermute | solution.py:31
  141.1 4.6 %collective-permute-start.26 = (f32[32,128]{1,0:T(8,128)S(1)}, f32[32,128]{1,0:T(8,128)S(1)}, u32[]{:S(2)}, u32[]{:S(2)}) collective-permute-start(f32[32,128]{1,0:T(8,128)S(1)} %get-tuple-element.394), channel_id=1, source_target_pairs={{0,4},{1,5},{2,6},{3,7},{4,0},{5,1},{6,2},{7,3},{8,12},{9,13},{10,... | collective-permute-start | bytes 49160 | tf_op jit(solution)/shard_map/ppermute | solution.py:31
  142.3 3.7 %collective-permute-start.25 = (f32[32,128]{1,0:T(8,128)S(1)}, f32[32,128]{1,0:T(8,128)S(1)}, u32[]{:S(2)}, u32[]{:S(2)}) collective-permute-start(f32[32,128]{1,0:T(8,128)S(1)} %get-tuple-element.394), channel_id=1, source_target_pairs={{0,2},{1,3},{2,0},{3,1},{4,6},{5,7},{6,4},{7,5},{8,10},{9,11},{10,... | collective-permute-start | bytes 49160 | tf_op jit(solution)/shard_map/ppermute | solution.py:31
  146.0 1.2 collective-permute-start.28
  147.2 4.6 %collective-permute-start.31 = (f32[32,128]{1,0:T(8,128)S(1)}, f32[32,128]{1,0:T(8,128)S(1)}, u32[]{:S(2)}, u32[]{:S(2)}) collective-permute-start(f32[32,128]{1,0:T(8,128)S(1)} %add.91), channel_id=1, source_target_pairs={{0,24},{8,16},{16,8},{24,0},{1,25},{9,17},{17,9},{25,1},{2,26},{10... | collective-permute-start | bytes 49160 | tf_op jit(solution)/shard_map/ppermute | solution.py:31
  147.9 4.2 %collective-permute-start.30 = (f32[32,128]{1,0:T(8,128)S(1)}, f32[32,128]{1,0:T(8,128)S(1)}, u32[]{:S(2)}, u32[]{:S(2)}) collective-permute-start(f32[32,128]{1,0:T(8,128)S(1)} %add.91), channel_id=1, source_target_pairs={{0,16},{8,24},{16,0},{24,8},{1,17},{9,25},{17,1},{25,9},{2,18},{10... | collective-permute-start | bytes 49160 | tf_op jit(solution)/shard_map/ppermute | solution.py:31
  150.4 3.7 %collective-permute-start.29 = (f32[32,128]{1,0:T(8,128)S(1)}, f32[32,128]{1,0:T(8,128)S(1)}, u32[]{:S(2)}, u32[]{:S(2)}) collective-permute-start(f32[32,128]{1,0:T(8,128)S(1)} %add.91), channel_id=1, source_target_pairs={{0,8},{8,0},{16,24},{24,16},{1,9},{9,1},{17,25},{25,17},{2,10},{10... | collective-permute-start | bytes 49160 | tf_op jit(solution)/shard_map/ppermute | solution.py:31
  (6 other events, 40.5 us)

commit v2 on v1

--- a/solution.py
+++ b/solution.py
@@ -63,16 +63,24 @@
     basis_ref, stats_ref, mine_ref, wide_ref, rows_ref, turned_ref, x_ref, m_ref, w_ref, sems = refs
     channels, size = theirs_ref.shape[1], theirs_ref.shape[2]
     loads = []
-    if pieces:
-        loads = [
-            held_copies(kind, 0, me_ref, table_ref, pieces, mine_ref.at[kind], sems)
-            for kind in range(2)
-        ]
-        for copies in loads:
-            run_copies(copies, "start")
+    for kind in range(2):
+        copies = []
+        if pieces:
+            copies = held_copies(kind, 0, me_ref, table_ref, pieces, mine_ref.at[kind], sems)
+        received = pltpu.make_async_copy(
+            theirs_ref.at[kind], mine_ref.at[kind], sems.at[2 * STREAMS + kind]
+        )
+        loads.append(copies + [(table_ref[1, kind] < 0, received)])
+        run_copies(loads[kind], "start")
     phys = state_ref.shape[0] // size
     count = basis_ref.shape[0]
     f32, bf16 = jnp.float32, jnp.bfloat16
+
+    basis_ref[...] = jnp.zeros_like(basis_ref)
+    start = state_ref[...]
+    start_sq = jnp.sum(start * start, keepdims=True)
+    start_scale = jnp.sqrt(jnp.maximum(start_sq, TINY))
+    basis_ref[0] = start / start_scale
 
     def load_left(part):
         def turn(n, carry):
@@ -92,25 +100,10 @@
         lax.fori_loop(0, channels // 8, turn, 0)
 
     for kind, load in enumerate((load_left, load_right)):
-        here = table_ref[1, kind] >= 0
-        if loads:
-            run_copies(loads[kind], "wait")
-
-        @pl.when(here)
-        def _(load=load):
-            load(mine_ref)
-
-        @pl.when(jnp.logical_not(here))
-        def _(load=load):
-            load(theirs_ref)
+        run_copies(loads[kind], "wait")
+        load(mine_ref)
 
     rows_ref[...] = wide_ref[...].astype(bf16)
-
-    basis_ref[...] = jnp.zeros_like(basis_ref)
-    start = state_ref[...]
-    start_sq = jnp.sum(start * start, keepdims=True)
-    start_scale = jnp.sqrt(jnp.maximum(start_sq, TINY))
-    basis_ref[0] = start / start_scale
 
     sub = lax.broadcasted_iota(jnp.int32, (8, LANES), 0)
     lane = lax.broadcasted_iota(jnp.int32, (8, LANES), 1)
@@ -208,10 +201,17 @@
     totals = lax.fori_loop(
         0, size * phys // 32, gram, [jnp.zeros((8, LANES), f32) for _ in pairs]
     )
-    for (i, k), total in zip(pairs, totals):
-        value = jnp.sum(total, keepdims=True)
-        here = (lane == 64 + 8 * i + k) | (lane == 64 + 8 * k + i)
-        stats = stats + jnp.where(here & (sub == 0), value, 0.0)
+    for first in range(0, len(pairs), 8):
+        stacked = jnp.zeros((8, LANES), f32)
+        place = jnp.full((8, LANES), -1, jnp.int32)
+        mirror = place
+        for row, (i, k) in enumerate(pairs[first : first + 8]):
+            value = jnp.sum(totals[first + row], axis=0, keepdims=True)
+            stacked = jnp.where(sub == row, value, stacked)
+            place = jnp.where(sub == row, 64 + 8 * i + k, place)
+            mirror = jnp.where(sub == row, 64 + 8 * k + i, mirror)
+        value = jnp.sum(stacked, axis=1, keepdims=True)
+        stats = stats + jnp.where((lane == place) | (lane == mirror), value, 0.0)
     seats = lax.broadcasted_iota(jnp.int32, stats_ref.shape, 0)
     stats_ref[...] = jnp.where(seats == me_ref[0], jnp.sum(stats, axis=0, keepdims=True), 0.0)
 
@@ -364,11 +364,14 @@
     return total
 
 
-def finish_kernel(entries, me_ref, all_ref, basis_ref, state_ref, hess_ref):
+def finish_kernel(entries, me_ref, *refs):
     f32 = jnp.float32
+    parts, (basis_ref, state_ref, hess_ref) = refs[:-3], refs[-3:]
     count = basis_ref.shape[0]
-    sectors = all_ref.shape[0]
-    data = all_ref[...]
+    sectors = parts[0].shape[0]
+    data = parts[0][...]
+    for part in parts[1:]:
+        data = data + part[...]
     if sectors < LANES:
         data = jnp.concatenate([data, jnp.zeros((LANES - sectors, LANES), f32)], axis=0)
     data = data.T
@@ -481,11 +484,23 @@
                 flow, mixing = lax.optimization_barrier((flow, mixing))
             held[stream] = held[stream] + [lax.ppermute(flow, "sector", along)]
 
+    def exchange(tails):
+        pieces = blocks + [piece for each in held for piece in each] + tails
+        theirs = pl.pallas_call(
+            last_kernel,
+            out_shape=jax.ShapeDtypeStruct((2, channels, size, size), bf16),
+            in_specs=[small] * 2 + [place] * len(pieces),
+            out_specs=whole,
+            scratch_shapes=[pltpu.SemaphoreType.DMA((2 * STREAMS,))],
+            name="last",
+        )(where, table, *pieces)
+        return lax.ppermute(theirs, "sector", swap)
+
     def more(carry):
         return carry[0] < rounds
 
     def again(carry):
-        turn, tails = carry
+        turn, tails, _ = carry
         moved = [
             lax.ppermute(stage(stream, turn, held[stream], tails[stream]), "sector", along)
             for stream in range(STREAMS)
@@ -494,7 +509,7 @@
             lax.dynamic_update_slice_in_dim(tail, piece[None], turn - FIXED_ROUNDS, axis=0)
             for tail, piece in zip(tails, moved)
         ]
-        return turn + 1, tails
+        return turn + 1, tails, exchange(tails)
 
     room = pl.pallas_call(
         lambda *refs: None,
@@ -502,18 +517,11 @@
         out_specs=tuple(place for _ in range(STREAMS)),
         name="room",
     )()
-    _, tails = lax.while_loop(more, again, (jnp.int32(FIXED_ROUNDS), list(room)))
-
+    _, tails, theirs = lax.while_loop(
+        more, again, (jnp.int32(FIXED_ROUNDS), list(room), exchange(list(room)))
+    )
     pieces = blocks + [piece for each in held for piece in each] + tails
-    theirs = pl.pallas_call(
-        last_kernel,
-        out_shape=jax.ShapeDtypeStruct((2, channels, size, size), bf16),
-        in_specs=[small] * 2 + [place] * len(pieces),
-        out_specs=whole,
-        scratch_shapes=[pltpu.SemaphoreType.DMA((2 * STREAMS,))],
-        name="last",
-    )(where, table, *pieces)
-    return table, mixing, lax.ppermute(theirs, "sector", swap), pieces
+    return table, mixing, theirs, pieces
 
 
 def spread_blocks(left_env, right_env, lists, sectors):
@@ -564,7 +572,7 @@
             jax.ShapeDtypeStruct((KRYLOV, rows, size), f32),
             jax.ShapeDtypeStruct((devices, LANES), f32),
         ),
-        in_specs=[small] * 2 + [whole] * 3 + [place] * len(pieces),
+        in_specs=[small] * 2 + [whole] * 2 + [place] * (1 + len(pieces)),
         out_specs=(whole, whole),
         scratch_shapes=[
             pltpu.VMEM((2, channels, size, size), bf16),
@@ -574,14 +582,16 @@
             pltpu.VMEM((size, rows), bf16),
             pltpu.VMEM((rows, channels * size), bf16),
             pltpu.VMEM((rows, size), f32),
-            pltpu.SemaphoreType.DMA((2 * STREAMS,)),
+            pltpu.SemaphoreType.DMA((2 * STREAMS + 2,)),
         ],
         compiler_params=pltpu.CompilerParams(vmem_limit_bytes=40 * 1024 * 1024),
         name="krylov",
     )(table, me, state.reshape(rows, size), mixing, theirs, *pieces)
 
     gathered = spread_rows(stats, "sector", jnp.add, lax.psum)
-    gathered = spread_rows(gathered, "group", jnp.add, lax.psum)
+    gathered = [gathered] + [
+        shifted(gathered, step) for step in range(1, lax.axis_size("group"))
+    ]
     entries = rows * size * devices
     evolved, hessenberg = pl.pallas_call(
         lambda *refs: finish_kernel(entries, *refs),
@@ -589,11 +599,11 @@
             jax.ShapeDtypeStruct((rows, size), f32),
             jax.ShapeDtypeStruct((KRYLOV, KRYLOV), f32),
         ),
-        in_specs=[small, whole, whole],
+        in_specs=[small] + [whole] * (len(gathered) + 1),
         out_specs=(whole, whole),
         compiler_params=pltpu.CompilerParams(vmem_limit_bytes=24 * 1024 * 1024),
         name="finish",
-    )(me, gathered, basis)
+    )(me, *gathered, basis)
     return (evolved.reshape(state.shape), hessenberg)
 
 

time: 158 us -> 160 us (1.013)
  waiting for transfers between devices: 20.1 us -> 23.7 us
  Pallas kernels: 64.9 us -> 62.5 us
    ppermute x10, waiting for transfers between devices: 2.08 us -> 8.83 us  [fetch_blocks(): held[stream] = held[stream] + [lax.ppermute(flow, 'sector', along)]]
    ppermute x14 -> x11, starting transfers between devices: 18.4 us -> 13.8 us  [spread_rows(): lax.ppermute(x, axis, [(k, k ^ count * turn) for k in range(size)])]
    ppermute x1, waiting for transfers between devices: 4.35 us -> 0.01 us  [exchange(): return lax.ppermute(theirs, 'sector', swap)]
    ppermute x3 -> x6, starting transfers between devices: 3.66 us -> 7.33 us  [shifted(): lax.ppermute(x, 'group', [((k + step) % group, k) for k in range(group)])]
    pallas_call x10, Pallas kernels: 18.7 us -> 15.6 us  [stage(): pl.pallas_call(lambda *refs: stage_kernel(stream, tail is not None, *refs...]
    ppermute x3 -> x6, waiting for transfers between devices: 0.01 us -> 2.85 us  [shifted(): lax.ppermute(x, 'group', [((k + step) % group, k) for k in range(group)])]
    ppermute x14 -> x11, waiting for transfers between devices: 13.7 us -> 12.1 us  [spread_rows(): lax.ppermute(x, axis, [(k, k ^ count * turn) for k in range(size)])]
  transfers between devices with their start and end apart: 30 -> 30, of which waited for: 13 -> 15; matrix products, arithmetic and copies ran while one was open for 4% -> 4% of each run, Pallas kernels for 13% -> 11%
where the time goes in v2:
time: 160 us; the launch traced here: 159 us
  starting transfers between devices  63.6 us (40%)
  Pallas kernels  62.5 us (39%)
  waiting for transfers between devices  23.7 us (15%)
  local copies, waits for them, and re-layouts  2.43 us (2%)
  between operations  2.23 us (1%)
  other arithmetic  2.19 us (1%)
    ppermute x10, starting transfers between devices, fetch_blocks(): held[stream] = held[stream] + [lax.ppermute(flow, 'sector', along)]  41.8 us
    pallas_call x1, Pallas kernels, local(): pl.pallas_call(krylov_kernel, out_shape=(jax.ShapeDtypeStruct((KRYLOV, ro...  38.4 us
    pallas_call x10, Pallas kernels, stage(): pl.pallas_call(lambda *refs: stage_kernel(stream, tail is not None, *refs...  15.6 us
    ppermute x11, starting transfers between devices, spread_rows(): lax.ppermute(x, axis, [(k, k ^ count * turn) for k in range(size)])  13.8 us
    ppermute x11, waiting for transfers between devices, spread_rows(): lax.ppermute(x, axis, [(k, k ^ count * turn) for k in range(size)])  12.1 us
    ppermute x10, waiting for transfers between devices, fetch_blocks(): held[stream] = held[stream] + [lax.ppermute(flow, 'sector', along)]  8.83 us
    ppermute x6, starting transfers between devices, shifted(): lax.ppermute(x, 'group', [((k + step) % group, k) for k in range(group)])  7.33 us
    pallas_call x1, Pallas kernels, local(): pl.pallas_call(lambda *refs: finish_kernel(entries, *refs), out_shape=(ja...  4.03 us
  transfers between devices with their start and end apart: 30, of which 15 were waited for; matrix products, arithmetic and copies ran while one was open for 4% of the time, Pallas kernels for 11%

profile of v2, /device:TPU:0, one launch (start us, length us, event | category | flops | bytes accessed | tf_op | source)
XLA Modules:
  0.0 158.9 jit_solution(6748384125747169253)
XLA Ops:
  2.6 4.1 %collective-permute-start.4 = (s32[8,128]{1,0:T(8,128)S(1)}, s32[8,128]{1,0:T(8,128)S(1)}, u32[]{:S(2)}, u32[]{:S(2)}) collective-permute-start(s32[8,128]{1,0:T(8,128)S(1)} %broadcast_select_fusion), channel_id=1, source_target_pairs={{0,4},{1,5},{2,6},{3,7},{4,0},{5,1},{6,2},{7,3},{8,12},{9,13},{10,... | collective-permute-start | bytes 12296 | tf_op jit(solution)/shard_map/ppermute | solution.py:31
  8.3 3.8 %collective-permute-done.5 = s32[8,128]{1,0:T(8,128)S(1)} collective-permute-done((s32[8,128]{1,0:T(8,128)S(1)}, s32[8,128]{1,0:T(8,128)S(1)}, u32[]{:S(2)}, u32[]{:S(2)}) %collective-permute-start.5) | collective-permute-done | bytes 4128 | tf_op jit(solution)/shard_map/ppermute | solution.py:31
  12.2 1.6 collective-permute-start.12
  15.8 2.4 %route.1 = (s32[8,128]{1,0:T(8,128)S(1)}, s32[8,128]{1,0:T(8,128)}) custom-call(s32[1]{0:T(128)} %bitcast.4.refs_0_.refs_1_.where_ref, s32[8,128]{1,0:T(8,128)} %max.24.refs_1_), custom_call_target="tpu_custom_call" | custom-call | tf_op jit(solution)/shard_map/route/pallas_call | solution.py:459
  18.2 2.4 %stage.24 = bf16[16,128,128]{2,1,0:T(8,128)(2,1)} custom-call(s32[1]{0:T(128)} %constant.67.clone.1.refs_0_, s32[1]{0:T(128)} %bitcast.4.refs_0_.refs_1_.where_ref, s32[8,128]{1,0:T(8,128)S(1)} %get-tuple-element.586.refs_2_.table_ref, bf16[32,128,128]{2,1,0:T(8,128)(2,1)} %bitcast.37, bf16[32,128,128]{2,1,0:T(8,128)(2,1)} %bitcast.50, ...), custom_call_target="tpu_custom_call" | custom-call | tf_op jit(solution)/shard_map/stage/pallas_call | solution.py:470
  20.6 2.5 %collective-permute-start.9 = (bf16[16,128,128]{2,1,0:T(8,128)(2,1)}, bf16[16,128,128]{2,1,0:T(8,128)(2,1)}, u32[]{:S(2)}, u32[]{:S(2)}) collective-permute-start(bf16[16,128,128]{2,1,0:T(8,128)(2,1)} %stage.24), channel_id=1, source_target_pairs={{0,2},{2,4},{4,6},{3,1},{5,3},{7,5},{8,10},{10,12},{12,14},{11,9},... | collective-permute-start | bytes 1572872 | tf_op jit(solution)/shard_map/ppermute | solution.py:485
  23.2 1.5 stage.29
  24.7 3.9 %collective-permute-start.17 = (bf16[16,128,128]{2,1,0:T(8,128)(2,1)}, bf16[16,128,128]{2,1,0:T(8,128)(2,1)}, u32[]{:S(2)}, u32[]{:S(2)}) collective-permute-start(bf16[16,128,128]{2,1,0:T(8,128)(2,1)} %stage.29), channel_id=1, source_target_pairs={{0,2},{2,4},{4,6},{3,1},{5,3},{7,5},{8,10},{10,12},{12,14},{11,9},... | collective-permute-start | bytes 1572872 | tf_op jit(solution)/shard_map/ppermute | solution.py:485
  30.8 5.2 %collective-permute-start.10 = (bf16[16,128,128]{2,1,0:T(8,128)(2,1)}, bf16[16,128,128]{2,1,0:T(8,128)(2,1)}, u32[]{:S(2)}, u32[]{:S(2)}) collective-permute-start(bf16[16,128,128]{2,1,0:T(8,128)(2,1)} %stage.25), channel_id=1, source_target_pairs={{0,2},{2,4},{4,6},{3,1},{5,3},{7,5},{8,10},{10,12},{12,14},{11,9},... | collective-permute-start | bytes 1572872 | tf_op jit(solution)/shard_map/ppermute | solution.py:485
  36.0 1.5 stage.30
  37.5 4.2 %collective-permute-start.18 = (bf16[16,128,128]{2,1,0:T(8,128)(2,1)}, bf16[16,128,128]{2,1,0:T(8,128)(2,1)}, u32[]{:S(2)}, u32[]{:S(2)}) collective-permute-start(bf16[16,128,128]{2,1,0:T(8,128)(2,1)} %stage.30), channel_id=1, source_target_pairs={{0,2},{2,4},{4,6},{3,1},{5,3},{7,5},{8,10},{10,12},{12,14},{11,9},... | collective-permute-start | bytes 1572872 | tf_op jit(solution)/shard_map/ppermute | solution.py:485
  41.7 1.6 fusion
  47.8 4.0 %collective-permute-start.14 = (bf16[16,128,128]{2,1,0:T(8,128)(2,1)}, bf16[16,128,128]{2,1,0:T(8,128)(2,1)}, u32[]{:S(2)}, u32[]{:S(2)}) collective-permute-start(bf16[16,128,128]{2,1,0:T(8,128)(2,1)} %stage.26), channel_id=1, source_target_pairs={{0,2},{2,4},{4,6},{3,1},{5,3},{7,5},{8,10},{10,12},{12,14},{11,9},... | collective-permute-start | bytes 1572872 | tf_op jit(solution)/shard_map/ppermute | solution.py:485
  53.2 3.3 %collective-permute-start.19 = (bf16[16,128,128]{2,1,0:T(8,128)(2,1)}, bf16[16,128,128]{2,1,0:T(8,128)(2,1)}, u32[]{:S(2)}, u32[]{:S(2)}) collective-permute-start(bf16[16,128,128]{2,1,0:T(8,128)(2,1)} %stage.31), channel_id=1, source_target_pairs={{0,2},{2,4},{4,6},{3,1},{5,3},{7,5},{8,10},{10,12},{12,14},{11,9},... | collective-permute-start | bytes 1572872 | tf_op jit(solution)/shard_map/ppermute | solution.py:485
  56.5 1.5 collective-permute-done.14.refs_9_.refs_6_
  59.4 5.2 %collective-permute-start.15 = (bf16[16,128,128]{2,1,0:T(8,128)(2,1)}, bf16[16,128,128]{2,1,0:T(8,128)(2,1)}, u32[]{:S(2)}, u32[]{:S(2)}) collective-permute-start(bf16[16,128,128]{2,1,0:T(8,128)(2,1)} %stage.27), channel_id=1, source_target_pairs={{0,2},{2,4},{4,6},{3,1},{5,3},{7,5},{8,10},{10,12},{12,14},{11,9},... | collective-permute-start | bytes 1572872 | tf_op jit(solution)/shard_map/ppermute | solution.py:485
  66.0 4.2 %collective-permute-start.20 = (bf16[16,128,128]{2,1,0:T(8,128)(2,1)}, bf16[16,128,128]{2,1,0:T(8,128)(2,1)}, u32[]{:S(2)}, u32[]{:S(2)}) collective-permute-start(bf16[16,128,128]{2,1,0:T(8,128)(2,1)} %stage.32), channel_id=1, source_target_pairs={{0,2},{2,4},{4,6},{3,1},{5,3},{7,5},{8,10},{10,12},{12,14},{11,9},... | collective-permute-start | bytes 1572872 | tf_op jit(solution)/shard_map/ppermute | solution.py:485
  70.8 1.5 stage.28
  72.3 5.2 %collective-permute-start.16 = (bf16[16,128,128]{2,1,0:T(8,128)(2,1)}, bf16[16,128,128]{2,1,0:T(8,128)(2,1)}, u32[]{:S(2)}, u32[]{:S(2)}) collective-permute-start(bf16[16,128,128]{2,1,0:T(8,128)(2,1)} %stage.28), channel_id=1, source_target_pairs={{0,2},{2,4},{4,6},{3,1},{5,3},{7,5},{8,10},{10,12},{12,14},{11,9},... | collective-permute-start | bytes 1572872 | tf_op jit(solution)/shard_map/ppermute | solution.py:485
  77.4 1.5 stage.33
  78.9 4.2 %collective-permute-start.21 = (bf16[16,128,128]{2,1,0:T(8,128)(2,1)}, bf16[16,128,128]{2,1,0:T(8,128)(2,1)}, u32[]{:S(2)}, u32[]{:S(2)}) collective-permute-start(bf16[16,128,128]{2,1,0:T(8,128)(2,1)} %stage.33), channel_id=1, source_target_pairs={{0,2},{2,4},{4,6},{3,1},{5,3},{7,5},{8,10},{10,12},{12,14},{11,9},... | collective-permute-start | bytes 1572872 | tf_op jit(solution)/shard_map/ppermute | solution.py:485
  83.7 5.6 %collective-permute-done.21.refs_13_ = bf16[16,128,128]{2,1,0:T(8,128)(2,1)} collective-permute-done((bf16[16,128,128]{2,1,0:T(8,128)(2,1)}, bf16[16,128,128]{2,1,0:T(8,128)(2,1)}, u32[]{:S(2)}, u32[]{:S(2)}) %collective-permute-start.21) | collective-permute-done | bytes 524320 | tf_op jit(solution)/shard_map/ppermute | solution.py:485
  89.3 2.1 %last.8 = bf16[2,32,128,128]{3,2,1,0:T(8,128)(2,1)} custom-call(s32[1]{0:T(128)} %bitcast.4.refs_0_.refs_1_.where_ref, s32[8,128]{1,0:T(8,128)S(1)} %get-tuple-element.586.refs_2_.table_ref, bf16[32,128,128]{2,1,0:T(8,128)(2,1)S(1)} %bitcast.47, bf16[32,128,128]{2,1,0:T(8,128)(2,1)S(1)} %bitcast.60, ...), custom_call_target="tpu_custom_call" | custom-call | tf_op jit(solution)/shard_map/last/pallas_call | solution.py:489
  91.5 1.7 %collective-permute-start.25 = (s32[8,128]{1,0:T(8,128)S(1)}, s32[8,128]{1,0:T(8,128)S(1)}, u32[]{:S(2)}, u32[]{:S(2)}) collective-permute-start(s32[8,128]{1,0:T(8,128)S(1)} %copy-done.3), channel_id=1, source_target_pairs={{0,24},{8,16},{16,8},{24,0},{1,25},{9,17},{17,9},{25,1},{2,26},{10... | collective-permute-start | bytes 12296 | tf_op jit(solution)/shard_map/ppermute | solution.py:31
  93.2 1.6 %collective-permute-start.24 = (s32[8,128]{1,0:T(8,128)S(1)}, s32[8,128]{1,0:T(8,128)S(1)}, u32[]{:S(2)}, u32[]{:S(2)}) collective-permute-start(s32[8,128]{1,0:T(8,128)S(1)} %copy-done.3), channel_id=1, source_target_pairs={{0,16},{8,24},{16,0},{24,8},{1,17},{9,25},{17,1},{25,9},{2,18},{10... | collective-permute-start | bytes 12296 | tf_op jit(solution)/shard_map/ppermute | solution.py:31
  96.8 1.6 %collective-permute-done.23 = s32[8,128]{1,0:T(8,128)S(1)} collective-permute-done((s32[8,128]{1,0:T(8,128)S(1)}, s32[8,128]{1,0:T(8,128)S(1)}, u32[]{:S(2)}, u32[]{:S(2)}) %collective-permute-start.23) | collective-permute-done | bytes 4128 | tf_op jit(solution)/shard_map/ppermute | solution.py:31
  99.9 38.4 %krylov.1 = (f32[8,512,128]{2,1,0:T(8,128)S(1)}, f32[32,128]{1,0:T(8,128)S(1)}) custom-call(s32[8,128]{1,0:T(8,128)S(1)} %get-tuple-element.673, s32[1]{0:T(128)} %bitcast.3.me_ref.refs_0_, f32[512,128]{1,0:T(8,128)S(1)} %bitcast.35, bf16[256,256]{1,0:T(8,128)(2,1)S(1)} %mul.42.mix_ref, bf16[2,32,128,128]{3,2,1,0:T(8,128)(2,1)} %get-tuple-element.405.theirs_ref, ...), custom_call_target="tpu_custom_call" | custom-call | tf_op jit(solution)/shard_map/krylov/pallas_call | solution.py:569
  138.3 3.5 %collective-permute-start.28 = (f32[32,128]{1,0:T(8,128)S(1)}, f32[32,128]{1,0:T(8,128)S(1)}, u32[]{:S(2)}, u32[]{:S(2)}) collective-permute-start(f32[32,128]{1,0:T(8,128)S(1)} %get-tuple-element.408), channel_id=1, source_target_pairs={{0,6},{1,7},{2,4},{3,5},{4,2},{5,3},{6,0},{7,1},{8,14},{9,15},{10,... | collective-permute-start | bytes 49160 | tf_op jit(solution)/shard_map/ppermute | solution.py:31
  143.9 2.6 %collective-permute-done.27 = f32[32,128]{1,0:T(8,128)S(1)} collective-permute-done((f32[32,128]{1,0:T(8,128)S(1)}, f32[32,128]{1,0:T(8,128)S(1)}, u32[]{:S(2)}, u32[]{:S(2)}) %collective-permute-start.27) | collective-permute-done | bytes 16416 | tf_op jit(solution)/shard_map/ppermute | solution.py:31
  149.2 2.0 %collective-permute-start.31 = (f32[32,128]{1,0:T(8,128)S(1)}, f32[32,128]{1,0:T(8,128)S(1)}, u32[]{:S(2)}, u32[]{:S(2)}) collective-permute-start(f32[32,128]{1,0:T(8,128)S(1)} %add.82.refs_1_), channel_id=1, source_target_pairs={{16,0},{24,8},{0,16},{8,24},{17,1},{25,9},{1,17},{9,25},{18,2},{26... | collective-permute-start | bytes 49160 | tf_op jit(solution)/shard_map/ppermute | solution.py:438
  152.9 2.0 %collective-permute-done.30.refs_2_ = f32[32,128]{1,0:T(8,128)S(1)} collective-permute-done((f32[32,128]{1,0:T(8,128)S(1)}, f32[32,128]{1,0:T(8,128)S(1)}, u32[]{:S(2)}, u32[]{:S(2)}) %collective-permute-start.30) | collective-permute-done | bytes 16416 | tf_op jit(solution)/shard_map/ppermute | solution.py:438
  154.9 4.0 %finish.1 = (f32[512,128]{1,0:T(8,128)}, f32[8,8]{1,0:T(8,128)}) custom-call(s32[1]{0:T(128)} %bitcast.3.me_ref.refs_0_, f32[32,128]{1,0:T(8,128)S(1)} %add.82.refs_1_, f32[32,128]{1,0:T(8,128)S(1)} %collective-permute-done.30.refs_2_, f32[32,128]{1,0:T(8,128)S(1)} %collective-permute-done.31.refs_3_, f32[32,128]{1,0:T(8,128)S(1)} %collective-permute-done.32.refs_4_, ...), custom_call_target="tpu_custom_call" | custom-call | tf_op jit(solution)/shard_map/finish/pallas_call | solution.py:596
  (73 shorter events, 26.5 us)
Async XLA Ops:
  0.6 22.5 %copy-start.1 = (bf16[1,32,128,128]{3,2,1,0:T(8,128)(2,1)S(1)}, bf16[1,32,128,128]{3,2,1,0:T(8,128)(2,1)}, u32[]{:S(2)}) copy-start(bf16[1,32,128,128]{3,2,1,0:T(8,128)(2,1)} %param.11) | copy-start | bytes 3145732
  0.6 22.5 %copy-start.2 = (bf16[1,32,128,128]{3,2,1,0:T(8,128)(2,1)S(1)}, bf16[1,32,128,128]{3,2,1,0:T(8,128)(2,1)}, u32[]{:S(2)}) copy-start(bf16[1,32,128,128]{3,2,1,0:T(8,128)(2,1)} %param.12) | copy-start | bytes 3145732
  0.7 17.5 %collective-permute-start.7 = (bf16[32,128,128]{2,1,0:T(8,128)(2,1)}, bf16[32,128,128]{2,1,0:T(8,128)(2,1)S(1)}, u32[]{:S(2)}, u32[]{:S(2)}) collective-permute-start(bf16[32,128,128]{2,1,0:T(8,128)(2,1)} %bitcast.36), channel_id=1, source_target_pairs={{0,1},{1,0},{2,3},{3,2},{4,5},{5,4},{6,7},{7,6},{8,9},{9,8},{10,11... | collective-permute-start | bytes 3145736 | tf_op jit(solution)/shard_map/ppermute | solution.py:457
  1.2 17.0 %collective-permute-start.8 = (bf16[32,128,128]{2,1,0:T(8,128)(2,1)}, bf16[32,128,128]{2,1,0:T(8,128)(2,1)}, u32[]{:S(2)}, u32[]{:S(2)}) collective-permute-start(bf16[32,128,128]{2,1,0:T(8,128)(2,1)} %bitcast.49), channel_id=1, source_target_pairs={{0,1},{1,0},{2,3},{3,2},{4,5},{5,4},{6,7},{7,6},{8,9},{9,8},{10,11... | collective-permute-start | bytes 3145736 | tf_op jit(solution)/shard_map/ppermute | solution.py:457
  2.6 5.7 %collective-permute-start.4 = (s32[8,128]{1,0:T(8,128)S(1)}, s32[8,128]{1,0:T(8,128)S(1)}, u32[]{:S(2)}, u32[]{:S(2)}) collective-permute-start(s32[8,128]{1,0:T(8,128)S(1)} %broadcast_select_fusion), channel_id=1, source_target_pairs={{0,4},{1,5},{2,6},{3,7},{4,0},{5,1},{6,2},{7,3},{8,12},{9,13},{10,... | collective-permute-start | bytes 12296 | tf_op jit(solution)/shard_map/ppermute | solution.py:31
  6.7 5.4 %collective-permute-start.5 = (s32[8,128]{1,0:T(8,128)S(1)}, s32[8,128]{1,0:T(8,128)S(1)}, u32[]{:S(2)}, u32[]{:S(2)}) collective-permute-start(s32[8,128]{1,0:T(8,128)S(1)} %broadcast_select_fusion), channel_id=1, source_target_pairs={{0,6},{1,7},{2,4},{3,5},{4,2},{5,3},{6,0},{7,1},{8,14},{9,15},{10,... | collective-permute-start | bytes 12296 | tf_op jit(solution)/shard_map/ppermute | solution.py:31
  8.1 4.1 %collective-permute-start.3 = (s32[8,128]{1,0:T(8,128)S(1)}, s32[8,128]{1,0:T(8,128)S(1)}, u32[]{:S(2)}, u32[]{:S(2)}) collective-permute-start(s32[8,128]{1,0:T(8,128)S(1)} %broadcast_select_fusion), channel_id=1, source_target_pairs={{0,2},{1,3},{2,0},{3,1},{4,6},{5,7},{6,4},{7,5},{8,10},{9,11},{10,... | collective-permute-start | bytes 12296 | tf_op jit(solution)/shard_map/ppermute | solution.py:31
  12.1 3.1 %collective-permute-start.6 = (s32[8,128]{1,0:T(8,128)S(1)}, s32[8,128]{1,0:T(8,128)S(1)}, u32[]{:S(2)}, u32[]{:S(2)}) collective-permute-start(s32[8,128]{1,0:T(8,128)S(1)} %maximum_maximum_fusion.1), channel_id=1, source_target_pairs={{0,1},{1,0},{2,3},{3,2},{4,5},{5,4},{6,7},{7,6},{8,9},{9,8},{10,11... | collective-permute-start | bytes 12296 | tf_op jit(solution)/shard_map/ppermute | solution.py:31
  12.2 29.4 %collective-permute-start.12 = (bf16[8,32,256]{2,1,0:T(8,128)(2,1)}, bf16[8,32,256]{2,1,0:T(8,128)(2,1)}, u32[]{:S(2)}, u32[]{:S(2)}) collective-permute-start(bf16[8,32,256]{2,1,0:T(8,128)(2,1)} %param.10), channel_id=1, source_target_pairs={{16,0},{24,8},{0,16},{8,24},{17,1},{25,9},{1,17},{9,25},{18,2},{26... | collective-permute-start | bytes 393224 | tf_op jit(solution)/shard_map/ppermute | solution.py:438
  13.8 27.9 %collective-permute-start.11 = (bf16[8,32,256]{2,1,0:T(8,128)(2,1)}, bf16[8,32,256]{2,1,0:T(8,128)(2,1)}, u32[]{:S(2)}, u32[]{:S(2)}) collective-permute-start(bf16[8,32,256]{2,1,0:T(8,128)(2,1)} %param.10), channel_id=1, source_target_pairs={{8,0},{16,8},{24,16},{0,24},{9,1},{17,9},{25,17},{1,25},{10,2},{18... | collective-permute-start | bytes 393224 | tf_op jit(solution)/shard_map/ppermute | solution.py:438
  20.6 8.7 %collective-permute-start.9 = (bf16[16,128,128]{2,1,0:T(8,128)(2,1)}, bf16[16,128,128]{2,1,0:T(8,128)(2,1)}, u32[]{:S(2)}, u32[]{:S(2)}) collective-permute-start(bf16[16,128,128]{2,1,0:T(8,128)(2,1)} %stage.24), channel_id=1, source_target_pairs={{0,2},{2,4},{4,6},{3,1},{5,3},{7,5},{8,10},{10,12},{12,14},{11,9},... | collective-permute-start | bytes 1572872 | tf_op jit(solution)/shard_map/ppermute | solution.py:485
  24.7 11.3 %collective-permute-start.17 = (bf16[16,128,128]{2,1,0:T(8,128)(2,1)}, bf16[16,128,128]{2,1,0:T(8,128)(2,1)}, u32[]{:S(2)}, u32[]{:S(2)}) collective-permute-start(bf16[16,128,128]{2,1,0:T(8,128)(2,1)} %stage.29), channel_id=1, source_target_pairs={{0,2},{2,4},{4,6},{3,1},{5,3},{7,5},{8,10},{10,12},{12,14},{11,9},... | collective-permute-start | bytes 1572872 | tf_op jit(solution)/shard_map/ppermute | solution.py:485
  28.6 13.0 %collective-permute-start.13 = (bf16[8,32,256]{2,1,0:T(8,128)(2,1)S(1)}, bf16[8,32,256]{2,1,0:T(8,128)(2,1)}, u32[]{:S(2)}, u32[]{:S(2)}) collective-permute-start(bf16[8,32,256]{2,1,0:T(8,128)(2,1)S(1)} %copy-done.5), channel_id=1, source_target_pairs={{24,0},{0,8},{8,16},{16,24},{25,1},{1,9},{9,17},{17,25},{26,2},{2,... | collective-permute-start | bytes 393224 | tf_op jit(solution)/shard_map/ppermute | solution.py:438
  30.8 15.6 %collective-permute-start.10 = (bf16[16,128,128]{2,1,0:T(8,128)(2,1)}, bf16[16,128,128]{2,1,0:T(8,128)(2,1)}, u32[]{:S(2)}, u32[]{:S(2)}) collective-permute-start(bf16[16,128,128]{2,1,0:T(8,128)(2,1)} %stage.25), channel_id=1, source_target_pairs={{0,2},{2,4},{4,6},{3,1},{5,3},{7,5},{8,10},{10,12},{12,14},{11,9},... | collective-permute-start | bytes 1572872 | tf_op jit(solution)/shard_map/ppermute | solution.py:485
  37.5 14.3 %collective-permute-start.18 = (bf16[16,128,128]{2,1,0:T(8,128)(2,1)}, bf16[16,128,128]{2,1,0:T(8,128)(2,1)}, u32[]{:S(2)}, u32[]{:S(2)}) collective-permute-start(bf16[16,128,128]{2,1,0:T(8,128)(2,1)} %stage.30), channel_id=1, source_target_pairs={{0,2},{2,4},{4,6},{3,1},{5,3},{7,5},{8,10},{10,12},{12,14},{11,9},... | collective-permute-start | bytes 1572872 | tf_op jit(solution)/shard_map/ppermute | solution.py:485
  47.8 10.2 %collective-permute-start.14 = (bf16[16,128,128]{2,1,0:T(8,128)(2,1)}, bf16[16,128,128]{2,1,0:T(8,128)(2,1)}, u32[]{:S(2)}, u32[]{:S(2)}) collective-permute-start(bf16[16,128,128]{2,1,0:T(8,128)(2,1)} %stage.26), channel_id=1, source_target_pairs={{0,2},{2,4},{4,6},{3,1},{5,3},{7,5},{8,10},{10,12},{12,14},{11,9},... | collective-permute-start | bytes 1572872 | tf_op jit(solution)/shard_map/ppermute | solution.py:485
  53.2 11.4 %collective-permute-start.19 = (bf16[16,128,128]{2,1,0:T(8,128)(2,1)}, bf16[16,128,128]{2,1,0:T(8,128)(2,1)}, u32[]{:S(2)}, u32[]{:S(2)}) collective-permute-start(bf16[16,128,128]{2,1,0:T(8,128)(2,1)} %stage.31), channel_id=1, source_target_pairs={{0,2},{2,4},{4,6},{3,1},{5,3},{7,5},{8,10},{10,12},{12,14},{11,9},... | collective-permute-start | bytes 1572872 | tf_op jit(solution)/shard_map/ppermute | solution.py:485
  59.4 11.4 %collective-permute-start.15 = (bf16[16,128,128]{2,1,0:T(8,128)(2,1)}, bf16[16,128,128]{2,1,0:T(8,128)(2,1)}, u32[]{:S(2)}, u32[]{:S(2)}) collective-permute-start(bf16[16,128,128]{2,1,0:T(8,128)(2,1)} %stage.27), channel_id=1, source_target_pairs={{0,2},{2,4},{4,6},{3,1},{5,3},{7,5},{8,10},{10,12},{12,14},{11,9},... | collective-permute-start | bytes 1572872 | tf_op jit(solution)/shard_map/ppermute | solution.py:485
  66.0 11.4 %collective-permute-start.20 = (bf16[16,128,128]{2,1,0:T(8,128)(2,1)}, bf16[16,128,128]{2,1,0:T(8,128)(2,1)}, u32[]{:S(2)}, u32[]{:S(2)}) collective-permute-start(bf16[16,128,128]{2,1,0:T(8,128)(2,1)} %stage.32), channel_id=1, source_target_pairs={{0,2},{2,4},{4,6},{3,1},{5,3},{7,5},{8,10},{10,12},{12,14},{11,9},... | collective-permute-start | bytes 1572872 | tf_op jit(solution)/shard_map/ppermute | solution.py:485
  72.3 11.4 %collective-permute-start.16 = (bf16[16,128,128]{2,1,0:T(8,128)(2,1)}, bf16[16,128,128]{2,1,0:T(8,128)(2,1)}, u32[]{:S(2)}, u32[]{:S(2)}) collective-permute-start(bf16[16,128,128]{2,1,0:T(8,128)(2,1)} %stage.28), channel_id=1, source_target_pairs={{0,2},{2,4},{4,6},{3,1},{5,3},{7,5},{8,10},{10,12},{12,14},{11,9},... | collective-permute-start | bytes 1572872 | tf_op jit(solution)/shard_map/ppermute | solution.py:485
  78.9 10.4 %collective-permute-start.21 = (bf16[16,128,128]{2,1,0:T(8,128)(2,1)}, bf16[16,128,128]{2,1,0:T(8,128)(2,1)}, u32[]{:S(2)}, u32[]{:S(2)}) collective-permute-start(bf16[16,128,128]{2,1,0:T(8,128)(2,1)} %stage.33), channel_id=1, source_target_pairs={{0,2},{2,4},{4,6},{3,1},{5,3},{7,5},{8,10},{10,12},{12,14},{11,9},... | collective-permute-start | bytes 1572872 | tf_op jit(solution)/shard_map/ppermute | solution.py:485
  91.4 7.5 %collective-permute-start.22 = (bf16[2,32,128,128]{3,2,1,0:T(8,128)(2,1)}, bf16[2,32,128,128]{3,2,1,0:T(8,128)(2,1)}, u32[]{:S(2)}, u32[]{:S(2)}) collective-permute-start(bf16[2,32,128,128]{3,2,1,0:T(8,128)(2,1)} %last.8), channel_id=1, source_target_pairs={{0,1},{1,0},{2,3},{3,2},{4,5},{5,4},{6,7},{7,6},{8,9},{9,8},{10,11... | collective-permute-start | bytes 6291464 | tf_op jit(solution)/shard_map/ppermute | solution.py:497
  91.5 4.6 %collective-permute-start.25 = (s32[8,128]{1,0:T(8,128)S(1)}, s32[8,128]{1,0:T(8,128)S(1)}, u32[]{:S(2)}, u32[]{:S(2)}) collective-permute-start(s32[8,128]{1,0:T(8,128)S(1)} %copy-done.3), channel_id=1, source_target_pairs={{0,24},{8,16},{16,8},{24,0},{1,25},{9,17},{17,9},{25,1},{2,26},{10... | collective-permute-start | bytes 12296 | tf_op jit(solution)/shard_map/ppermute | solution.py:31
  93.2 3.6 %collective-permute-start.24 = (s32[8,128]{1,0:T(8,128)S(1)}, s32[8,128]{1,0:T(8,128)S(1)}, u32[]{:S(2)}, u32[]{:S(2)}) collective-permute-start(s32[8,128]{1,0:T(8,128)S(1)} %copy-done.3), channel_id=1, source_target_pairs={{0,16},{8,24},{16,0},{24,8},{1,17},{9,25},{17,1},{25,9},{2,18},{10... | collective-permute-start | bytes 12296 | tf_op jit(solution)/shard_map/ppermute | solution.py:31
  94.8 3.6 %collective-permute-start.23 = (s32[8,128]{1,0:T(8,128)S(1)}, s32[8,128]{1,0:T(8,128)S(1)}, u32[]{:S(2)}, u32[]{:S(2)}) collective-permute-start(s32[8,128]{1,0:T(8,128)S(1)} %copy-done.3), channel_id=1, source_target_pairs={{0,8},{8,0},{16,24},{24,16},{1,9},{9,1},{17,25},{25,17},{2,10},{10... | collective-permute-start | bytes 12296 | tf_op jit(solution)/shard_map/ppermute | solution.py:31
  138.3 5.6 %collective-permute-start.28 = (f32[32,128]{1,0:T(8,128)S(1)}, f32[32,128]{1,0:T(8,128)S(1)}, u32[]{:S(2)}, u32[]{:S(2)}) collective-permute-start(f32[32,128]{1,0:T(8,128)S(1)} %get-tuple-element.408), channel_id=1, source_target_pairs={{0,6},{1,7},{2,4},{3,5},{4,2},{5,3},{6,0},{7,1},{8,14},{9,15},{10,... | collective-permute-start | bytes 49160 | tf_op jit(solution)/shard_map/ppermute | solution.py:31
  141.9 4.6 %collective-permute-start.27 = (f32[32,128]{1,0:T(8,128)S(1)}, f32[32,128]{1,0:T(8,128)S(1)}, u32[]{:S(2)}, u32[]{:S(2)}) collective-permute-start(f32[32,128]{1,0:T(8,128)S(1)} %get-tuple-element.408), channel_id=1, source_target_pairs={{0,4},{1,5},{2,6},{3,7},{4,0},{5,1},{6,2},{7,3},{8,12},{9,13},{10,... | collective-permute-start | bytes 49160 | tf_op jit(solution)/shard_map/ppermute | solution.py:31
  141.9 4.6 %collective-permute-start.26 = (f32[32,128]{1,0:T(8,128)S(1)}, f32[32,128]{1,0:T(8,128)S(1)}, u32[]{:S(2)}, u32[]{:S(2)}) collective-permute-start(f32[32,128]{1,0:T(8,128)S(1)} %get-tuple-element.408), channel_id=1, source_target_pairs={{0,2},{1,3},{2,0},{3,1},{4,6},{5,7},{6,4},{7,5},{8,10},{9,11},{10,... | collective-permute-start | bytes 49160 | tf_op jit(solution)/shard_map/ppermute | solution.py:31
  146.5 1.2 collective-permute-start.29
  147.8 4.6 %collective-permute-start.32 = (f32[32,128]{1,0:T(8,128)S(1)}, f32[32,128]{1,0:T(8,128)S(1)}, u32[]{:S(2)}, u32[]{:S(2)}) collective-permute-start(f32[32,128]{1,0:T(8,128)S(1)} %add.82.refs_1_), channel_id=1, source_target_pairs={{24,0},{0,8},{8,16},{16,24},{25,1},{1,9},{9,17},{17,25},{26,2},{2,... | collective-permute-start | bytes 49160 | tf_op jit(solution)/shard_map/ppermute | solution.py:438
  149.2 3.7 %collective-permute-start.31 = (f32[32,128]{1,0:T(8,128)S(1)}, f32[32,128]{1,0:T(8,128)S(1)}, u32[]{:S(2)}, u32[]{:S(2)}) collective-permute-start(f32[32,128]{1,0:T(8,128)S(1)} %add.82.refs_1_), channel_id=1, source_target_pairs={{16,0},{24,8},{0,16},{8,24},{17,1},{25,9},{1,17},{9,25},{18,2},{26... | collective-permute-start | bytes 49160 | tf_op jit(solution)/shard_map/ppermute | solution.py:438
  151.2 3.7 %collective-permute-start.30 = (f32[32,128]{1,0:T(8,128)S(1)}, f32[32,128]{1,0:T(8,128)S(1)}, u32[]{:S(2)}, u32[]{:S(2)}) collective-permute-start(f32[32,128]{1,0:T(8,128)S(1)} %add.82.refs_1_), channel_id=1, source_target_pairs={{8,0},{16,8},{24,16},{0,24},{9,1},{17,9},{25,17},{1,25},{10,2},{18... | collective-permute-start | bytes 49160 | tf_op jit(solution)/shard_map/ppermute | solution.py:438
  (4 other events, 24.0 us)

commit v3 on v1

--- a/solution.py
+++ b/solution.py
@@ -43,24 +43,33 @@
     ).astype(jnp.bfloat16)
     panel = jnp.concatenate(slices, axis=0)
     mixed = jnp.einsum("acz,qpz->cpqa", panel, choose, preferred_element_type=jnp.float32)
-    return mixed.astype(jnp.bfloat16)
-
-
-def arrange_mix(mixed, share):
-    group = lax.axis_size("group")
-    turned = (group - lax.axis_index("group")) % group * share
-    mixed = lax.dynamic_slice_in_dim(
-        jnp.concatenate([mixed, mixed], axis=3), turned, mixed.shape[3], axis=3
-    )
-    channels, phys = mixed.shape[0], mixed.shape[1]
-    same = jnp.eye(2, dtype=jnp.bfloat16)
-    both = mixed[:, None, :, None] * same[None, :, None, :, None, None]
-    return both.reshape(channels * 2 * phys, 2 * phys * channels)
+    count = mixed.shape[0] * mixed.shape[1]
+    return mixed.astype(jnp.bfloat16).reshape(count, count)
+
+
+def two_row_mix(mixed, turned, channels, phys):
+    f32, bf16 = jnp.float32, jnp.bfloat16
+    count = mixed.shape[0]
+    row = lax.broadcasted_iota(jnp.int32, (count, count), 0)
+    col = lax.broadcasted_iota(jnp.int32, (count, count), 1)
+    same = (row & -channels) == (col & -channels)
+    moved = ((row + turned) & (channels - 1)) == (col & (channels - 1))
+    order = jnp.where(same & moved, 1.0, 0.0).astype(bf16)
+    mixed = jnp.dot(mixed, order, preferred_element_type=f32).astype(bf16)
+    row = lax.broadcasted_iota(jnp.int32, (2 * count, count), 0)
+    col = lax.broadcasted_iota(jnp.int32, (2 * count, count), 1)
+    base = ((row & (-2 * phys)) >> 1) + (row & (phys - 1))
+    halves = []
+    for i2 in range(2):
+        here = (base == col) & ((row & phys) == i2 * phys)
+        widen = jnp.where(here, 1.0, 0.0).astype(bf16)
+        halves.append(jnp.dot(widen, mixed, preferred_element_type=f32).astype(bf16))
+    return halves
 
 
 def krylov_kernel(table_ref, me_ref, state_ref, mix_ref, theirs_ref, *refs):
-    pieces, refs = refs[:-10], refs[-10:]
-    basis_ref, stats_ref, mine_ref, wide_ref, rows_ref, turned_ref, x_ref, m_ref, w_ref, sems = refs
+    pieces, refs = refs[:-11], refs[-11:]
+    basis_ref, stats_ref, both_ref, mine_ref, wide_ref, rows_ref, turned_ref, x_ref, m_ref, w_ref, sems = refs
     channels, size = theirs_ref.shape[1], theirs_ref.shape[2]
     loads = []
     if pieces:
@@ -71,6 +80,8 @@
         for copies in loads:
             run_copies(copies, "start")
     phys = state_ref.shape[0] // size
+    for at, half in enumerate(two_row_mix(mix_ref[...], me_ref[1], channels, phys)):
+        both_ref[:, at * half.shape[1] : (at + 1) * half.shape[1]] = half
     count = basis_ref.shape[0]
     f32, bf16 = jnp.float32, jnp.bfloat16
 
@@ -149,7 +160,7 @@
                             )
                     halves.append(jnp.concatenate(pieces, axis=0))
                 mixed = jnp.dot(
-                    mix_ref[...], jnp.concatenate(halves, axis=1), preferred_element_type=f32
+                    both_ref[...], jnp.concatenate(halves, axis=1), preferred_element_type=f32
                 )
                 to = pl.multiple_of(n * chunk * phys, chunk * phys) + k * 4 * phys
                 for c in range(channels):
@@ -435,7 +446,7 @@
     return lax.ppermute(x, "group", [((k + step) % group, k) for k in range(group)])
 
 
-def fetch_blocks(left_env, right_env, lists, mixing, sectors, me):
+def fetch_blocks(left_env, right_env, lists, slices, sectors, me):
     channels, size = left_env.shape[0], left_env.shape[1]
     share = channels // STREAMS
     bf16 = left_env.dtype
@@ -478,7 +489,7 @@
         for stream in range(STREAMS):
             flow = stage(stream, turn, held[stream])
             if (turn, stream) == (2, 0):
-                flow, mixing = lax.optimization_barrier((flow, mixing))
+                flow, slices = lax.optimization_barrier((flow, slices))
             held[stream] = held[stream] + [lax.ppermute(flow, "sector", along)]
 
     def more(carry):
@@ -513,7 +524,8 @@
         scratch_shapes=[pltpu.SemaphoreType.DMA((2 * STREAMS,))],
         name="last",
     )(where, table, *pieces)
-    return table, mixing, lax.ppermute(theirs, "sector", swap), pieces
+    theirs, slices = lax.optimization_barrier((theirs, slices))
+    return table, slices, lax.ppermute(theirs, "sector", swap), pieces
 
 
 def spread_blocks(left_env, right_env, lists, sectors):
@@ -543,21 +555,22 @@
     lists = spread_rows(lists, "sector", jnp.maximum, lax.pmax)
 
     slices = [panel] + [shifted(panel, step) for step in range(1, lax.axis_size("group"))]
-    mixing = arrange_mix(select_mix(slices, phys_states[0]), panel.shape[0])
     if sector_count <= 2 * LINE:
-        table, mixing, theirs, pieces = fetch_blocks(
-            left_env[0], right_env[0], lists, mixing, sector_count, seat
+        table, slices, theirs, pieces = fetch_blocks(
+            left_env[0], right_env[0], lists, slices, sector_count, seat
         )
     else:
         theirs, pieces = spread_blocks(left_env[0], right_env[0], lists, sector_count), []
         table = jnp.full((8, LANES), -1, jnp.int32)
+    mixing = select_mix(slices, phys_states[0])
 
     whole = pl.BlockSpec(memory_space=pltpu.VMEM)
     rows, f32, bf16 = size * phys, jnp.float32, jnp.bfloat16
     small = pl.BlockSpec(memory_space=pltpu.SMEM)
     place = pl.BlockSpec(memory_space=pl.ANY)
     devices = lax.axis_size("group") * sector_count
-    me = (lax.axis_index("group").astype(jnp.int32) * sector_count + seat).reshape(1)
+    group = lax.axis_index("group").astype(jnp.int32)
+    me = jnp.stack([group * sector_count + seat, group * panel.shape[0]])
     basis, stats = pl.pallas_call(
         krylov_kernel,
         out_shape=(
@@ -567,6 +580,7 @@
         in_specs=[small] * 2 + [whole] * 3 + [place] * len(pieces),
         out_specs=(whole, whole),
         scratch_shapes=[
+            pltpu.VMEM((2 * phys * channels, 2 * phys * channels), bf16),
             pltpu.VMEM((2, channels, size, size), bf16),
             pltpu.VMEM((channels * size, size), f32),
             pltpu.VMEM((channels * size, size), bf16),

time: 158 us -> 159 us (level)
  waiting for transfers between devices: 20.1 us -> 24.9 us
  starting transfers between devices: 63.2 us -> 58.9 us
    ppermute x14, waiting for transfers between devices: 13.7 us -> 20.3 us  [spread_rows(): lax.ppermute(x, axis, [(k, k ^ count * turn) for k in range(size)])]
    ppermute x1, waiting for transfers between devices: 4.35 us -> 0.01 us  [fetch_blocks(): return (table, slices, lax.ppermute(theirs, 'sector', swap), pieces)]
    ppermute x10, starting transfers between devices: 40.5 us -> 36.5 us  [fetch_blocks(): held[stream] = held[stream] + [lax.ppermute(flow, 'sector', along)]]
    ppermute x10, waiting for transfers between devices: 2.08 us -> 4.58 us  [fetch_blocks(): held[stream] = held[stream] + [lax.ppermute(flow, 'sector', along)]]
    convert_element_type x0 -> x1, local copies, waits for them, and re-layouts: none -> 1.73 us  [select_mix(): return mixed.astype(jnp.bfloat16).reshape(count, count)]
  transfers between devices with their start and end apart: 30 -> 30, of which waited for: 13 -> 14; matrix products, arithmetic and copies ran while one was open for 4% -> 4% of each run, Pallas kernels for 13% -> 11%
where the time goes in v3:
time: 159 us
  Pallas kernels  64.5 us (41%)
  starting transfers between devices  58.9 us (37%)
  waiting for transfers between devices  24.9 us (16%)
  local copies, waits for them, and re-layouts  4.35 us (3%)
  between operations  2.3 us (1%)
  matrix products  2.25 us (1%)
    pallas_call x1, Pallas kernels, local(): pl.pallas_call(krylov_kernel, out_shape=(jax.ShapeDtypeStruct((KRYLOV, ro...  37.8 us
    ppermute x10, starting transfers between devices, fetch_blocks(): held[stream] = held[stream] + [lax.ppermute(flow, 'sector', along)]  36.5 us
    ppermute x14, waiting for transfers between devices, spread_rows(): lax.ppermute(x, axis, [(k, k ^ count * turn) for k in range(size)])  20.3 us
    ppermute x14, starting transfers between devices, spread_rows(): lax.ppermute(x, axis, [(k, k ^ count * turn) for k in range(size)])  17.7 us
    pallas_call x10, Pallas kernels, stage(): pl.pallas_call(lambda *refs: stage_kernel(stream, tail is not None, *refs...  17.7 us
    ppermute x10, waiting for transfers between devices, fetch_blocks(): held[stream] = held[stream] + [lax.ppermute(flow, 'sector', along)]  4.58 us
    pallas_call x1, Pallas kernels, local(): pl.pallas_call(lambda *refs: finish_kernel(entries, *refs), out_shape=(ja...  4.57 us
    ppermute x3, starting transfers between devices, shifted(): lax.ppermute(x, 'group', [((k + step) % group, k) for k in range(group)])  4.01 us
  transfers between devices with their start and end apart: 30, of which 14 were waited for; matrix products, arithmetic and copies ran while one was open for 4% of the time, Pallas kernels for 11%

profile of v3, /device:TPU:0, one launch (start us, length us, event | category | flops | bytes accessed | tf_op | source)
XLA Modules:
  0.0 158.6 jit_solution(1315457975302039738)
XLA Ops:
  2.6 3.1 %collective-permute-start.2 = (s32[8,128]{1,0:T(8,128)S(1)}, s32[8,128]{1,0:T(8,128)S(1)}, u32[]{:S(2)}, u32[]{:S(2)}) collective-permute-start(s32[8,128]{1,0:T(8,128)S(1)} %broadcast_select_fusion), channel_id=1, source_target_pairs={{0,2},{1,3},{2,0},{3,1},{4,6},{5,7},{6,4},{7,5},{8,10},{9,11},{10,... | collective-permute-start | bytes 12296 | tf_op jit(solution)/shard_map/ppermute | solution.py:31
  5.7 2.6 %collective-permute-start.3 = (s32[8,128]{1,0:T(8,128)S(1)}, s32[8,128]{1,0:T(8,128)S(1)}, u32[]{:S(2)}, u32[]{:S(2)}) collective-permute-start(s32[8,128]{1,0:T(8,128)S(1)} %broadcast_select_fusion), channel_id=1, source_target_pairs={{0,4},{1,5},{2,6},{3,7},{4,0},{5,1},{6,2},{7,3},{8,12},{9,13},{10,... | collective-permute-start | bytes 12296 | tf_op jit(solution)/shard_map/ppermute | solution.py:31
  8.3 1.9 %collective-permute-done.3 = s32[8,128]{1,0:T(8,128)S(1)} collective-permute-done((s32[8,128]{1,0:T(8,128)S(1)}, s32[8,128]{1,0:T(8,128)S(1)}, u32[]{:S(2)}, u32[]{:S(2)}) %collective-permute-start.3) | collective-permute-done | bytes 4128 | tf_op jit(solution)/shard_map/ppermute | solution.py:31
  10.2 3.5 %collective-permute-done.4 = s32[8,128]{1,0:T(8,128)S(1)} collective-permute-done((s32[8,128]{1,0:T(8,128)S(1)}, s32[8,128]{1,0:T(8,128)S(1)}, u32[]{:S(2)}, u32[]{:S(2)}) %collective-permute-start.4) | collective-permute-done | bytes 4128 | tf_op jit(solution)/shard_map/ppermute | solution.py:31
  15.5 2.3 %route.1 = (s32[8,128]{1,0:T(8,128)S(1)}, s32[8,128]{1,0:T(8,128)}) custom-call(s32[1]{0:T(128)} %bitcast.5.refs_0_.refs_1_.where_ref, s32[8,128]{1,0:T(8,128)} %max.24.refs_1_), custom_call_target="tpu_custom_call" | custom-call | tf_op jit(solution)/shard_map/route/pallas_call | solution.py:467
  17.9 2.5 %stage.29 = bf16[16,128,128]{2,1,0:T(8,128)(2,1)} custom-call(s32[1]{0:T(128)} %constant.55.clone.1.refs_0_, s32[1]{0:T(128)} %bitcast.5.refs_0_.refs_1_.where_ref, s32[8,128]{1,0:T(8,128)S(1)} %get-tuple-element.581.refs_2_.table_ref, bf16[32,128,128]{2,1,0:T(8,128)(2,1)} %bitcast.38, bf16[32,128,128]{2,1,0:T(8,128)(2,1)} %bitcast.50, ...), custom_call_target="tpu_custom_call" | custom-call | tf_op jit(solution)/shard_map/stage/pallas_call | solution.py:478
  23.2 2.2 %collective-permute-start.8 = (bf16[16,128,128]{2,1,0:T(8,128)(2,1)}, bf16[16,128,128]{2,1,0:T(8,128)(2,1)S(1)}, u32[]{:S(2)}, u32[]{:S(2)}) collective-permute-start(bf16[16,128,128]{2,1,0:T(8,128)(2,1)} %stage.24), channel_id=1, source_target_pairs={{0,2},{2,4},{4,6},{3,1},{5,3},{7,5},{8,10},{10,12},{12,14},{11,9},... | collective-permute-start | bytes 1572872 | tf_op jit(solution)/shard_map/ppermute | solution.py:493
  25.4 3.3 %collective-permute-done.16.refs_7_.refs_9_ = bf16[16,128,128]{2,1,0:T(8,128)(2,1)S(1)} collective-permute-done((bf16[16,128,128]{2,1,0:T(8,128)(2,1)}, bf16[16,128,128]{2,1,0:T(8,128)(2,1)S(1)}, u32[]{:S(2)}, u32[]{:S(2)}) %collective-permute-start.16) | collective-permute-done | bytes 524320 | tf_op jit(solution)/shard_map/ppermute | solution.py:493
  28.7 2.5 %stage.30 = bf16[16,128,128]{2,1,0:T(8,128)(2,1)} custom-call(s32[1]{0:T(128)} %constant.56.clone.1.refs_0_, s32[1]{0:T(128)} %bitcast.5.refs_0_.refs_1_.where_ref, s32[8,128]{1,0:T(8,128)S(1)} %get-tuple-element.581.refs_2_.table_ref, bf16[32,128,128]{2,1,0:T(8,128)(2,1)S(1)} %bitcast.40, bf16[32,128,128]{2,1,0:T(8,128)(2,1)S(1)} %bitcast.52, ...), custom_call_target="tpu_custom_call" | custom-call | tf_op jit(solution)/shard_map/stage/pallas_call | solution.py:478
  31.2 4.2 %collective-permute-start.17 = (bf16[16,128,128]{2,1,0:T(8,128)(2,1)}, bf16[16,128,128]{2,1,0:T(8,128)(2,1)}, u32[]{:S(2)}, u32[]{:S(2)}) collective-permute-start(bf16[16,128,128]{2,1,0:T(8,128)(2,1)} %stage.30), channel_id=1, source_target_pairs={{0,2},{2,4},{4,6},{3,1},{5,3},{7,5},{8,10},{10,12},{12,14},{11,9},... | collective-permute-start | bytes 1572872 | tf_op jit(solution)/shard_map/ppermute | solution.py:493
  35.4 2.5 %stage.25 = bf16[16,128,128]{2,1,0:T(8,128)(2,1)} custom-call(s32[1]{0:T(128)} %constant.56.clone.1.refs_0_, s32[1]{0:T(128)} %bitcast.5.refs_0_.refs_1_.where_ref, s32[8,128]{1,0:T(8,128)S(1)} %get-tuple-element.581.refs_2_.table_ref, bf16[32,128,128]{2,1,0:T(8,128)(2,1)S(1)} %bitcast.41, bf16[32,128,128]{2,1,0:T(8,128)(2,1)S(1)} %bitcast.53, ...), custom_call_target="tpu_custom_call" | custom-call | tf_op jit(solution)/shard_map/stage/pallas_call | solution.py:478
  37.9 3.0 %collective-permute-start.9 = (bf16[16,128,128]{2,1,0:T(8,128)(2,1)}, bf16[16,128,128]{2,1,0:T(8,128)(2,1)}, u32[]{:S(2)}, u32[]{:S(2)}) collective-permute-start(bf16[16,128,128]{2,1,0:T(8,128)(2,1)} %stage.25), channel_id=1, source_target_pairs={{0,2},{2,4},{4,6},{3,1},{5,3},{7,5},{8,10},{10,12},{12,14},{11,9},... | collective-permute-start | bytes 1572872 | tf_op jit(solution)/shard_map/ppermute | solution.py:493
  40.9 3.4 %collective-permute-start.10 = (bf16[8,32,256]{2,1,0:T(8,128)(2,1)S(1)}, bf16[8,32,256]{2,1,0:T(8,128)(2,1)S(1)}, u32[]{:S(2)}, u32[]{:S(2)}) collective-permute-start(bf16[8,32,256]{2,1,0:T(8,128)(2,1)S(1)} %copy-done.7), channel_id=1, source_target_pairs={{8,0},{16,8},{24,16},{0,24},{9,1},{17,9},{25,17},{1,25},{10,2},{18... | collective-permute-start | bytes 393224 | tf_op jit(solution)/shard_map/ppermute | solution.py:446
  46.4 3.1 %collective-permute-start.18 = (bf16[16,128,128]{2,1,0:T(8,128)(2,1)}, bf16[16,128,128]{2,1,0:T(8,128)(2,1)}, u32[]{:S(2)}, u32[]{:S(2)}) collective-permute-start(bf16[16,128,128]{2,1,0:T(8,128)(2,1)} %stage.31), channel_id=1, source_target_pairs={{0,2},{2,4},{4,6},{3,1},{5,3},{7,5},{8,10},{10,12},{12,14},{11,9},... | collective-permute-start | bytes 1572872 | tf_op jit(solution)/shard_map/ppermute | solution.py:493
  50.9 4.0 %collective-permute-start.13 = (bf16[16,128,128]{2,1,0:T(8,128)(2,1)}, bf16[16,128,128]{2,1,0:T(8,128)(2,1)}, u32[]{:S(2)}, u32[]{:S(2)}) collective-permute-start(bf16[16,128,128]{2,1,0:T(8,128)(2,1)} %stage.26), channel_id=1, source_target_pairs={{0,2},{2,4},{4,6},{3,1},{5,3},{7,5},{8,10},{10,12},{12,14},{11,9},... | collective-permute-start | bytes 1572872 | tf_op jit(solution)/shard_map/ppermute | solution.py:493
  57.1 5.2 %collective-permute-start.19 = (bf16[16,128,128]{2,1,0:T(8,128)(2,1)}, bf16[16,128,128]{2,1,0:T(8,128)(2,1)}, u32[]{:S(2)}, u32[]{:S(2)}) collective-permute-start(bf16[16,128,128]{2,1,0:T(8,128)(2,1)} %stage.32), channel_id=1, source_target_pairs={{0,2},{2,4},{4,6},{3,1},{5,3},{7,5},{8,10},{10,12},{12,14},{11,9},... | collective-permute-start | bytes 1572872 | tf_op jit(solution)/shard_map/ppermute | solution.py:493
  63.8 4.1 %collective-permute-start.14 = (bf16[16,128,128]{2,1,0:T(8,128)(2,1)}, bf16[16,128,128]{2,1,0:T(8,128)(2,1)}, u32[]{:S(2)}, u32[]{:S(2)}) collective-permute-start(bf16[16,128,128]{2,1,0:T(8,128)(2,1)} %stage.27), channel_id=1, source_target_pairs={{0,2},{2,4},{4,6},{3,1},{5,3},{7,5},{8,10},{10,12},{12,14},{11,9},... | collective-permute-start | bytes 1572872 | tf_op jit(solution)/shard_map/ppermute | solution.py:493
  70.0 5.2 %collective-permute-start.20 = (bf16[16,128,128]{2,1,0:T(8,128)(2,1)}, bf16[16,128,128]{2,1,0:T(8,128)(2,1)}, u32[]{:S(2)}, u32[]{:S(2)}) collective-permute-start(bf16[16,128,128]{2,1,0:T(8,128)(2,1)} %stage.33), channel_id=1, source_target_pairs={{0,2},{2,4},{4,6},{3,1},{5,3},{7,5},{8,10},{10,12},{12,14},{11,9},... | collective-permute-start | bytes 1572872 | tf_op jit(solution)/shard_map/ppermute | solution.py:493
  76.7 4.2 %collective-permute-start.15 = (bf16[16,128,128]{2,1,0:T(8,128)(2,1)}, bf16[16,128,128]{2,1,0:T(8,128)(2,1)}, u32[]{:S(2)}, u32[]{:S(2)}) collective-permute-start(bf16[16,128,128]{2,1,0:T(8,128)(2,1)} %stage.28), channel_id=1, source_target_pairs={{0,2},{2,4},{4,6},{3,1},{5,3},{7,5},{8,10},{10,12},{12,14},{11,9},... | collective-permute-start | bytes 1572872 | tf_op jit(solution)/shard_map/ppermute | solution.py:493
  80.8 1.9 %collective-permute-start.21 = (s32[8,128]{1,0:T(8,128)S(1)}, s32[8,128]{1,0:T(8,128)S(1)}, u32[]{:S(2)}, u32[]{:S(2)}) collective-permute-start(s32[8,128]{1,0:T(8,128)S(1)} %copy-done.5), channel_id=1, source_target_pairs={{0,8},{8,0},{16,24},{24,16},{1,9},{9,1},{17,25},{25,17},{2,10},{10... | collective-permute-start | bytes 12296 | tf_op jit(solution)/shard_map/ppermute | solution.py:31
  84.4 1.9 %collective-permute-done.22 = s32[8,128]{1,0:T(8,128)S(1)} collective-permute-done((s32[8,128]{1,0:T(8,128)S(1)}, s32[8,128]{1,0:T(8,128)S(1)}, u32[]{:S(2)}, u32[]{:S(2)}) %collective-permute-start.22) | collective-permute-done | bytes 4128 | tf_op jit(solution)/shard_map/ppermute | solution.py:31
  86.4 1.8 %collective-permute-done.23 = s32[8,128]{1,0:T(8,128)S(1)} collective-permute-done((s32[8,128]{1,0:T(8,128)S(1)}, s32[8,128]{1,0:T(8,128)S(1)}, u32[]{:S(2)}, u32[]{:S(2)}) %collective-permute-start.23) | collective-permute-done | bytes 4128 | tf_op jit(solution)/shard_map/ppermute | solution.py:31
  90.5 2.1 %last.1 = bf16[2,32,128,128]{3,2,1,0:T(8,128)(2,1)} custom-call(s32[1]{0:T(128)} %bitcast.5.refs_0_.refs_1_.where_ref, s32[8,128]{1,0:T(8,128)S(1)} %get-tuple-element.663, bf16[32,128,128]{2,1,0:T(8,128)(2,1)S(1)} %get-tuple-element.653, bf16[32,128,128]{2,1,0:T(8,128)(2,1)S(1)} %get-tuple-element.655, ...), custom_call_target="tpu_custom_call" | custom-call | tf_op jit(solution)/shard_map/last/pallas_call | solution.py:519
  92.9 2.3 %fusion = bf16[32,4,4,32]{0,1,3,2:T(4,128)(2,1)} fusion(bf16[8,32,256]{2,1,0:T(8,128)(2,1)} %collective-permute-done.12, bf16[8,32,256]{2,1,0:T(8,128)(2,1)} %collective-permute-done.11, bf16[8,32,256]{2,1,0:T(8,128)(2,1)} %copy-done.8, bf16[8,32,256]{2,1,0:T(8,128)(2,1)} %param.10, s32[4,4]{1,0:T(4,128)S(1)} %broadcast_add_fusion), kind=kOutput, calls=%fused_computation.3 | convolution fusion | flops 10506240 | bytes 557120 | tf_op jit(solution)/shard_map/acz,qpz->cpqa/dot_general | solution.py:45
  95.1 1.7 %copy.9 = bf16[32,4,4,32]{3,2,1,0:T(4,128)(2,1)} copy(bf16[32,4,4,32]{0,1,3,2:T(4,128)(2,1)} %fusion) | data formatting | bytes 65536 | tf_op jit(solution)/shard_map/convert_element_type | solution.py:47
  97.9 37.8 %krylov.1 = (f32[8,512,128]{2,1,0:T(8,128)S(1)}, f32[32,128]{1,0:T(8,128)S(1)}) custom-call(s32[8,128]{1,0:T(8,128)S(1)} %get-tuple-element.663, s32[2]{0:T(128)S(1)} %pad_add_fusion.me_ref.refs_0_, f32[512,128]{1,0:T(8,128)S(1)} %bitcast.36, bf16[128,128]{1,0:T(8,128)(2,1)S(1)} %reshape.59.mix_ref, ...), custom_call_target="tpu_custom_call" | custom-call | tf_op jit(solution)/shard_map/krylov/pallas_call | solution.py:574
  135.7 2.1 %collective-permute-start.25 = (f32[32,128]{1,0:T(8,128)S(1)}, f32[32,128]{1,0:T(8,128)S(1)}, u32[]{:S(2)}, u32[]{:S(2)}) collective-permute-start(f32[32,128]{1,0:T(8,128)S(1)} %get-tuple-element.410), channel_id=1, source_target_pairs={{0,2},{1,3},{2,0},{3,1},{4,6},{5,7},{6,4},{7,5},{8,10},{9,11},{10,... | collective-permute-start | bytes 49160 | tf_op jit(solution)/shard_map/ppermute | solution.py:31
  140.2 2.2 %collective-permute-done.26 = f32[32,128]{1,0:T(8,128)S(1)} collective-permute-done((f32[32,128]{1,0:T(8,128)S(1)}, f32[32,128]{1,0:T(8,128)S(1)}, u32[]{:S(2)}, u32[]{:S(2)}) %collective-permute-start.26) | collective-permute-done | bytes 16416 | tf_op jit(solution)/shard_map/ppermute | solution.py:31
  142.5 1.8 %collective-permute-done.27 = f32[32,128]{1,0:T(8,128)S(1)} collective-permute-done((f32[32,128]{1,0:T(8,128)S(1)}, f32[32,128]{1,0:T(8,128)S(1)}, u32[]{:S(2)}, u32[]{:S(2)}) %collective-permute-start.27) | collective-permute-done | bytes 16416 | tf_op jit(solution)/shard_map/ppermute | solution.py:31
  146.5 2.9 %collective-permute-start.30 = (f32[32,128]{1,0:T(8,128)S(1)}, f32[32,128]{1,0:T(8,128)S(1)}, u32[]{:S(2)}, u32[]{:S(2)}) collective-permute-start(f32[32,128]{1,0:T(8,128)S(1)} %add.82), channel_id=1, source_target_pairs={{0,16},{8,24},{16,0},{24,8},{1,17},{9,25},{17,1},{25,9},{2,18},{10... | collective-permute-start | bytes 49160 | tf_op jit(solution)/shard_map/ppermute | solution.py:31
  151.1 2.9 %collective-permute-done.31 = f32[32,128]{1,0:T(8,128)S(1)} collective-permute-done((f32[32,128]{1,0:T(8,128)S(1)}, f32[32,128]{1,0:T(8,128)S(1)}, u32[]{:S(2)}, u32[]{:S(2)}) %collective-permute-start.31) | collective-permute-done | bytes 16416 | tf_op jit(solution)/shard_map/ppermute | solution.py:31
  154.0 4.6 %finish.1 = (f32[512,128]{1,0:T(8,128)}, f32[8,8]{1,0:T(8,128)}) custom-call(s32[2]{0:T(128)S(1)} %pad_add_fusion.me_ref.refs_0_, f32[32,128]{1,0:T(8,128)S(1)} %add_add_fusion.refs_1_, f32[8,512,128]{2,1,0:T(8,128)S(1)} %get-tuple-element.411.refs_2_), custom_call_target="tpu_custom_call" | custom-call | tf_op jit(solution)/shard_map/finish/pallas_call | solution.py:600
  (78 shorter events, 27.4 us)
Async XLA Ops:
  0.6 21.1 %copy-start.1 = (bf16[1,32,128,128]{3,2,1,0:T(8,128)(2,1)S(1)}, bf16[1,32,128,128]{3,2,1,0:T(8,128)(2,1)}, u32[]{:S(2)}) copy-start(bf16[1,32,128,128]{3,2,1,0:T(8,128)(2,1)} %param.11) | copy-start | bytes 3145732
  0.6 21.1 %copy-start.2 = (bf16[1,32,128,128]{3,2,1,0:T(8,128)(2,1)S(1)}, bf16[1,32,128,128]{3,2,1,0:T(8,128)(2,1)}, u32[]{:S(2)}) copy-start(bf16[1,32,128,128]{3,2,1,0:T(8,128)(2,1)} %param.12) | copy-start | bytes 3145732
  0.7 17.2 %collective-permute-start.6 = (bf16[32,128,128]{2,1,0:T(8,128)(2,1)}, bf16[32,128,128]{2,1,0:T(8,128)(2,1)}, u32[]{:S(2)}, u32[]{:S(2)}) collective-permute-start(bf16[32,128,128]{2,1,0:T(8,128)(2,1)} %bitcast.37), channel_id=1, source_target_pairs={{0,1},{1,0},{2,3},{3,2},{4,5},{5,4},{6,7},{7,6},{8,9},{9,8},{10,11... | collective-permute-start | bytes 3145736 | tf_op jit(solution)/shard_map/ppermute | solution.py:465
  1.2 16.7 %collective-permute-start.7 = (bf16[32,128,128]{2,1,0:T(8,128)(2,1)}, bf16[32,128,128]{2,1,0:T(8,128)(2,1)}, u32[]{:S(2)}, u32[]{:S(2)}) collective-permute-start(bf16[32,128,128]{2,1,0:T(8,128)(2,1)} %bitcast.49), channel_id=1, source_target_pairs={{0,1},{1,0},{2,3},{3,2},{4,5},{5,4},{6,7},{7,6},{8,9},{9,8},{10,11... | collective-permute-start | bytes 3145736 | tf_op jit(solution)/shard_map/ppermute | solution.py:465
  2.6 5.7 %collective-permute-start.2 = (s32[8,128]{1,0:T(8,128)S(1)}, s32[8,128]{1,0:T(8,128)S(1)}, u32[]{:S(2)}, u32[]{:S(2)}) collective-permute-start(s32[8,128]{1,0:T(8,128)S(1)} %broadcast_select_fusion), channel_id=1, source_target_pairs={{0,2},{1,3},{2,0},{3,1},{4,6},{5,7},{6,4},{7,5},{8,10},{9,11},{10,... | collective-permute-start | bytes 12296 | tf_op jit(solution)/shard_map/ppermute | solution.py:31
  5.7 4.5 %collective-permute-start.3 = (s32[8,128]{1,0:T(8,128)S(1)}, s32[8,128]{1,0:T(8,128)S(1)}, u32[]{:S(2)}, u32[]{:S(2)}) collective-permute-start(s32[8,128]{1,0:T(8,128)S(1)} %broadcast_select_fusion), channel_id=1, source_target_pairs={{0,4},{1,5},{2,6},{3,7},{4,0},{5,1},{6,2},{7,3},{8,12},{9,13},{10,... | collective-permute-start | bytes 12296 | tf_op jit(solution)/shard_map/ppermute | solution.py:31
  8.3 5.4 %collective-permute-start.4 = (s32[8,128]{1,0:T(8,128)S(1)}, s32[8,128]{1,0:T(8,128)S(1)}, u32[]{:S(2)}, u32[]{:S(2)}) collective-permute-start(s32[8,128]{1,0:T(8,128)S(1)} %broadcast_select_fusion), channel_id=1, source_target_pairs={{0,6},{1,7},{2,4},{3,5},{4,2},{5,3},{6,0},{7,1},{8,14},{9,15},{10,... | collective-permute-start | bytes 12296 | tf_op jit(solution)/shard_map/ppermute | solution.py:31
  13.7 1.2 collective-permute-start.5
  20.4 8.3 %collective-permute-start.16 = (bf16[16,128,128]{2,1,0:T(8,128)(2,1)}, bf16[16,128,128]{2,1,0:T(8,128)(2,1)S(1)}, u32[]{:S(2)}, u32[]{:S(2)}) collective-permute-start(bf16[16,128,128]{2,1,0:T(8,128)(2,1)} %stage.29), channel_id=1, source_target_pairs={{0,2},{2,4},{4,6},{3,1},{5,3},{7,5},{8,10},{10,12},{12,14},{11,9},... | collective-permute-start | bytes 1572872 | tf_op jit(solution)/shard_map/ppermute | solution.py:493
  23.2 12.2 %collective-permute-start.8 = (bf16[16,128,128]{2,1,0:T(8,128)(2,1)}, bf16[16,128,128]{2,1,0:T(8,128)(2,1)S(1)}, u32[]{:S(2)}, u32[]{:S(2)}) collective-permute-start(bf16[16,128,128]{2,1,0:T(8,128)(2,1)} %stage.24), channel_id=1, source_target_pairs={{0,2},{2,4},{4,6},{3,1},{5,3},{7,5},{8,10},{10,12},{12,14},{11,9},... | collective-permute-start | bytes 1572872 | tf_op jit(solution)/shard_map/ppermute | solution.py:493
  31.2 13.7 %collective-permute-start.17 = (bf16[16,128,128]{2,1,0:T(8,128)(2,1)}, bf16[16,128,128]{2,1,0:T(8,128)(2,1)}, u32[]{:S(2)}, u32[]{:S(2)}) collective-permute-start(bf16[16,128,128]{2,1,0:T(8,128)(2,1)} %stage.30), channel_id=1, source_target_pairs={{0,2},{2,4},{4,6},{3,1},{5,3},{7,5},{8,10},{10,12},{12,14},{11,9},... | collective-permute-start | bytes 1572872 | tf_op jit(solution)/shard_map/ppermute | solution.py:493
  37.9 11.6 %collective-permute-start.9 = (bf16[16,128,128]{2,1,0:T(8,128)(2,1)}, bf16[16,128,128]{2,1,0:T(8,128)(2,1)}, u32[]{:S(2)}, u32[]{:S(2)}) collective-permute-start(bf16[16,128,128]{2,1,0:T(8,128)(2,1)} %stage.25), channel_id=1, source_target_pairs={{0,2},{2,4},{4,6},{3,1},{5,3},{7,5},{8,10},{10,12},{12,14},{11,9},... | collective-permute-start | bytes 1572872 | tf_op jit(solution)/shard_map/ppermute | solution.py:493
  40.9 10.0 %collective-permute-start.10 = (bf16[8,32,256]{2,1,0:T(8,128)(2,1)S(1)}, bf16[8,32,256]{2,1,0:T(8,128)(2,1)S(1)}, u32[]{:S(2)}, u32[]{:S(2)}) collective-permute-start(bf16[8,32,256]{2,1,0:T(8,128)(2,1)S(1)} %copy-done.7), channel_id=1, source_target_pairs={{8,0},{16,8},{24,16},{0,24},{9,1},{17,9},{25,17},{1,25},{10,2},{18... | collective-permute-start | bytes 393224 | tf_op jit(solution)/shard_map/ppermute | solution.py:446
  44.3 6.6 %collective-permute-start.11 = (bf16[8,32,256]{2,1,0:T(8,128)(2,1)S(1)}, bf16[8,32,256]{2,1,0:T(8,128)(2,1)}, u32[]{:S(2)}, u32[]{:S(2)}) collective-permute-start(bf16[8,32,256]{2,1,0:T(8,128)(2,1)S(1)} %copy-done.7), channel_id=1, source_target_pairs={{16,0},{24,8},{0,16},{8,24},{17,1},{25,9},{1,17},{9,25},{18,2},{26... | collective-permute-start | bytes 393224 | tf_op jit(solution)/shard_map/ppermute | solution.py:446
  44.8 6.1 %collective-permute-start.12 = (bf16[8,32,256]{2,1,0:T(8,128)(2,1)S(1)}, bf16[8,32,256]{2,1,0:T(8,128)(2,1)}, u32[]{:S(2)}, u32[]{:S(2)}) collective-permute-start(bf16[8,32,256]{2,1,0:T(8,128)(2,1)S(1)} %copy-done.7), channel_id=1, source_target_pairs={{24,0},{0,8},{8,16},{16,24},{25,1},{1,9},{9,17},{17,25},{26,2},{2,... | collective-permute-start | bytes 393224 | tf_op jit(solution)/shard_map/ppermute | solution.py:446
  46.4 9.3 %collective-permute-start.18 = (bf16[16,128,128]{2,1,0:T(8,128)(2,1)}, bf16[16,128,128]{2,1,0:T(8,128)(2,1)}, u32[]{:S(2)}, u32[]{:S(2)}) collective-permute-start(bf16[16,128,128]{2,1,0:T(8,128)(2,1)} %stage.31), channel_id=1, source_target_pairs={{0,2},{2,4},{4,6},{3,1},{5,3},{7,5},{8,10},{10,12},{12,14},{11,9},... | collective-permute-start | bytes 1572872 | tf_op jit(solution)/shard_map/ppermute | solution.py:493
  50.9 11.4 %collective-permute-start.13 = (bf16[16,128,128]{2,1,0:T(8,128)(2,1)}, bf16[16,128,128]{2,1,0:T(8,128)(2,1)}, u32[]{:S(2)}, u32[]{:S(2)}) collective-permute-start(bf16[16,128,128]{2,1,0:T(8,128)(2,1)} %stage.26), channel_id=1, source_target_pairs={{0,2},{2,4},{4,6},{3,1},{5,3},{7,5},{8,10},{10,12},{12,14},{11,9},... | collective-permute-start | bytes 1572872 | tf_op jit(solution)/shard_map/ppermute | solution.py:493
  57.1 11.4 %collective-permute-start.19 = (bf16[16,128,128]{2,1,0:T(8,128)(2,1)}, bf16[16,128,128]{2,1,0:T(8,128)(2,1)}, u32[]{:S(2)}, u32[]{:S(2)}) collective-permute-start(bf16[16,128,128]{2,1,0:T(8,128)(2,1)} %stage.32), channel_id=1, source_target_pairs={{0,2},{2,4},{4,6},{3,1},{5,3},{7,5},{8,10},{10,12},{12,14},{11,9},... | collective-permute-start | bytes 1572872 | tf_op jit(solution)/shard_map/ppermute | solution.py:493
  63.8 11.4 %collective-permute-start.14 = (bf16[16,128,128]{2,1,0:T(8,128)(2,1)}, bf16[16,128,128]{2,1,0:T(8,128)(2,1)}, u32[]{:S(2)}, u32[]{:S(2)}) collective-permute-start(bf16[16,128,128]{2,1,0:T(8,128)(2,1)} %stage.27), channel_id=1, source_target_pairs={{0,2},{2,4},{4,6},{3,1},{5,3},{7,5},{8,10},{10,12},{12,14},{11,9},... | collective-permute-start | bytes 1572872 | tf_op jit(solution)/shard_map/ppermute | solution.py:493
  70.0 18.8 %collective-permute-start.20 = (bf16[16,128,128]{2,1,0:T(8,128)(2,1)}, bf16[16,128,128]{2,1,0:T(8,128)(2,1)}, u32[]{:S(2)}, u32[]{:S(2)}) collective-permute-start(bf16[16,128,128]{2,1,0:T(8,128)(2,1)} %stage.33), channel_id=1, source_target_pairs={{0,2},{2,4},{4,6},{3,1},{5,3},{7,5},{8,10},{10,12},{12,14},{11,9},... | collective-permute-start | bytes 1572872 | tf_op jit(solution)/shard_map/ppermute | solution.py:493
  76.7 12.1 %collective-permute-start.15 = (bf16[16,128,128]{2,1,0:T(8,128)(2,1)}, bf16[16,128,128]{2,1,0:T(8,128)(2,1)}, u32[]{:S(2)}, u32[]{:S(2)}) collective-permute-start(bf16[16,128,128]{2,1,0:T(8,128)(2,1)} %stage.28), channel_id=1, source_target_pairs={{0,2},{2,4},{4,6},{3,1},{5,3},{7,5},{8,10},{10,12},{12,14},{11,9},... | collective-permute-start | bytes 1572872 | tf_op jit(solution)/shard_map/ppermute | solution.py:493
  80.8 3.6 %collective-permute-start.21 = (s32[8,128]{1,0:T(8,128)S(1)}, s32[8,128]{1,0:T(8,128)S(1)}, u32[]{:S(2)}, u32[]{:S(2)}) collective-permute-start(s32[8,128]{1,0:T(8,128)S(1)} %copy-done.5), channel_id=1, source_target_pairs={{0,8},{8,0},{16,24},{24,16},{1,9},{9,1},{17,25},{25,17},{2,10},{10... | collective-permute-start | bytes 12296 | tf_op jit(solution)/shard_map/ppermute | solution.py:31
  82.8 3.6 %collective-permute-start.22 = (s32[8,128]{1,0:T(8,128)S(1)}, s32[8,128]{1,0:T(8,128)S(1)}, u32[]{:S(2)}, u32[]{:S(2)}) collective-permute-start(s32[8,128]{1,0:T(8,128)S(1)} %copy-done.5), channel_id=1, source_target_pairs={{0,16},{8,24},{16,0},{24,8},{1,17},{9,25},{17,1},{25,9},{2,18},{10... | collective-permute-start | bytes 12296 | tf_op jit(solution)/shard_map/ppermute | solution.py:31
  83.7 4.5 %collective-permute-start.23 = (s32[8,128]{1,0:T(8,128)S(1)}, s32[8,128]{1,0:T(8,128)S(1)}, u32[]{:S(2)}, u32[]{:S(2)}) collective-permute-start(s32[8,128]{1,0:T(8,128)S(1)} %copy-done.5), channel_id=1, source_target_pairs={{0,24},{8,16},{16,8},{24,0},{1,25},{9,17},{17,9},{25,1},{2,26},{10... | collective-permute-start | bytes 12296 | tf_op jit(solution)/shard_map/ppermute | solution.py:31
  92.6 5.3 %collective-permute-start.24 = (bf16[2,32,128,128]{3,2,1,0:T(8,128)(2,1)}, bf16[2,32,128,128]{3,2,1,0:T(8,128)(2,1)S(1)}, u32[]{:S(2)}, u32[]{:S(2)}) collective-permute-start(bf16[2,32,128,128]{3,2,1,0:T(8,128)(2,1)} %last.1), channel_id=1, source_target_pairs={{0,1},{1,0},{2,3},{3,2},{4,5},{5,4},{6,7},{7,6},{8,9},{9,8},{10,11... | collective-permute-start | bytes 6291464 | tf_op jit(solution)/shard_map/ppermute | solution.py:528
  135.7 4.6 %collective-permute-start.25 = (f32[32,128]{1,0:T(8,128)S(1)}, f32[32,128]{1,0:T(8,128)S(1)}, u32[]{:S(2)}, u32[]{:S(2)}) collective-permute-start(f32[32,128]{1,0:T(8,128)S(1)} %get-tuple-element.410), channel_id=1, source_target_pairs={{0,2},{1,3},{2,0},{3,1},{4,6},{5,7},{6,4},{7,5},{8,10},{9,11},{10,... | collective-permute-start | bytes 49160 | tf_op jit(solution)/shard_map/ppermute | solution.py:31
  137.8 4.7 %collective-permute-start.26 = (f32[32,128]{1,0:T(8,128)S(1)}, f32[32,128]{1,0:T(8,128)S(1)}, u32[]{:S(2)}, u32[]{:S(2)}) collective-permute-start(f32[32,128]{1,0:T(8,128)S(1)} %get-tuple-element.410), channel_id=1, source_target_pairs={{0,4},{1,5},{2,6},{3,7},{4,0},{5,1},{6,2},{7,3},{8,12},{9,13},{10,... | collective-permute-start | bytes 49160 | tf_op jit(solution)/shard_map/ppermute | solution.py:31
  138.7 5.5 %collective-permute-start.27 = (f32[32,128]{1,0:T(8,128)S(1)}, f32[32,128]{1,0:T(8,128)S(1)}, u32[]{:S(2)}, u32[]{:S(2)}) collective-permute-start(f32[32,128]{1,0:T(8,128)S(1)} %get-tuple-element.410), channel_id=1, source_target_pairs={{0,6},{1,7},{2,4},{3,5},{4,2},{5,3},{6,0},{7,1},{8,14},{9,15},{10,... | collective-permute-start | bytes 49160 | tf_op jit(solution)/shard_map/ppermute | solution.py:31
  144.3 1.2 collective-permute-start.28
  145.5 3.9 %collective-permute-start.29 = (f32[32,128]{1,0:T(8,128)S(1)}, f32[32,128]{1,0:T(8,128)S(1)}, u32[]{:S(2)}, u32[]{:S(2)}) collective-permute-start(f32[32,128]{1,0:T(8,128)S(1)} %add.82), channel_id=1, source_target_pairs={{0,8},{8,0},{16,24},{24,16},{1,9},{9,1},{17,25},{25,17},{2,10},{10... | collective-permute-start | bytes 49160 | tf_op jit(solution)/shard_map/ppermute | solution.py:31
  146.5 4.6 %collective-permute-start.30 = (f32[32,128]{1,0:T(8,128)S(1)}, f32[32,128]{1,0:T(8,128)S(1)}, u32[]{:S(2)}, u32[]{:S(2)}) collective-permute-start(f32[32,128]{1,0:T(8,128)S(1)} %add.82), channel_id=1, source_target_pairs={{0,16},{8,24},{16,0},{24,8},{1,17},{9,25},{17,1},{25,9},{2,18},{10... | collective-permute-start | bytes 49160 | tf_op jit(solution)/shard_map/ppermute | solution.py:31
  149.4 4.6 %collective-permute-start.31 = (f32[32,128]{1,0:T(8,128)S(1)}, f32[32,128]{1,0:T(8,128)S(1)}, u32[]{:S(2)}, u32[]{:S(2)}) collective-permute-start(f32[32,128]{1,0:T(8,128)S(1)} %add.82), channel_id=1, source_target_pairs={{0,24},{8,16},{16,8},{24,0},{1,25},{9,17},{17,9},{25,1},{2,26},{10... | collective-permute-start | bytes 49160 | tf_op jit(solution)/shard_map/ppermute | solution.py:31
  (7 other events, 45.0 us)

commit v4 on v1

--- a/solution.py
+++ b/solution.py
@@ -118,7 +118,7 @@
 
     group_rows = 4 * channels
     chunk = 64
-    once = 64
+    once = 32
 
     def column(j, stats):
         for q in range(phys):

time: 158 us -> 157 us (level)
  starting transfers between devices: 63.2 us -> 59.8 us
    ppermute x10, starting transfers between devices: 40.5 us -> 37.6 us  [fetch_blocks(): held[stream] = held[stream] + [lax.ppermute(flow, 'sector', along)]]
  transfers between devices with their start and end apart: 30 -> 30, of which waited for: 13 -> 13; matrix products, arithmetic and copies ran while one was open for 4% -> 4% of each run, Pallas kernels for 13% -> 14%
where the time goes in v4:
time: 157 us; the launch traced here: 156 us
  Pallas kernels  65.5 us (42%)
  starting transfers between devices  59.8 us (38%)
  waiting for transfers between devices  20.4 us (13%)
  local copies, waits for them, and re-layouts  3.13 us (2%)
  between operations  2.3 us (1%)
  other arithmetic  2.21 us (1%)
  matrix products  1.58 us (1%)
    pallas_call x1, Pallas kernels, local(): pl.pallas_call(krylov_kernel, out_shape=(jax.ShapeDtypeStruct((KRYLOV, ro...  38.3 us
    ppermute x10, starting transfers between devices, fetch_blocks(): held[stream] = held[stream] + [lax.ppermute(flow, 'sector', along)]  37.6 us
    pallas_call x10, Pallas kernels, stage(): pl.pallas_call(lambda *refs: stage_kernel(stream, tail is not None, *refs...  18.7 us
    ppermute x14, starting transfers between devices, spread_rows(): lax.ppermute(x, axis, [(k, k ^ count * turn) for k in range(size)])  17.9 us
    ppermute x14, waiting for transfers between devices, spread_rows(): lax.ppermute(x, axis, [(k, k ^ count * turn) for k in range(size)])  14 us
    ppermute x1, waiting for transfers between devices, fetch_blocks(): return (table, mixing, lax.ppermute(theirs, 'sector', swap), pieces)  4.35 us
    pallas_call x1, Pallas kernels, local(): pl.pallas_call(lambda *refs: finish_kernel(entries, *refs), out_shape=(ja...  4.03 us
    ppermute x3, starting transfers between devices, shifted(): lax.ppermute(x, 'group', [((k + step) % group, k) for k in range(group)])  3.66 us
  transfers between devices with their start and end apart: 30, of which 13 were waited for; matrix products, arithmetic and copies ran while one was open for 4% of the time, Pallas kernels for 14%

profile of v4, /device:TPU:0, one launch (start us, length us, event | category | flops | bytes accessed | tf_op | source)
XLA Modules:
  0.0 155.6 jit_solution(7938149619454152050)
XLA Ops:
  2.6 4.1 %collective-permute-start.3 = (s32[8,128]{1,0:T(8,128)S(1)}, s32[8,128]{1,0:T(8,128)S(1)}, u32[]{:S(2)}, u32[]{:S(2)}) collective-permute-start(s32[8,128]{1,0:T(8,128)S(1)} %broadcast_select_fusion), channel_id=1, source_target_pairs={{0,4},{1,5},{2,6},{3,7},{4,0},{5,1},{6,2},{7,3},{8,12},{9,13},{10,... | collective-permute-start | bytes 12296 | tf_op jit(solution)/shard_map/ppermute | solution.py:31
  8.3 3.8 %collective-permute-done.4 = s32[8,128]{1,0:T(8,128)S(1)} collective-permute-done((s32[8,128]{1,0:T(8,128)S(1)}, s32[8,128]{1,0:T(8,128)S(1)}, u32[]{:S(2)}, u32[]{:S(2)}) %collective-permute-start.4) | collective-permute-done | bytes 4128 | tf_op jit(solution)/shard_map/ppermute | solution.py:31
  12.2 1.6 %collective-permute-start.11 = (bf16[8,32,256]{2,1,0:T(8,128)(2,1)}, bf16[8,32,256]{2,1,0:T(8,128)(2,1)}, u32[]{:S(2)}, u32[]{:S(2)}) collective-permute-start(bf16[8,32,256]{2,1,0:T(8,128)(2,1)} %param.10), channel_id=1, source_target_pairs={{16,0},{24,8},{0,16},{8,24},{17,1},{25,9},{1,17},{9,25},{18,2},{26... | collective-permute-start | bytes 393224 | tf_op jit(solution)/shard_map/ppermute | solution.py:435
  15.8 2.4 %route.1 = (s32[8,128]{1,0:T(8,128)S(1)}, s32[8,128]{1,0:T(8,128)}) custom-call(s32[1]{0:T(128)} %bitcast.4.refs_0_.refs_1_.where_ref, s32[8,128]{1,0:T(8,128)} %max.24.refs_1_), custom_call_target="tpu_custom_call" | custom-call | tf_op jit(solution)/shard_map/route/pallas_call | solution.py:456
  18.2 2.5 %stage.24 = bf16[16,128,128]{2,1,0:T(8,128)(2,1)} custom-call(s32[1]{0:T(128)} %constant.67.clone.1.refs_0_, s32[1]{0:T(128)} %bitcast.4.refs_0_.refs_1_.where_ref, s32[8,128]{1,0:T(8,128)S(1)} %get-tuple-element.565.refs_2_.table_ref, bf16[32,128,128]{2,1,0:T(8,128)(2,1)} %bitcast.37, bf16[32,128,128]{2,1,0:T(8,128)(2,1)} %bitcast.49, ...), custom_call_target="tpu_custom_call" | custom-call | tf_op jit(solution)/shard_map/stage/pallas_call | solution.py:467
  20.7 1.7 %collective-permute-start.8 = (bf16[16,128,128]{2,1,0:T(8,128)(2,1)}, bf16[16,128,128]{2,1,0:T(8,128)(2,1)S(1)}, u32[]{:S(2)}, u32[]{:S(2)}) collective-permute-start(bf16[16,128,128]{2,1,0:T(8,128)(2,1)} %stage.24), channel_id=1, source_target_pairs={{0,2},{2,4},{4,6},{3,1},{5,3},{7,5},{8,10},{10,12},{12,14},{11,9},... | collective-permute-start | bytes 1572872 | tf_op jit(solution)/shard_map/ppermute | solution.py:482
  22.4 2.5 %stage.29 = bf16[16,128,128]{2,1,0:T(8,128)(2,1)} custom-call(s32[1]{0:T(128)} %constant.67.clone.1.refs_0_, s32[1]{0:T(128)} %bitcast.4.refs_0_.refs_1_.where_ref, s32[8,128]{1,0:T(8,128)S(1)} %get-tuple-element.565.refs_2_.table_ref, bf16[32,128,128]{2,1,0:T(8,128)(2,1)S(1)} %bitcast.38, bf16[32,128,128]{2,1,0:T(8,128)(2,1)S(1)} %bitcast.50, ...), custom_call_target="tpu_custom_call" | custom-call | tf_op jit(solution)/shard_map/stage/pallas_call | solution.py:467
  24.9 2.9 %collective-permute-start.16 = (bf16[16,128,128]{2,1,0:T(8,128)(2,1)}, bf16[16,128,128]{2,1,0:T(8,128)(2,1)S(1)}, u32[]{:S(2)}, u32[]{:S(2)}) collective-permute-start(bf16[16,128,128]{2,1,0:T(8,128)(2,1)} %stage.29), channel_id=1, source_target_pairs={{0,2},{2,4},{4,6},{3,1},{5,3},{7,5},{8,10},{10,12},{12,14},{11,9},... | collective-permute-start | bytes 1572872 | tf_op jit(solution)/shard_map/ppermute | solution.py:482
  30.8 5.1 %collective-permute-start.9 = (bf16[16,128,128]{2,1,0:T(8,128)(2,1)}, bf16[16,128,128]{2,1,0:T(8,128)(2,1)}, u32[]{:S(2)}, u32[]{:S(2)}) collective-permute-start(bf16[16,128,128]{2,1,0:T(8,128)(2,1)} %stage.25), channel_id=1, source_target_pairs={{0,2},{2,4},{4,6},{3,1},{5,3},{7,5},{8,10},{10,12},{12,14},{11,9},... | collective-permute-start | bytes 1572872 | tf_op jit(solution)/shard_map/ppermute | solution.py:482
  35.9 1.5 stage.30
  37.4 4.2 %collective-permute-start.17 = (bf16[16,128,128]{2,1,0:T(8,128)(2,1)}, bf16[16,128,128]{2,1,0:T(8,128)(2,1)}, u32[]{:S(2)}, u32[]{:S(2)}) collective-permute-start(bf16[16,128,128]{2,1,0:T(8,128)(2,1)} %stage.30), channel_id=1, source_target_pairs={{0,2},{2,4},{4,6},{3,1},{5,3},{7,5},{8,10},{10,12},{12,14},{11,9},... | collective-permute-start | bytes 1572872 | tf_op jit(solution)/shard_map/ppermute | solution.py:482
  41.6 1.6 %fusion = bf16[32,4,4,32]{0,1,3,2:T(4,128)(2,1)S(1)} fusion(bf16[8,32,256]{2,1,0:T(8,128)(2,1)} %collective-permute-done.12, bf16[8,32,256]{2,1,0:T(8,128)(2,1)} %collective-permute-done.11, bf16[8,32,256]{2,1,0:T(8,128)(2,1)} %collective-permute-done.10, bf16[8,32,256]{2,1,0:T(8,128)(2,1)} %param.10, s32[4,4]{1,0:T(4,128)S(1)} %broadcast_add_fusion), kind=kOutput, calls=%fused_computation.3 | convolution fusion | flops 10506240 | bytes 557120 | tf_op jit(solution)/shard_map/acz,qpz->cpqa/dot_general | solution.py:45
  46.3 2.5 %stage.26 = bf16[16,128,128]{2,1,0:T(8,128)(2,1)} custom-call(s32[1]{0:T(128)} %constant.66.clone.1.refs_0_, s32[1]{0:T(128)} %bitcast.4.refs_0_.refs_1_.where_ref, s32[8,128]{1,0:T(8,128)S(1)} %get-tuple-element.565.refs_2_.table_ref, bf16[32,128,128]{2,1,0:T(8,128)(2,1)S(1)} %bitcast.41, bf16[32,128,128]{2,1,0:T(8,128)(2,1)S(1)} %bitcast.53, ...), custom_call_target="tpu_custom_call" | custom-call | tf_op jit(solution)/shard_map/stage/pallas_call | solution.py:467
  48.8 2.1 %collective-permute-start.13 = (bf16[16,128,128]{2,1,0:T(8,128)(2,1)}, bf16[16,128,128]{2,1,0:T(8,128)(2,1)}, u32[]{:S(2)}, u32[]{:S(2)}) collective-permute-start(bf16[16,128,128]{2,1,0:T(8,128)(2,1)} %stage.26), channel_id=1, source_target_pairs={{0,2},{2,4},{4,6},{3,1},{5,3},{7,5},{8,10},{10,12},{12,14},{11,9},... | collective-permute-start | bytes 1572872 | tf_op jit(solution)/shard_map/ppermute | solution.py:482
  50.9 2.5 %stage.31 = bf16[16,128,128]{2,1,0:T(8,128)(2,1)} custom-call(s32[1]{0:T(128)} %constant.66.clone.1.refs_0_, s32[1]{0:T(128)} %bitcast.4.refs_0_.refs_1_.where_ref, s32[8,128]{1,0:T(8,128)S(1)} %get-tuple-element.565.refs_2_.table_ref, bf16[32,128,128]{2,1,0:T(8,128)(2,1)S(1)} %bitcast.42, bf16[32,128,128]{2,1,0:T(8,128)(2,1)S(1)} %bitcast.54, ...), custom_call_target="tpu_custom_call" | custom-call | tf_op jit(solution)/shard_map/stage/pallas_call | solution.py:467
  53.4 3.0 %collective-permute-start.18 = (bf16[16,128,128]{2,1,0:T(8,128)(2,1)}, bf16[16,128,128]{2,1,0:T(8,128)(2,1)}, u32[]{:S(2)}, u32[]{:S(2)}) collective-permute-start(bf16[16,128,128]{2,1,0:T(8,128)(2,1)} %stage.31), channel_id=1, source_target_pairs={{0,2},{2,4},{4,6},{3,1},{5,3},{7,5},{8,10},{10,12},{12,14},{11,9},... | collective-permute-start | bytes 1572872 | tf_op jit(solution)/shard_map/ppermute | solution.py:482
  58.6 5.2 %collective-permute-start.14 = (bf16[16,128,128]{2,1,0:T(8,128)(2,1)}, bf16[16,128,128]{2,1,0:T(8,128)(2,1)}, u32[]{:S(2)}, u32[]{:S(2)}) collective-permute-start(bf16[16,128,128]{2,1,0:T(8,128)(2,1)} %stage.27), channel_id=1, source_target_pairs={{0,2},{2,4},{4,6},{3,1},{5,3},{7,5},{8,10},{10,12},{12,14},{11,9},... | collective-permute-start | bytes 1572872 | tf_op jit(solution)/shard_map/ppermute | solution.py:482
  63.7 1.5 stage.32
  65.2 4.1 %collective-permute-start.19 = (bf16[16,128,128]{2,1,0:T(8,128)(2,1)}, bf16[16,128,128]{2,1,0:T(8,128)(2,1)}, u32[]{:S(2)}, u32[]{:S(2)}) collective-permute-start(bf16[16,128,128]{2,1,0:T(8,128)(2,1)} %stage.32), channel_id=1, source_target_pairs={{0,2},{2,4},{4,6},{3,1},{5,3},{7,5},{8,10},{10,12},{12,14},{11,9},... | collective-permute-start | bytes 1572872 | tf_op jit(solution)/shard_map/ppermute | solution.py:482
  69.9 1.5 stage.28
  71.4 5.2 %collective-permute-start.15 = (bf16[16,128,128]{2,1,0:T(8,128)(2,1)}, bf16[16,128,128]{2,1,0:T(8,128)(2,1)}, u32[]{:S(2)}, u32[]{:S(2)}) collective-permute-start(bf16[16,128,128]{2,1,0:T(8,128)(2,1)} %stage.28), channel_id=1, source_target_pairs={{0,2},{2,4},{4,6},{3,1},{5,3},{7,5},{8,10},{10,12},{12,14},{11,9},... | collective-permute-start | bytes 1572872 | tf_op jit(solution)/shard_map/ppermute | solution.py:482
  78.1 4.1 %collective-permute-start.20 = (bf16[16,128,128]{2,1,0:T(8,128)(2,1)}, bf16[16,128,128]{2,1,0:T(8,128)(2,1)}, u32[]{:S(2)}, u32[]{:S(2)}) collective-permute-start(bf16[16,128,128]{2,1,0:T(8,128)(2,1)} %stage.33), channel_id=1, source_target_pairs={{0,2},{2,4},{4,6},{3,1},{5,3},{7,5},{8,10},{10,12},{12,14},{11,9},... | collective-permute-start | bytes 1572872 | tf_op jit(solution)/shard_map/ppermute | solution.py:482
  82.3 2.4 %collective-permute-start.23 = (s32[8,128]{1,0:T(8,128)S(1)}, s32[8,128]{1,0:T(8,128)S(1)}, u32[]{:S(2)}, u32[]{:S(2)}) collective-permute-start(s32[8,128]{1,0:T(8,128)S(1)} %copy-done.5), channel_id=1, source_target_pairs={{0,24},{8,16},{16,8},{24,0},{1,25},{9,17},{17,9},{25,1},{2,26},{10... | collective-permute-start | bytes 12296 | tf_op jit(solution)/shard_map/ppermute | solution.py:31
  90.4 2.1 %last.1 = bf16[2,32,128,128]{3,2,1,0:T(8,128)(2,1)} custom-call(s32[1]{0:T(128)} %bitcast.4.refs_0_.refs_1_.where_ref, s32[8,128]{1,0:T(8,128)S(1)} %get-tuple-element.647, bf16[32,128,128]{2,1,0:T(8,128)(2,1)S(1)} %get-tuple-element.637, bf16[32,128,128]{2,1,0:T(8,128)(2,1)S(1)} %get-tuple-element.639, ...), custom_call_target="tpu_custom_call" | custom-call | tf_op jit(solution)/shard_map/last/pallas_call | solution.py:508
  92.7 4.3 %collective-permute-done.24.theirs_ref = bf16[2,32,128,128]{3,2,1,0:T(8,128)(2,1)S(1)} collective-permute-done((bf16[2,32,128,128]{3,2,1,0:T(8,128)(2,1)}, bf16[2,32,128,128]{3,2,1,0:T(8,128)(2,1)S(1)}, u32[]{:S(2)}, u32[]{:S(2)}) %collective-permute-start.24) | collective-permute-done | bytes 2097184 | tf_op jit(solution)/shard_map/ppermute | solution.py:516
  97.0 38.3 %krylov.1 = (f32[8,512,128]{2,1,0:T(8,128)S(1)}, f32[32,128]{1,0:T(8,128)S(1)}) custom-call(s32[8,128]{1,0:T(8,128)S(1)} %get-tuple-element.647, s32[1]{0:T(128)} %bitcast.3.me_ref.refs_0_, f32[512,128]{1,0:T(8,128)S(1)} %bitcast.35, bf16[256,256]{1,0:T(8,128)(2,1)S(1)} %mul.42.mix_ref, bf16[2,32,128,128]{3,2,1,0:T(8,128)(2,1)S(1)} %collective-permute-done.24.theirs_ref, ...), custom_call_target="tpu_custom_call" | custom-call | tf_op jit(solution)/shard_map/krylov/pallas_call | solution.py:561
  135.3 3.2 %collective-permute-start.27 = (f32[32,128]{1,0:T(8,128)S(1)}, f32[32,128]{1,0:T(8,128)S(1)}, u32[]{:S(2)}, u32[]{:S(2)}) collective-permute-start(f32[32,128]{1,0:T(8,128)S(1)} %get-tuple-element.394), channel_id=1, source_target_pairs={{0,6},{1,7},{2,4},{3,5},{4,2},{5,3},{6,0},{7,1},{8,14},{9,15},{10,... | collective-permute-start | bytes 49160 | tf_op jit(solution)/shard_map/ppermute | solution.py:31
  138.5 1.5 collective-permute-start.26
  140.9 2.2 %collective-permute-done.26 = f32[32,128]{1,0:T(8,128)S(1)} collective-permute-done((f32[32,128]{1,0:T(8,128)S(1)}, f32[32,128]{1,0:T(8,128)S(1)}, u32[]{:S(2)}, u32[]{:S(2)}) %collective-permute-start.26) | collective-permute-done | bytes 16416 | tf_op jit(solution)/shard_map/ppermute | solution.py:31
  145.7 2.1 %collective-permute-start.30 = (f32[32,128]{1,0:T(8,128)S(1)}, f32[32,128]{1,0:T(8,128)S(1)}, u32[]{:S(2)}, u32[]{:S(2)}) collective-permute-start(f32[32,128]{1,0:T(8,128)S(1)} %add.91), channel_id=1, source_target_pairs={{0,16},{8,24},{16,0},{24,8},{1,17},{9,25},{17,1},{25,9},{2,18},{10... | collective-permute-start | bytes 49160 | tf_op jit(solution)/shard_map/ppermute | solution.py:31
  149.7 1.8 %collective-permute-done.29 = f32[32,128]{1,0:T(8,128)S(1)} collective-permute-done((f32[32,128]{1,0:T(8,128)S(1)}, f32[32,128]{1,0:T(8,128)S(1)}, u32[]{:S(2)}, u32[]{:S(2)}) %collective-permute-start.29) | collective-permute-done | bytes 16416 | tf_op jit(solution)/shard_map/ppermute | solution.py:31
  151.6 4.0 %finish.1 = (f32[512,128]{1,0:T(8,128)}, f32[8,8]{1,0:T(8,128)}) custom-call(s32[1]{0:T(128)} %bitcast.3.me_ref.refs_0_, f32[32,128]{1,0:T(8,128)S(1)} %add_add_fusion.refs_1_, f32[8,512,128]{2,1,0:T(8,128)S(1)} %get-tuple-element.395.refs_2_), custom_call_target="tpu_custom_call" | custom-call | tf_op jit(solution)/shard_map/finish/pallas_call | solution.py:586
  (78 shorter events, 25.8 us)
Async XLA Ops:
  0.6 21.8 %copy-start.1 = (bf16[1,32,128,128]{3,2,1,0:T(8,128)(2,1)S(1)}, bf16[1,32,128,128]{3,2,1,0:T(8,128)(2,1)}, u32[]{:S(2)}) copy-start(bf16[1,32,128,128]{3,2,1,0:T(8,128)(2,1)} %param.11) | copy-start | bytes 3145732
  0.6 21.8 %copy-start.2 = (bf16[1,32,128,128]{3,2,1,0:T(8,128)(2,1)S(1)}, bf16[1,32,128,128]{3,2,1,0:T(8,128)(2,1)}, u32[]{:S(2)}) copy-start(bf16[1,32,128,128]{3,2,1,0:T(8,128)(2,1)} %param.12) | copy-start | bytes 3145732
  0.7 17.5 %collective-permute-start.6 = (bf16[32,128,128]{2,1,0:T(8,128)(2,1)}, bf16[32,128,128]{2,1,0:T(8,128)(2,1)}, u32[]{:S(2)}, u32[]{:S(2)}) collective-permute-start(bf16[32,128,128]{2,1,0:T(8,128)(2,1)} %bitcast.36), channel_id=1, source_target_pairs={{0,1},{1,0},{2,3},{3,2},{4,5},{5,4},{6,7},{7,6},{8,9},{9,8},{10,11... | collective-permute-start | bytes 3145736 | tf_op jit(solution)/shard_map/ppermute | solution.py:454
  1.2 17.0 %collective-permute-start.7 = (bf16[32,128,128]{2,1,0:T(8,128)(2,1)}, bf16[32,128,128]{2,1,0:T(8,128)(2,1)}, u32[]{:S(2)}, u32[]{:S(2)}) collective-permute-start(bf16[32,128,128]{2,1,0:T(8,128)(2,1)} %bitcast.48), channel_id=1, source_target_pairs={{0,1},{1,0},{2,3},{3,2},{4,5},{5,4},{6,7},{7,6},{8,9},{9,8},{10,11... | collective-permute-start | bytes 3145736 | tf_op jit(solution)/shard_map/ppermute | solution.py:454
  2.6 5.7 %collective-permute-start.3 = (s32[8,128]{1,0:T(8,128)S(1)}, s32[8,128]{1,0:T(8,128)S(1)}, u32[]{:S(2)}, u32[]{:S(2)}) collective-permute-start(s32[8,128]{1,0:T(8,128)S(1)} %broadcast_select_fusion), channel_id=1, source_target_pairs={{0,4},{1,5},{2,6},{3,7},{4,0},{5,1},{6,2},{7,3},{8,12},{9,13},{10,... | collective-permute-start | bytes 12296 | tf_op jit(solution)/shard_map/ppermute | solution.py:31
  6.7 5.4 %collective-permute-start.4 = (s32[8,128]{1,0:T(8,128)S(1)}, s32[8,128]{1,0:T(8,128)S(1)}, u32[]{:S(2)}, u32[]{:S(2)}) collective-permute-start(s32[8,128]{1,0:T(8,128)S(1)} %broadcast_select_fusion), channel_id=1, source_target_pairs={{0,6},{1,7},{2,4},{3,5},{4,2},{5,3},{6,0},{7,1},{8,14},{9,15},{10,... | collective-permute-start | bytes 12296 | tf_op jit(solution)/shard_map/ppermute | solution.py:31
  8.1 4.1 %collective-permute-start.2 = (s32[8,128]{1,0:T(8,128)S(1)}, s32[8,128]{1,0:T(8,128)S(1)}, u32[]{:S(2)}, u32[]{:S(2)}) collective-permute-start(s32[8,128]{1,0:T(8,128)S(1)} %broadcast_select_fusion), channel_id=1, source_target_pairs={{0,2},{1,3},{2,0},{3,1},{4,6},{5,7},{6,4},{7,5},{8,10},{9,11},{10,... | collective-permute-start | bytes 12296 | tf_op jit(solution)/shard_map/ppermute | solution.py:31
  12.1 3.1 %collective-permute-start.5 = (s32[8,128]{1,0:T(8,128)S(1)}, s32[8,128]{1,0:T(8,128)S(1)}, u32[]{:S(2)}, u32[]{:S(2)}) collective-permute-start(s32[8,128]{1,0:T(8,128)S(1)} %maximum_maximum_fusion.1), channel_id=1, source_target_pairs={{0,1},{1,0},{2,3},{3,2},{4,5},{5,4},{6,7},{7,6},{8,9},{9,8},{10,11... | collective-permute-start | bytes 12296 | tf_op jit(solution)/shard_map/ppermute | solution.py:31
  12.2 29.4 %collective-permute-start.11 = (bf16[8,32,256]{2,1,0:T(8,128)(2,1)}, bf16[8,32,256]{2,1,0:T(8,128)(2,1)}, u32[]{:S(2)}, u32[]{:S(2)}) collective-permute-start(bf16[8,32,256]{2,1,0:T(8,128)(2,1)} %param.10), channel_id=1, source_target_pairs={{16,0},{24,8},{0,16},{8,24},{17,1},{25,9},{1,17},{9,25},{18,2},{26... | collective-permute-start | bytes 393224 | tf_op jit(solution)/shard_map/ppermute | solution.py:435
  13.8 27.8 %collective-permute-start.10 = (bf16[8,32,256]{2,1,0:T(8,128)(2,1)}, bf16[8,32,256]{2,1,0:T(8,128)(2,1)}, u32[]{:S(2)}, u32[]{:S(2)}) collective-permute-start(bf16[8,32,256]{2,1,0:T(8,128)(2,1)} %param.10), channel_id=1, source_target_pairs={{8,0},{16,8},{24,16},{0,24},{9,1},{17,9},{25,17},{1,25},{10,2},{18... | collective-permute-start | bytes 393224 | tf_op jit(solution)/shard_map/ppermute | solution.py:435
  20.7 8.7 %collective-permute-start.8 = (bf16[16,128,128]{2,1,0:T(8,128)(2,1)}, bf16[16,128,128]{2,1,0:T(8,128)(2,1)S(1)}, u32[]{:S(2)}, u32[]{:S(2)}) collective-permute-start(bf16[16,128,128]{2,1,0:T(8,128)(2,1)} %stage.24), channel_id=1, source_target_pairs={{0,2},{2,4},{4,6},{3,1},{5,3},{7,5},{8,10},{10,12},{12,14},{11,9},... | collective-permute-start | bytes 1572872 | tf_op jit(solution)/shard_map/ppermute | solution.py:482
  24.9 11.0 %collective-permute-start.16 = (bf16[16,128,128]{2,1,0:T(8,128)(2,1)}, bf16[16,128,128]{2,1,0:T(8,128)(2,1)S(1)}, u32[]{:S(2)}, u32[]{:S(2)}) collective-permute-start(bf16[16,128,128]{2,1,0:T(8,128)(2,1)} %stage.29), channel_id=1, source_target_pairs={{0,2},{2,4},{4,6},{3,1},{5,3},{7,5},{8,10},{10,12},{12,14},{11,9},... | collective-permute-start | bytes 1572872 | tf_op jit(solution)/shard_map/ppermute | solution.py:482
  27.8 13.8 %collective-permute-start.12 = (bf16[8,32,256]{2,1,0:T(8,128)(2,1)S(1)}, bf16[8,32,256]{2,1,0:T(8,128)(2,1)}, u32[]{:S(2)}, u32[]{:S(2)}) collective-permute-start(bf16[8,32,256]{2,1,0:T(8,128)(2,1)S(1)} %copy-done.7), channel_id=1, source_target_pairs={{24,0},{0,8},{8,16},{16,24},{25,1},{1,9},{9,17},{17,25},{26,2},{2,... | collective-permute-start | bytes 393224 | tf_op jit(solution)/shard_map/ppermute | solution.py:435
  30.8 15.5 %collective-permute-start.9 = (bf16[16,128,128]{2,1,0:T(8,128)(2,1)}, bf16[16,128,128]{2,1,0:T(8,128)(2,1)}, u32[]{:S(2)}, u32[]{:S(2)}) collective-permute-start(bf16[16,128,128]{2,1,0:T(8,128)(2,1)} %stage.25), channel_id=1, source_target_pairs={{0,2},{2,4},{4,6},{3,1},{5,3},{7,5},{8,10},{10,12},{12,14},{11,9},... | collective-permute-start | bytes 1572872 | tf_op jit(solution)/shard_map/ppermute | solution.py:482
  37.4 13.5 %collective-permute-start.17 = (bf16[16,128,128]{2,1,0:T(8,128)(2,1)}, bf16[16,128,128]{2,1,0:T(8,128)(2,1)}, u32[]{:S(2)}, u32[]{:S(2)}) collective-permute-start(bf16[16,128,128]{2,1,0:T(8,128)(2,1)} %stage.30), channel_id=1, source_target_pairs={{0,2},{2,4},{4,6},{3,1},{5,3},{7,5},{8,10},{10,12},{12,14},{11,9},... | collective-permute-start | bytes 1572872 | tf_op jit(solution)/shard_map/ppermute | solution.py:482
  48.8 8.3 %collective-permute-start.13 = (bf16[16,128,128]{2,1,0:T(8,128)(2,1)}, bf16[16,128,128]{2,1,0:T(8,128)(2,1)}, u32[]{:S(2)}, u32[]{:S(2)}) collective-permute-start(bf16[16,128,128]{2,1,0:T(8,128)(2,1)} %stage.26), channel_id=1, source_target_pairs={{0,2},{2,4},{4,6},{3,1},{5,3},{7,5},{8,10},{10,12},{12,14},{11,9},... | collective-permute-start | bytes 1572872 | tf_op jit(solution)/shard_map/ppermute | solution.py:482
  53.4 10.3 %collective-permute-start.18 = (bf16[16,128,128]{2,1,0:T(8,128)(2,1)}, bf16[16,128,128]{2,1,0:T(8,128)(2,1)}, u32[]{:S(2)}, u32[]{:S(2)}) collective-permute-start(bf16[16,128,128]{2,1,0:T(8,128)(2,1)} %stage.31), channel_id=1, source_target_pairs={{0,2},{2,4},{4,6},{3,1},{5,3},{7,5},{8,10},{10,12},{12,14},{11,9},... | collective-permute-start | bytes 1572872 | tf_op jit(solution)/shard_map/ppermute | solution.py:482
  58.6 11.4 %collective-permute-start.14 = (bf16[16,128,128]{2,1,0:T(8,128)(2,1)}, bf16[16,128,128]{2,1,0:T(8,128)(2,1)}, u32[]{:S(2)}, u32[]{:S(2)}) collective-permute-start(bf16[16,128,128]{2,1,0:T(8,128)(2,1)} %stage.27), channel_id=1, source_target_pairs={{0,2},{2,4},{4,6},{3,1},{5,3},{7,5},{8,10},{10,12},{12,14},{11,9},... | collective-permute-start | bytes 1572872 | tf_op jit(solution)/shard_map/ppermute | solution.py:482
  65.2 11.4 %collective-permute-start.19 = (bf16[16,128,128]{2,1,0:T(8,128)(2,1)}, bf16[16,128,128]{2,1,0:T(8,128)(2,1)}, u32[]{:S(2)}, u32[]{:S(2)}) collective-permute-start(bf16[16,128,128]{2,1,0:T(8,128)(2,1)} %stage.32), channel_id=1, source_target_pairs={{0,2},{2,4},{4,6},{3,1},{5,3},{7,5},{8,10},{10,12},{12,14},{11,9},... | collective-permute-start | bytes 1572872 | tf_op jit(solution)/shard_map/ppermute | solution.py:482
  71.4 17.4 %collective-permute-start.15 = (bf16[16,128,128]{2,1,0:T(8,128)(2,1)}, bf16[16,128,128]{2,1,0:T(8,128)(2,1)}, u32[]{:S(2)}, u32[]{:S(2)}) collective-permute-start(bf16[16,128,128]{2,1,0:T(8,128)(2,1)} %stage.28), channel_id=1, source_target_pairs={{0,2},{2,4},{4,6},{3,1},{5,3},{7,5},{8,10},{10,12},{12,14},{11,9},... | collective-permute-start | bytes 1572872 | tf_op jit(solution)/shard_map/ppermute | solution.py:482
  78.1 10.7 %collective-permute-start.20 = (bf16[16,128,128]{2,1,0:T(8,128)(2,1)}, bf16[16,128,128]{2,1,0:T(8,128)(2,1)}, u32[]{:S(2)}, u32[]{:S(2)}) collective-permute-start(bf16[16,128,128]{2,1,0:T(8,128)(2,1)} %stage.33), channel_id=1, source_target_pairs={{0,2},{2,4},{4,6},{3,1},{5,3},{7,5},{8,10},{10,12},{12,14},{11,9},... | collective-permute-start | bytes 1572872 | tf_op jit(solution)/shard_map/ppermute | solution.py:482
  82.3 4.5 %collective-permute-start.23 = (s32[8,128]{1,0:T(8,128)S(1)}, s32[8,128]{1,0:T(8,128)S(1)}, u32[]{:S(2)}, u32[]{:S(2)}) collective-permute-start(s32[8,128]{1,0:T(8,128)S(1)} %copy-done.5), channel_id=1, source_target_pairs={{0,24},{8,16},{16,8},{24,0},{1,25},{9,17},{17,9},{25,1},{2,26},{10... | collective-permute-start | bytes 12296 | tf_op jit(solution)/shard_map/ppermute | solution.py:31
  84.6 3.6 %collective-permute-start.22 = (s32[8,128]{1,0:T(8,128)S(1)}, s32[8,128]{1,0:T(8,128)S(1)}, u32[]{:S(2)}, u32[]{:S(2)}) collective-permute-start(s32[8,128]{1,0:T(8,128)S(1)} %copy-done.5), channel_id=1, source_target_pairs={{0,16},{8,24},{16,0},{24,8},{1,17},{9,25},{17,1},{25,9},{2,18},{10... | collective-permute-start | bytes 12296 | tf_op jit(solution)/shard_map/ppermute | solution.py:31
  84.6 3.6 %collective-permute-start.21 = (s32[8,128]{1,0:T(8,128)S(1)}, s32[8,128]{1,0:T(8,128)S(1)}, u32[]{:S(2)}, u32[]{:S(2)}) collective-permute-start(s32[8,128]{1,0:T(8,128)S(1)} %copy-done.5), channel_id=1, source_target_pairs={{0,8},{8,0},{16,24},{24,16},{1,9},{9,1},{17,25},{25,17},{2,10},{10... | collective-permute-start | bytes 12296 | tf_op jit(solution)/shard_map/ppermute | solution.py:31
  92.6 4.4 %collective-permute-start.24 = (bf16[2,32,128,128]{3,2,1,0:T(8,128)(2,1)}, bf16[2,32,128,128]{3,2,1,0:T(8,128)(2,1)S(1)}, u32[]{:S(2)}, u32[]{:S(2)}) collective-permute-start(bf16[2,32,128,128]{3,2,1,0:T(8,128)(2,1)} %last.1), channel_id=1, source_target_pairs={{0,1},{1,0},{2,3},{3,2},{4,5},{5,4},{6,7},{7,6},{8,9},{9,8},{10,11... | collective-permute-start | bytes 6291464 | tf_op jit(solution)/shard_map/ppermute | solution.py:516
  135.3 5.6 %collective-permute-start.27 = (f32[32,128]{1,0:T(8,128)S(1)}, f32[32,128]{1,0:T(8,128)S(1)}, u32[]{:S(2)}, u32[]{:S(2)}) collective-permute-start(f32[32,128]{1,0:T(8,128)S(1)} %get-tuple-element.394), channel_id=1, source_target_pairs={{0,6},{1,7},{2,4},{3,5},{4,2},{5,3},{6,0},{7,1},{8,14},{9,15},{10,... | collective-permute-start | bytes 49160 | tf_op jit(solution)/shard_map/ppermute | solution.py:31
  138.5 4.6 %collective-permute-start.26 = (f32[32,128]{1,0:T(8,128)S(1)}, f32[32,128]{1,0:T(8,128)S(1)}, u32[]{:S(2)}, u32[]{:S(2)}) collective-permute-start(f32[32,128]{1,0:T(8,128)S(1)} %get-tuple-element.394), channel_id=1, source_target_pairs={{0,4},{1,5},{2,6},{3,7},{4,0},{5,1},{6,2},{7,3},{8,12},{9,13},{10,... | collective-permute-start | bytes 49160 | tf_op jit(solution)/shard_map/ppermute | solution.py:31
  140.0 3.7 %collective-permute-start.25 = (f32[32,128]{1,0:T(8,128)S(1)}, f32[32,128]{1,0:T(8,128)S(1)}, u32[]{:S(2)}, u32[]{:S(2)}) collective-permute-start(f32[32,128]{1,0:T(8,128)S(1)} %get-tuple-element.394), channel_id=1, source_target_pairs={{0,2},{1,3},{2,0},{3,1},{4,6},{5,7},{6,4},{7,5},{8,10},{9,11},{10,... | collective-permute-start | bytes 49160 | tf_op jit(solution)/shard_map/ppermute | solution.py:31
  143.8 1.2 collective-permute-start.28
  145.0 4.7 %collective-permute-start.31 = (f32[32,128]{1,0:T(8,128)S(1)}, f32[32,128]{1,0:T(8,128)S(1)}, u32[]{:S(2)}, u32[]{:S(2)}) collective-permute-start(f32[32,128]{1,0:T(8,128)S(1)} %add.91), channel_id=1, source_target_pairs={{0,24},{8,16},{16,8},{24,0},{1,25},{9,17},{17,9},{25,1},{2,26},{10... | collective-permute-start | bytes 49160 | tf_op jit(solution)/shard_map/ppermute | solution.py:31
  145.7 4.0 %collective-permute-start.30 = (f32[32,128]{1,0:T(8,128)S(1)}, f32[32,128]{1,0:T(8,128)S(1)}, u32[]{:S(2)}, u32[]{:S(2)}) collective-permute-start(f32[32,128]{1,0:T(8,128)S(1)} %add.91), channel_id=1, source_target_pairs={{0,16},{8,24},{16,0},{24,8},{1,17},{9,25},{17,1},{25,9},{2,18},{10... | collective-permute-start | bytes 49160 | tf_op jit(solution)/shard_map/ppermute | solution.py:31
  147.9 3.7 %collective-permute-start.29 = (f32[32,128]{1,0:T(8,128)S(1)}, f32[32,128]{1,0:T(8,128)S(1)}, u32[]{:S(2)}, u32[]{:S(2)}) collective-permute-start(f32[32,128]{1,0:T(8,128)S(1)} %add.91), channel_id=1, source_target_pairs={{0,8},{8,0},{16,24},{24,16},{1,9},{9,1},{17,25},{25,17},{2,10},{10... | collective-permute-start | bytes 49160 | tf_op jit(solution)/shard_map/ppermute | solution.py:31
  (6 other events, 38.5 us)
